TPU v7x, 128 devices: a whole 4x4x4 slice. The times are simulated.
128 devices in a mesh: ctx: 16 (over y_hi, z, core), tp: 8 (over y_lo, x).
Axes of the slice: x: 4, y: 4 (y_hi: 2, y_lo: 2; y = y_hi * 2 + y_lo), z: 4, core: 2. Of those that a mesh axis runs over, the one named last changes fastest.
Arguments:
- queries: bfloat16 [2048, 4096], P('ctx', 'tp'), may hold values from -6 to 6
- keys: bfloat16 [2048, 256], P('ctx'), may hold values from -6 to 6
- values: bfloat16 [2048, 256], P('ctx'), may hold values from -6 to 6
- resid: bfloat16 [2048, 4096], P(('ctx', 'tp')), may hold values from -4 to 4
- out_proj: bfloat16 [4096, 4096], P('tp'), may hold values from -0.375 to 0.375
- norm_gain: float32 [4096], replicated, may hold values from 0.1 to 1.9
- expert_ids: int32 [2048, 8], P(('ctx', 'tp')), may hold values from 0 to 31, all different within a row; in each aligned block of 16 rows (0 to 15, 16 to 31, ...) at most 5 rows name the same one
- gates: float32 [2048, 8], P(('ctx', 'tp')), may hold values from 0.1 to 0.5
- w_gate: bfloat16 [32, 1536, 4096], P('ctx', 'tp'), may hold values from -0.09375 to 0.09375
- w_up: bfloat16 [32, 1536, 4096], P('ctx', 'tp'), may hold values from -0.09375 to 0.09375
- w_down: bfloat16 [32, 1536, 4096], P('ctx', 'tp'), may hold values from -0.15625 to 0.15625
- cotangent: bfloat16 [2048, 4096], P(('ctx', 'tp')), may hold values from -2 to 2
Outputs:
- layer_out: bfloat16 [2048, 4096], P(('ctx', 'tp'))
- grad_gate: bfloat16 [32, 1536, 4096], P('ctx', 'tp')
- grad_up: bfloat16 [32, 1536, 4096], P('ctx', 'tp')
- grad_down: bfloat16 [32, 1536, 4096], P('ctx', 'tp')
Inputs may be any that keep to these rules, and one draw needn't show every extreme that they name: `expert_ids`: in the 16 rows of one device (aligned blocks of rows) no expert is named more than 5 times, a bound that some block reaches; each row names 8 different experts.
All inputs are finite; a program needn't handle non-finite values.
Results may differ from a plain program's by a relative error of at most 0.025.
Values may be sent and summed in bfloat16 or wider, within the bound.
No kernel may reach another device: no remote copies, remote signals or barrier semaphores. Data moves between devices by JAX's collectives and lax.ppermute only.
A program may use at most 192 MiB of HBM per device.

v0:
```python
import math

import jax
import jax.numpy as jnp
from jax import lax
from jax.sharding import PartitionSpec as P

D = 4096
QHEADS = 32
KVHEADS = 2
HEAD = 128
TOPK = 8


def shards(
    queries,
    keys,
    values,
    resid,
    out_proj,
    norm_gain,
    expert_ids,
    gates,
    w_gate,
    w_up,
    w_down,
    cotangent,
):
    groups = lax.axis_size("ctx")
    tensor = lax.axis_size("tp")
    tok_ctx = queries.shape[0]
    heads_dev = queries.shape[1] // HEAD
    group_size = QHEADS // KVHEADS
    kv_head = lax.axis_index("tp") * heads_dev // group_size
    key_mine = lax.dynamic_slice_in_dim(keys, kv_head * HEAD, HEAD, 1)
    value_mine = lax.dynamic_slice_in_dim(values, kv_head * HEAD, HEAD, 1)
    query_pos = lax.axis_index("ctx") * tok_ctx + jnp.arange(tok_ctx, dtype=jnp.int32)
    query_heads = queries.reshape(tok_ctx, heads_dev, HEAD)
    score_scale = 1.0 / math.sqrt(HEAD)
    running = jnp.full((heads_dev, tok_ctx), -1e30, jnp.float32)
    key_piece = lax.all_gather(key_mine, "ctx", axis=0, tiled=True)
    value_piece = lax.all_gather(value_mine, "ctx", axis=0, tiled=True)
    scores = (
        jnp.einsum("qhd,kd->hqk", query_heads, key_piece, preferred_element_type=jnp.float32)
        * score_scale
    )
    key_pos = jnp.arange(key_piece.shape[0], dtype=jnp.int32)
    visible = key_pos[None, None, :] <= query_pos[None, :, None]
    block_max = jnp.max(jnp.where(visible, scores, -1e30), axis=2)
    new_running = jnp.maximum(running, block_max)
    weights = jnp.where(visible, jnp.exp(scores - new_running[:, :, None]), 0.0)
    denom = jnp.sum(weights, axis=2)
    accumulated = jnp.einsum(
        "hqk,kd->hqd", weights.astype(jnp.bfloat16), value_piece, preferred_element_type=jnp.float32
    )
    attn_heads = (accumulated / denom[:, :, None]).astype(jnp.bfloat16)
    attn = jnp.transpose(attn_heads, (1, 0, 2)).reshape(tok_ctx, heads_dev * HEAD)
    row_total = resid.shape[0]
    head_mix = lax.psum_scatter(
        jnp.dot(attn, out_proj, preferred_element_type=jnp.float32).astype(jnp.bfloat16),
        "tp",
        scatter_dimension=0,
        tiled=True,
    ).astype(jnp.float32)
    stream = resid.astype(jnp.float32) + head_mix
    normed = (
        stream * lax.rsqrt(jnp.mean(stream * stream, axis=1, keepdims=True) + 1e-06) * norm_gain
    ).astype(jnp.bfloat16)
    exp_dev = w_gate.shape[0]
    experts_all = exp_dev * groups
    capacity = 5 * row_total * TOPK // (4 * experts_all)
    slot_total = experts_all * capacity
    flat_ids = expert_ids.reshape(-1)
    pick_table = (flat_ids[:, None] == jnp.arange(experts_all, dtype=jnp.int32)[None, :]).astype(
        jnp.int32
    )
    before = jnp.cumsum(pick_table, axis=0) - pick_table
    rank_in = jnp.sum(before * pick_table, axis=1)
    owner_group = flat_ids // exp_dev
    local_exp = flat_ids % exp_dev
    target = (local_exp * groups + owner_group) * capacity + rank_in
    placement = (target[:, None] == jnp.arange(slot_total, dtype=jnp.int32)[None, :]).astype(
        jnp.float32
    )
    placement = placement.reshape(row_total, TOPK, slot_total)
    hit_table = jnp.sum(placement, axis=1)
    weighted = jnp.sum(placement * gates[:, :, None], axis=1)
    send_rows = jnp.einsum(
        "rs,rd->sd", hit_table.astype(jnp.bfloat16), normed, preferred_element_type=jnp.float32
    ).astype(jnp.bfloat16)
    send_grads = jnp.einsum(
        "rs,rd->sd", weighted, cotangent.astype(jnp.float32), precision=lax.Precision.HIGHEST
    ).astype(jnp.bfloat16)
    send_rows = send_rows.reshape(exp_dev, groups, capacity, D)
    send_grads = send_grads.reshape(exp_dev, groups, capacity, D)

    def spread_out(block_in):
        widened = jnp.broadcast_to(block_in[:, :, None], (exp_dev, groups, tensor, capacity, D))
        return widened.reshape(exp_dev, groups * tensor, capacity, D)

    rows_in, grads_in = (
        lax.all_to_all(
            spread_out(send_rows), ("ctx", "tp"), split_axis=1, concat_axis=1, tiled=True
        ),
        lax.all_to_all(
            spread_out(send_grads), ("ctx", "tp"), split_axis=1, concat_axis=1, tiled=True
        ),
    )
    expert_rows = rows_in.reshape(exp_dev, -1, D)
    expert_grads = grads_in.reshape(exp_dev, -1, D)
    gate_val = jnp.einsum("end,efd->enf", expert_rows, w_gate, preferred_element_type=jnp.float32)
    up_val = jnp.einsum("end,efd->enf", expert_rows, w_up, preferred_element_type=jnp.float32)
    sigmoid_val = jax.nn.sigmoid(gate_val)
    silu_val = gate_val * sigmoid_val
    activated = (silu_val * up_val).astype(jnp.bfloat16)
    partial_value = jnp.einsum(
        "enf,efd->end", activated, w_down, preferred_element_type=jnp.float32
    )
    partial_value = partial_value.astype(jnp.bfloat16).reshape(rows_in.shape)
    back_act = jnp.einsum("end,efd->enf", expert_grads, w_down, preferred_element_type=jnp.float32)
    d_gate = (back_act * up_val * sigmoid_val * (1.0 + gate_val * (1.0 - sigmoid_val))).astype(
        jnp.bfloat16
    )
    d_up = (back_act * silu_val).astype(jnp.bfloat16)
    grad_down = jnp.einsum(
        "enf,end->efd", activated, expert_grads, preferred_element_type=jnp.float32
    )
    grad_gate = jnp.einsum("enf,end->efd", d_gate, expert_rows, preferred_element_type=jnp.float32)
    grad_up = jnp.einsum("enf,end->efd", d_up, expert_rows, preferred_element_type=jnp.float32)
    partial_value, grad_outs = (
        partial_value,
        (
            grad_gate.astype(jnp.bfloat16),
            grad_up.astype(jnp.bfloat16),
            grad_down.astype(jnp.bfloat16),
        ),
    )
    returned = lax.all_to_all(partial_value, ("ctx", "tp"), split_axis=1, concat_axis=1, tiled=True)
    returned = returned.reshape(exp_dev, groups, tensor, capacity, D).astype(jnp.float32)
    result = jnp.sum(returned, axis=2).astype(jnp.bfloat16)
    combined = jnp.einsum(
        "rs,sd->rd",
        weighted,
        result.reshape(slot_total, D).astype(jnp.float32),
        precision=lax.Precision.HIGHEST,
    )
    layer_out = (stream + combined).astype(jnp.bfloat16)
    return (layer_out, grad_outs[0], grad_outs[1], grad_outs[2])


def solution(mesh):
    in_specs = (
        P("ctx", "tp"),
        P("ctx", None),
        P("ctx", None),
        P(("ctx", "tp"), None),
        P("tp", None),
        P(),
        P(("ctx", "tp"), None),
        P(("ctx", "tp"), None),
        P("ctx", "tp", None),
        P("ctx", "tp", None),
        P("ctx", "tp", None),
        P(("ctx", "tp"), None),
    )
    out_specs = (
        P(("ctx", "tp"), None),
        P("ctx", "tp", None),
        P("ctx", "tp", None),
        P("ctx", "tp", None),
    )
    return jax.shard_map(shards, mesh=mesh, in_specs=in_specs, out_specs=out_specs, check_vma=False)
```

profile of v0, /device:TPU:39, one launch (start us, length us, event | category | flops | bytes accessed | tf_op | source)
XLA Modules:
  0.0 627.9 jit_solution(15526818067554748710)
XLA Ops:
  9.2 22.4 %all_gather.7 = bf16[2048,128]{0,1:T(8,128)(2,1)S(1)} all-gather(bf16[128,128]{0,1:T(8,128)(2,1)S(1)} %copy.82), channel_id=1, replica_groups=mesh['ctx'=16,'tp'=8] {'ctx'}, dimensions={0}, use_global_device_ids=true | all-gather | bytes 557056 | tf_op jit(solution)/shard_map/all_gather | solution.py:42
  31.7 25.6 %all_gather.6 = bf16[2048,128]{1,0:T(8,128)(2,1)S(1)} all-gather(bf16[128,128]{1,0:T(8,128)(2,1)S(1)} %constant_dynamic-slice_fusion.1), channel_id=1, replica_groups=mesh['ctx'=16,'tp'=8] {'ctx'}, dimensions={0}, use_global_device_ids=true | all-gather | bytes 557056 | tf_op jit(solution)/shard_map/all_gather | solution.py:41
  57.2 1.6 fusion.22
  60.7 1.2 copy-done.1
  62.0 1.7 convolution_convert_fusion.3
  64.7 29.4 %reduce-scatter.2.cloned.1.call-done = bf16[16,4096]{1,0:T(8,128)(2,1)} async-done(((bf16[128,4096]{1,0:T(8,128)(2,1)}), bf16[16,4096]{1,0:T(8,128)(2,1)}) %reduce-scatter.2.cloned.1.call-update) | async-done | bytes 131088 | tf_op jit(solution)/shard_map/reduce_scatter | solution.py:59
  95.1 2.5 convolution_convert_fusion.2
  97.6 2.7 broadcast_in_dim.49
  100.3 3.1 copy.71
  103.4 11.0 %broadcast_in_dim.50 = bf16[2,16,8,5,4096]{4,0,3,2,1:T(2,128)(2,1)} broadcast(bf16[2,16,5,4096]{3,0,2,1:T(2,128)(2,1)S(1)} %copy.71), dimensions={0,1,3,4} | broadcast | bytes 11796480 | tf_op jit(solution)/shard_map/broadcast_in_dim | solution.py:98
  114.4 13.8 %all-to-all-start = ((bf16[2,128,5,4096]{3,0,2,1:T(2,128)(2,1)}), bf16[2,128,5,4096]{3,0,2,1:T(2,128)(2,1)}, u32[]{:S(2)}, u32[]{:S(2)}) async-start(bf16[2,128,5,4096]{3,0,2,1:T(2,128)(2,1)} %bitcast.67), calls=%async_computation.1 | async-start | bytes 20971520 | tf_op jit(solution)/shard_map/all_to_all | solution.py:102
  128.2 2.3 convolution_convert_fusion.1
  130.5 2.7 broadcast_in_dim.51
  133.1 4.2 copy.76
  137.3 139.7 %all-to-all-done = bf16[2,128,5,4096]{3,0,2,1:T(2,128)(2,1)} async-done(((bf16[2,128,5,4096]{3,0,2,1:T(2,128)(2,1)}), bf16[2,128,5,4096]{3,0,2,1:T(2,128)(2,1)}, u32[]{:S(2)}, u32[]{:S(2)}) %all-to-all-start) | async-done | bytes 10485792 | tf_op jit(solution)/shard_map/all_to_all | solution.py:102
  277.0 11.7 %broadcast_in_dim.52 = bf16[2,16,8,5,4096]{4,0,3,2,1:T(2,128)(2,1)} broadcast(bf16[2,16,5,4096]{3,0,2,1:T(2,128)(2,1)} %copy.76), dimensions={0,1,3,4} | broadcast | bytes 11796480 | tf_op jit(solution)/shard_map/broadcast_in_dim | solution.py:98
  288.7 6.5 %all-to-all-start.2 = ((bf16[2,128,5,4096]{3,0,2,1:T(2,128)(2,1)}), bf16[2,128,5,4096]{3,0,2,1:T(2,128)(2,1)}, u32[]{:S(2)}, u32[]{:S(2)}) async-start(bf16[2,128,5,4096]{3,0,2,1:T(2,128)(2,1)} %bitcast.66), calls=%async_computation.3 | async-start | bytes 20971520 | tf_op jit(solution)/shard_map/all_to_all | solution.py:105
  295.2 17.6 %fusion.10 = f32[2,640,192]{1,2,0:T(8,128)S(1)} fusion(bf16[2,192,4096]{2,1,0:T(8,128)(2,1)} %param.20, bf16[2,640,4096]{2,0,1:T(2,128)(2,1)} %bitcast.7), kind=kOutput, calls=%fused_computation.12 | convolution fusion | flops 2013265920 | bytes 14614528 | tf_op jit(solution)/shard_map/end,efd->enf/dot_general | solution.py:111
  312.8 17.8 %multiply_convert_fusion.2 = (bf16[2,640,192]{1,2,0:T(8,128)(2,1)S(1)}, f32[2,640,192]{1,2,0:T(8,128)}) fusion(f32[2,640,192]{1,2,0:T(8,128)S(1)} %fusion.10, bf16[2,192,4096]{2,1,0:T(8,128)(2,1)S(1)} %copy-done.10, bf16[2,640,4096]{2,0,1:T(2,128)(2,1)} %bitcast.7), kind=kOutput, calls=%fused_computation.37 | convolution fusion | flops 2014740480 | bytes 16089088 | tf_op jit(solution)/shard_map/end,efd->enf/dot_general | solution.py:112
  330.6 3.2 convolution_convert_fusion
  333.8 27.7 %copy.74 = bf16[2,640,4096]{2,0,1:T(2,128)(2,1)} copy(bf16[2,640,4096]{2,1,0:T(8,128)(2,1)S(1)} %convolution_convert_fusion) | data formatting | bytes 20971520 | tf_op jit(solution)/shard_map/convert_element_type | solution.py:119
  361.5 82.3 %all-to-all-done.2 = bf16[2,128,5,4096]{3,0,2,1:T(2,128)(2,1)} async-done(((bf16[2,128,5,4096]{3,0,2,1:T(2,128)(2,1)}), bf16[2,128,5,4096]{3,0,2,1:T(2,128)(2,1)}, u32[]{:S(2)}, u32[]{:S(2)}) %all-to-all-start.2) | async-done | bytes 10485792 | tf_op jit(solution)/shard_map/all_to_all | solution.py:105
  443.8 6.2 all-to-all-start.1
  450.0 16.6 %fusion.2 = f32[2,640,192]{1,2,0:T(8,128)S(1)} fusion(bf16[2,192,4096]{2,1,0:T(8,128)(2,1)S(1)} %copy-done, bf16[2,640,4096]{2,0,1:T(2,128)(2,1)} %bitcast.11), kind=kOutput, calls=%fused_computation.3 | convolution fusion | flops 2013265920 | bytes 14614528 | tf_op jit(solution)/shard_map/end,efd->enf/dot_general | solution.py:120
  466.6 18.3 %fusion.18 = bf16[2,192,4096]{2,1,0:T(8,128)(2,1)} fusion(bf16[2,640,192]{1,2,0:T(8,128)(2,1)S(1)} %copy-done.5, bf16[2,640,4096]{2,0,1:T(2,128)(2,1)} %bitcast.11), kind=kOutput, calls=%fused_computation.16 | convolution fusion | flops 2014838784 | bytes 14123008 | tf_op jit(solution)/shard_map/enf,end->efd/dot_general | solution.py:125
  484.9 18.4 %fusion.15 = bf16[2,192,4096]{2,1,0:T(8,128)(2,1)} fusion(bf16[2,640,4096]{2,0,1:T(2,128)(2,1)} %bitcast.7, f32[2,640,192]{1,2,0:T(8,128)S(1)} %fusion.2, f32[2,640,192]{1,2,0:T(8,128)S(1)} %copy-done.12), kind=kOutput, calls=%fused_computation.15 | convolution fusion | flops 2016313344 | bytes 15597568 | tf_op jit(solution)/shard_map/enf,end->efd/dot_general | solution.py:129
  503.3 18.5 %fusion.12 = bf16[2,192,4096]{2,1,0:T(8,128)(2,1)} fusion(bf16[2,640,4096]{2,0,1:T(2,128)(2,1)} %bitcast.7, f32[2,640,192]{1,2,0:T(8,128)S(1)} %copy-done.12, f32[2,640,192]{1,2,0:T(8,128)S(1)} %fusion.2, f32[2,640,192]{1,2,0:T(8,128)S(1)} %copy-done.13), kind=kOutput, calls=%fused_computation.14 | convolution fusion | flops 2017296384 | bytes 16580608 | tf_op jit(solution)/shard_map/enf,end->efd/dot_general | solution.py:128
  521.7 77.1 %all-to-all-done.1 = bf16[2,128,5,4096]{3,0,2,1:T(2,128)(2,1)} async-done(((bf16[2,128,5,4096]{3,0,2,1:T(2,128)(2,1)}), bf16[2,128,5,4096]{3,0,2,1:T(2,128)(2,1)}, u32[]{:S(2)}, u32[]{:S(2)}) %all-to-all-start.1) | async-done | bytes 10485792 | tf_op jit(solution)/shard_map/all_to_all | solution.py:138
  598.8 13.0 %bitcast_reduce_fusion = bf16[2,16,5,4096]{3,0,2,1:T(2,128)(2,1)} fusion(bf16[2,128,5,4096]{3,0,2,1:T(2,128)(2,1)} %all-to-all-done.1), kind=kLoop, calls=%fused_computation | loop fusion | flops 4587520 | bytes 11796480 | tf_op jit(solution)/shard_map/reduce_sum | solution.py:140
  611.9 3.5 copy.75
  615.4 2.7 reshape.143
  618.1 2.6 fusion.21
  (48 shorter events, 5.9 us)
Async XLA Ops:
  7.2 323.4 %copy-start = (bf16[2,192,4096]{2,1,0:T(8,128)(2,1)S(1)}, bf16[2,192,4096]{2,1,0:T(8,128)(2,1)}, u32[]{:S(2)}) copy-start(bf16[2,192,4096]{2,1,0:T(8,128)(2,1)} %param.22) | copy-start | bytes 9437188
  7.2 86.9 %reduce-scatter.2.cloned.1.call-start = ((), (), s32[]{:S(2)}) async-start(), calls=%async_computation.4 | async-start | bytes 1179648 | tf_op jit(solution)/shard_map/reduce_scatter | solution.py:59
  59.8 2.2 copy-start.1
  60.7 3.0 copy-start.8
  60.7 3.2 copy-start.9
  60.7 33.3 %copy-start.2 = (bf16[16,4096]{1,0:T(8,128)(2,1)S(1)}, bf16[16,4096]{1,0:T(8,128)(2,1)}, u32[]{:S(2)}) copy-start(bf16[16,4096]{1,0:T(8,128)(2,1)} %param.15) | copy-start | bytes 393220
  60.7 34.4 %copy-start.7 = (f32[4096]{0:T(1024)S(1)}, f32[4096]{0:T(1024)}, u32[]{:S(2)}) copy-start(f32[4096]{0:T(1024)} %param.17) | copy-start | bytes 49156
  114.4 13.8 %copy-start.6 = (bf16[16,4096]{1,0:T(8,128)(2,1)S(1)}, bf16[16,4096]{1,0:T(8,128)(2,1)}, u32[]{:S(2)}) copy-start(bf16[16,4096]{1,0:T(8,128)(2,1)} %param.23) | copy-start | bytes 393220
  114.4 162.6 %all-to-all-start = ((bf16[2,128,5,4096]{3,0,2,1:T(2,128)(2,1)}), bf16[2,128,5,4096]{3,0,2,1:T(2,128)(2,1)}, u32[]{:S(2)}, u32[]{:S(2)}) async-start(bf16[2,128,5,4096]{3,0,2,1:T(2,128)(2,1)} %bitcast.67), calls=%async_computation.1 | async-start | bytes 20971520 | tf_op jit(solution)/shard_map/all_to_all | solution.py:102
  288.7 155.1 %all-to-all-start.2 = ((bf16[2,128,5,4096]{3,0,2,1:T(2,128)(2,1)}), bf16[2,128,5,4096]{3,0,2,1:T(2,128)(2,1)}, u32[]{:S(2)}, u32[]{:S(2)}) async-start(bf16[2,128,5,4096]{3,0,2,1:T(2,128)(2,1)} %bitcast.66), calls=%async_computation.3 | async-start | bytes 20971520 | tf_op jit(solution)/shard_map/all_to_all | solution.py:105
  295.2 17.6 %copy-start.10 = (bf16[2,192,4096]{2,1,0:T(8,128)(2,1)S(1)}, bf16[2,192,4096]{2,1,0:T(8,128)(2,1)}, u32[]{:S(2)}) copy-start(bf16[2,192,4096]{2,1,0:T(8,128)(2,1)} %param.21) | copy-start | bytes 9437188
  312.8 17.8 %copy-start.11 = (f32[2,640,192]{1,2,0:T(8,128)}, f32[2,640,192]{1,2,0:T(8,128)S(1)}, u32[]{:S(2)}) copy-start(f32[2,640,192]{1,2,0:T(8,128)S(1)} %fusion.10) | copy-start | bytes 2949124
  330.6 3.2 copy-start.4
  443.8 155.1 %all-to-all-start.1 = ((bf16[2,128,5,4096]{3,0,2,1:T(2,128)(2,1)}), bf16[2,128,5,4096]{3,0,2,1:T(2,128)(2,1)}, u32[]{:S(2)}, u32[]{:S(2)}) async-start(bf16[2,128,5,4096]{3,0,2,1:T(2,128)(2,1)} %bitcast.65), calls=%async_computation.2 | async-start | bytes 20971520 | tf_op jit(solution)/shard_map/all_to_all | solution.py:138
  450.0 16.6 %copy-start.5 = (bf16[2,640,192]{1,2,0:T(8,128)(2,1)S(1)}, bf16[2,640,192]{1,2,0:T(8,128)(2,1)}, u32[]{:S(2)}) copy-start(bf16[2,640,192]{1,2,0:T(8,128)(2,1)} %copy-done.4) | copy-start | bytes 1474564
  466.6 18.3 %copy-start.12 = (f32[2,640,192]{1,2,0:T(8,128)S(1)}, f32[2,640,192]{1,2,0:T(8,128)}, u32[]{:S(2)}) copy-start(f32[2,640,192]{1,2,0:T(8,128)} %copy-done.11) | copy-start | bytes 2949124
  484.9 18.4 %copy-start.13 = (f32[2,640,192]{1,2,0:T(8,128)S(1)}, f32[2,640,192]{1,2,0:T(8,128)}, u32[]{:S(2)}) copy-start(f32[2,640,192]{1,2,0:T(8,128)} %get-tuple-element.9) | copy-start | bytes 2949124
  611.9 6.2 copy-start.3
Sparse Core Ops, SparseCore 0:
  63.8 30.1 reduce-scatter.1
where the time goes:
time: 637 us; the launch traced here: 628 us
  waiting for transfers between devices  329 us (52%)
  matrix products  122 us (19%)
  local copies, waits for them, and re-layouts  72.6 us (11%)
  blocking collectives  48 us (8%)
  starting transfers between devices  26.5 us (4%)
  other arithmetic  15.8 us (2%)
  between operations  14.8 us (2%)
    all_to_all x1, waiting for transfers between devices, shards(): lax.all_to_all(spread_out(send_rows), ('ctx', 'tp'), split_axis=1, concat...  140 us
    all_to_all x1, waiting for transfers between devices, shards(): lax.all_to_all(spread_out(send_grads), ('ctx', 'tp'), split_axis=1, conca...  82.3 us
    all_to_all x1, waiting for transfers between devices, shards(): lax.all_to_all(partial_value, ('ctx', 'tp'), split_axis=1, concat_axis=1,...  77.1 us
    broadcast_in_dim x6, local copies, waits for them, and re-layouts, spread_out(): jnp.broadcast_to(block_in[:, :, None], (exp_dev, groups, tensor, capacity...  35.3 us
    reduce_scatter x1, waiting for transfers between devices, shards(): lax.psum_scatter(jnp.dot(attn, out_proj, preferred_element_type=jnp.float...  29.4 us
    convert_element_type x1, local copies, waits for them, and re-layouts, shards(): partial_value = partial_value.astype(jnp.bfloat16).reshape(rows_in.shape)  27.7 us
    all_gather x1, blocking collectives, shards(): key_piece = lax.all_gather(key_mine, 'ctx', axis=0, tiled=True)  25.6 us
    all_gather x1, blocking collectives, shards(): value_piece = lax.all_gather(value_mine, 'ctx', axis=0, tiled=True)  22.4 us
  transfers between devices with their start and end apart: 4, of which 4 were waited for; matrix products, arithmetic and copies ran while one was open for 24% of the time, Pallas kernels for 0%

commit v1 on v0

v1 whole, which is shorter than its diff:
```python
import math

import jax
import jax.numpy as jnp
from jax import lax
from jax.experimental import pallas as pl
from jax.experimental.pallas import tpu as pltpu
from jax.sharding import Mesh
from jax.sharding import PartitionSpec as P

QHEADS = 32
KVHEADS = 2
HEAD = 128
TOPK = 8
CAP = 5
ROWS = 16
META = 128
SIZES = (2, 4, 2, 2, 4)
AXES = ("yh", "z", "k", "yl", "x")
VMEM_LIMIT = 56 * 1024 * 1024


def device_index(yh, z, k, yl, x):
    return (((yh * 4 + z) * 2 + k) * 2 + yl) * 4 + x


def shifted(dims, step):
    pairs = []
    for x in range(4):
        for y in range(4):
            for z in range(4):
                for k in range(2):
                    at = {"x": x, "y": y, "z": z}
                    to = dict(at)
                    to[dims[k]] = (to[dims[k]] + step) % 4
                    pairs.append(
                        (
                            device_index(at["y"] // 2, at["z"], k, at["y"] % 2, at["x"]),
                            device_index(to["y"] // 2, to["z"], k, to["y"] % 2, to["x"]),
                        )
                    )
    return pairs


def send(array, dims, step):
    return lax.ppermute(array, AXES, shifted(dims, step))


def swap_cores(array):
    return lax.ppermute(array, "k", [(0, 1), (1, 0)])


def gather_step(block, dims):
    return [block, send(block, dims, 1), send(block, dims, -1), send(block, dims, 2)]


def gather_last(block, dims):
    half = block.shape[0] // 2
    left = send(block, dims, 1)
    right = send(block, dims, -1)
    return block, left, right, send(left[:half], dims, 1), send(right[half:], dims, -1)


ORDERS = ("xyz", "zxy")


def stage_dims(stage):
    return (ORDERS[0][stage], ORDERS[1][stage])


def gather_chips(block):
    for stage in range(2):
        block = jnp.concatenate(gather_step(block, stage_dims(stage)), 0)
    return gather_last(block, stage_dims(2))


def add(*terms):
    total = terms[0].astype(jnp.float32)
    for term in terms[1:]:
        total = total + term.astype(jnp.float32)
    return total


def scatter_chips(mine, left, right, far_a, far_b):
    dims = stage_dims(2)
    half = far_a.shape[0]
    from_right = send(far_a, dims, -1)
    from_left = send(far_b, dims, 1)
    left = jnp.concatenate([add(left[:half], from_right).astype(jnp.bfloat16), left[half:]], 0)
    right = jnp.concatenate([right[:half], add(right[half:], from_left).astype(jnp.bfloat16)], 0)
    total = add(mine, send(left, dims, -1), send(right, dims, 1))
    for stage in (1, 0):
        dims = stage_dims(stage)
        parts = total.astype(jnp.bfloat16).reshape(4, -1, total.shape[1])
        total = add(
            parts[0], send(parts[1], dims, -1), send(parts[2], dims, 1), send(parts[3], dims, -2)
        )
    return total


def placement(meta, experts, me):
    rows = meta.shape[0]
    slots = rows // ROWS * CAP
    turned = meta.astype(jnp.float32).T
    ids = turned[0:TOPK]
    gates = turned[TOPK : 2 * TOPK] + turned[2 * TOPK : 3 * TOPK] + turned[3 * TOPK : 4 * TOPK]
    token = lax.broadcasted_iota(jnp.int32, (rows, rows), 0)
    later = lax.broadcasted_iota(jnp.int32, (rows, rows), 1)
    earlier = ((token // ROWS == later // ROWS) & (token < later)).astype(jnp.float32)
    block = (lax.broadcasted_iota(jnp.int32, (1, rows), 1) // ROWS).astype(jnp.float32)
    slot_at = lax.broadcasted_iota(jnp.int32, (slots, rows), 0).astype(jnp.float32)
    places, weights = [], []
    for side in range(2):
        for local in range(experts):
            expert = ((me ^ side) * experts + local).astype(jnp.float32)
            named = ids == expert
            hit = jnp.max(named.astype(jnp.float32), axis=0, keepdims=True)
            gate = jnp.sum(jnp.where(named, gates, 0.0), axis=0, keepdims=True)
            rank = jnp.dot(
                jnp.broadcast_to(hit, (8, rows)), earlier, preferred_element_type=jnp.float32
            )[0:1]
            slot = jnp.where(hit > 0.0, block * CAP + rank, -1.0)
            place = (slot_at == slot).astype(jnp.float32)
            places.append(place)
            weights.append(jnp.sum(place * gate, axis=1, keepdims=True))
    return jnp.concatenate(places, 0), jnp.concatenate(weights, 0)


def tiles_of(refs):
    mine, left, right, far_a, far_b = refs
    return [mine[...], left[...], right[...], jnp.concatenate([far_a[...], far_b[...]], 0)]


def store_slots(found, tile, own_ref, other_ref):
    slots = found.shape[0] // 4
    span = pl.ds(tile * slots, slots)
    own_ref[0, span, :] = found[0:slots]
    own_ref[1, span, :] = found[slots : 2 * slots]
    other_ref[0, span, :] = found[2 * slots : 3 * slots]
    other_ref[1, span, :] = found[3 * slots :]


def pack_grads_kernel(me_ref, *refs):
    metas, rows = refs[0:5], refs[5:10]
    own_ref, other_ref, place_ref, weight_ref = refs[10:]

    @pl.when(pl.program_id(0) == 0)
    def _():
        for tile, meta in enumerate(tiles_of(metas)):
            place, weight = placement(meta, 2, me_ref[0])
            place_ref[tile] = place.astype(jnp.bfloat16)
            weight_ref[tile] = jnp.broadcast_to(weight, weight_ref.shape[1:])

    for tile, block in enumerate(tiles_of(rows)):
        found = jnp.dot(place_ref[tile], block, preferred_element_type=jnp.float32)
        found = (found * weight_ref[tile][:, 0:1]).astype(jnp.bfloat16)
        store_slots(found, tile, own_ref, other_ref)


def pack_rows_kernel(place_ref, *refs):
    own_ref, other_ref = refs[5:]
    for tile, block in enumerate(tiles_of(refs[0:5])):
        found = jnp.dot(place_ref[tile], block, preferred_element_type=jnp.float32)
        store_slots(found.astype(jnp.bfloat16), tile, own_ref, other_ref)


def merge_kernel(place_ref, weight_ref, own_ref, other_ref, *outs):
    slots = own_ref.shape[1] // 4
    for tile in range(4):
        span = pl.ds(tile * slots, slots)
        block = jnp.concatenate(
            [own_ref[0, span, :], own_ref[1, span, :], other_ref[0, span, :], other_ref[1, span, :]],
            0,
        )
        scaled = (block.astype(jnp.float32) * weight_ref[tile][:, 0:1]).astype(jnp.bfloat16)
        total = lax.dot_general(
            place_ref[tile], scaled, (((0,), (0,)), ((), ())), preferred_element_type=jnp.float32
        ).astype(jnp.bfloat16)
        if tile < 3:
            outs[tile][...] = total
        else:
            half = total.shape[0] // 2
            outs[3][...] = total[:half]
            outs[4][...] = total[half:]


def params():
    return pltpu.CompilerParams(vmem_limit_bytes=VMEM_LIMIT)


def pack_grads(me, parts, width, chunk):
    part_rows = [part.shape[0] for part in parts]
    tile_rows = part_rows[0]
    slots = tile_rows // ROWS * CAP
    meta_at = width // META
    metas = [pl.BlockSpec((n, META), lambda j: (0, meta_at)) for n in part_rows]
    blocks = [pl.BlockSpec((n, chunk), lambda j: (0, j)) for n in part_rows]
    out_block = pl.BlockSpec((2, 4 * slots, chunk), lambda j: (0, 0, j))
    return pl.pallas_call(
        pack_grads_kernel,
        grid=(width // chunk,),
        in_specs=[pl.BlockSpec(memory_space=pltpu.SMEM)] + metas + blocks,
        out_specs=[
            out_block,
            out_block,
            pl.BlockSpec((4, 4 * slots, tile_rows), lambda j: (0, 0, 0)),
            pl.BlockSpec((4, 4 * slots, META), lambda j: (0, 0, 0)),
        ],
        out_shape=[
            jax.ShapeDtypeStruct((2, 4 * slots, width), jnp.bfloat16),
            jax.ShapeDtypeStruct((2, 4 * slots, width), jnp.bfloat16),
            jax.ShapeDtypeStruct((4, 4 * slots, tile_rows), jnp.bfloat16),
            jax.ShapeDtypeStruct((4, 4 * slots, META), jnp.float32),
        ],
        compiler_params=params(),
    )(me, *parts, *parts)


def pack_rows(place, parts, chunk):
    width = parts[0].shape[1]
    slots = place.shape[1] // 4
    blocks = [pl.BlockSpec((part.shape[0], chunk), lambda j: (0, j)) for part in parts]
    out_block = pl.BlockSpec((2, 4 * slots, chunk), lambda j: (0, 0, j))
    return pl.pallas_call(
        pack_rows_kernel,
        grid=(width // chunk,),
        in_specs=[pl.BlockSpec(place.shape, lambda j: (0, 0, 0))] + blocks,
        out_specs=[out_block, out_block],
        out_shape=[jax.ShapeDtypeStruct((2, 4 * slots, width), jnp.bfloat16)] * 2,
        compiler_params=params(),
    )(place, *parts)


def merge(place, weight, own, other, chunk):
    width = own.shape[2]
    rows = place.shape[2]
    slot_block = pl.BlockSpec((2, own.shape[1], chunk), lambda j: (0, 0, j))
    sizes = [rows, rows, rows, rows // 2, rows // 2]
    return pl.pallas_call(
        merge_kernel,
        grid=(width // chunk,),
        in_specs=[
            pl.BlockSpec(place.shape, lambda j: (0, 0, 0)),
            pl.BlockSpec(weight.shape, lambda j: (0, 0, 0)),
            slot_block,
            slot_block,
        ],
        out_specs=[pl.BlockSpec((n, chunk), lambda j: (0, j)) for n in sizes],
        out_shape=[jax.ShapeDtypeStruct((n, width), jnp.bfloat16) for n in sizes],
        compiler_params=params(),
    )(place, weight, own, other)


def dot_t(a, b):
    return lax.dot_general(a, b, (((1,), (1,)), ((), ())), preferred_element_type=jnp.float32)


def t_dot(a, b):
    return lax.dot_general(a, b, (((0,), (0,)), ((), ())), preferred_element_type=jnp.float32)


def forward_kernel(own_ref, other_ref, wg_ref, wu_ref, wd_ref, *outs):
    for side, rows_ref in enumerate((own_ref, other_ref)):
        out_ref, hidden_ref = outs[side], outs[2]
        gate = dot_t(rows_ref[0], wg_ref[0])
        up = dot_t(rows_ref[0], wu_ref[0])
        hidden_ref[0, side, 0] = gate
        hidden_ref[0, side, 1] = up
        active = (gate * jax.nn.sigmoid(gate) * up).astype(jnp.bfloat16)
        out_ref[0] = jnp.dot(active, wd_ref[0], preferred_element_type=jnp.float32).astype(
            jnp.bfloat16
        )


def forward(own, other, w_gate, w_up, w_down):
    experts, rows, width = own.shape
    hidden = w_gate.shape[1]
    row_block = pl.BlockSpec((1, rows, width), lambda e: (e, 0, 0))
    weight_block = pl.BlockSpec((1, hidden, width), lambda e: (e, 0, 0))
    return pl.pallas_call(
        forward_kernel,
        grid=(experts,),
        in_specs=[row_block, row_block, weight_block, weight_block, weight_block],
        out_specs=[
            row_block,
            row_block,
            pl.BlockSpec((1, 2, 2, rows, hidden), lambda e: (e, 0, 0, 0, 0)),
        ],
        out_shape=[
            jax.ShapeDtypeStruct(own.shape, jnp.bfloat16),
            jax.ShapeDtypeStruct(own.shape, jnp.bfloat16),
            jax.ShapeDtypeStruct((experts, 2, 2, rows, hidden), jnp.float32),
        ],
        compiler_params=params(),
    )(own, other, w_gate, w_up, w_down)


def backward_kernel(
    own_ref, other_ref, gown_ref, gother_ref, wd_ref, hidden_ref, dg_ref, du_ref, dd_ref
):
    d_gates, d_ups, actives = [], [], []
    for side, grads_ref in enumerate((gown_ref, gother_ref)):
        gate, up = hidden_ref[0, side, 0], hidden_ref[0, side, 1]
        sig = jax.nn.sigmoid(gate)
        silu = gate * sig
        back = dot_t(grads_ref[0], wd_ref[0])
        actives.append((silu * up).astype(jnp.bfloat16))
        d_gates.append((back * up * sig * (1.0 + gate * (1.0 - sig))).astype(jnp.bfloat16))
        d_ups.append((back * silu).astype(jnp.bfloat16))
    dd = t_dot(actives[0], gown_ref[0]) + t_dot(actives[1], gother_ref[0])
    dd_ref[0] = dd.astype(jnp.bfloat16)
    dg = t_dot(d_gates[0], own_ref[0]) + t_dot(d_gates[1], other_ref[0])
    dg_ref[0] = dg.astype(jnp.bfloat16)
    du = t_dot(d_ups[0], own_ref[0]) + t_dot(d_ups[1], other_ref[0])
    du_ref[0] = du.astype(jnp.bfloat16)


def backward(own, other, gown, gother, w_down, hidden):
    experts, rows, width = own.shape
    units = w_down.shape[1]
    row_block = pl.BlockSpec((1, rows, width), lambda e: (e, 0, 0))
    weight_block = pl.BlockSpec((1, units, width), lambda e: (e, 0, 0))
    return pl.pallas_call(
        backward_kernel,
        grid=(experts,),
        in_specs=[row_block] * 4
        + [weight_block, pl.BlockSpec((1, 2, 2, rows, units), lambda e: (e, 0, 0, 0, 0))],
        out_specs=[weight_block] * 3,
        out_shape=[jax.ShapeDtypeStruct(w_down.shape, jnp.bfloat16)] * 3,
        compiler_params=params(),
    )(own, other, gown, gother, w_down, hidden)


def gather_keys(pair):
    block = jnp.concatenate([pair, lax.ppermute(pair, "yh", [(0, 1), (1, 0)])], 0)
    block = jnp.concatenate(gather_step(block, "zz"), 0)
    return jnp.concatenate([block, swap_cores(block)], 0)


def key_positions(tok_ctx):
    yh, z, k = (lax.axis_index(name) for name in ("yh", "z", "k"))
    starts = []
    for flip_k in range(2):
        for dz in (0, 3, 1, 2):
            for flip_y in range(2):
                starts.append((((yh ^ flip_y) * 4 + (z + dz) % 4) * 2 + (k ^ flip_k)) * tok_ctx)
    starts = jnp.stack(starts).astype(jnp.int32)
    return (starts[:, None] + jnp.arange(tok_ctx, dtype=jnp.int32)[None, :]).reshape(-1)


def shards(
    queries,
    keys,
    values,
    resid,
    out_proj,
    norm_gain,
    expert_ids,
    gates,
    w_gate,
    w_up,
    w_down,
    cotangent,
):
    width = resid.shape[1]
    chunk = min(512, width)
    yh, z, k, yl = (lax.axis_index(name) for name in ("yh", "z", "k", "yl"))
    ctx = ((yh * 4 + z) * 2 + k).astype(jnp.int32)

    tok_ctx = queries.shape[0]
    heads_dev = queries.shape[1] // HEAD
    key_mine = lax.dynamic_slice_in_dim(keys, yl * HEAD, HEAD, 1)
    value_mine = lax.dynamic_slice_in_dim(values, yl * HEAD, HEAD, 1)
    pairs = gather_keys(jnp.concatenate([key_mine, value_mine], 1))

    rest = gates
    pieces = [expert_ids.astype(jnp.bfloat16)]
    for _ in range(3):
        piece = lax.reduce_precision(rest, 8, 7)
        pieces.append(piece.astype(jnp.bfloat16))
        rest = rest - piece
    pieces.append(jnp.zeros((ROWS, META - 4 * TOPK), jnp.bfloat16))
    cot_parts = gather_chips(jnp.concatenate([cotangent] + pieces, 1))
    me = ctx.reshape(1)
    grads_own, grads_other, place, weight = pack_grads(me, cot_parts, width, chunk)
    grads_got = swap_cores(grads_other)

    key_all, value_all = pairs[:, :HEAD], pairs[:, HEAD:]
    query_pos = ctx * tok_ctx + jnp.arange(tok_ctx, dtype=jnp.int32)
    query_heads = queries.reshape(tok_ctx, heads_dev, HEAD)
    scores = jnp.einsum(
        "qhd,kd->hqk", query_heads, key_all, preferred_element_type=jnp.float32
    ) * (1.0 / math.sqrt(HEAD))
    visible = key_positions(tok_ctx)[None, None, :] <= query_pos[None, :, None]
    top = jnp.max(jnp.where(visible, scores, -1e30), axis=2)
    probs = jnp.where(visible, jnp.exp(scores - top[:, :, None]), 0.0)
    denom = jnp.sum(probs, axis=2)
    heads_out = jnp.einsum(
        "hqk,kd->hqd", probs.astype(jnp.bfloat16), value_all, preferred_element_type=jnp.float32
    )
    heads_out = (heads_out / denom[:, :, None]).astype(jnp.bfloat16)
    attn = jnp.transpose(heads_out, (1, 0, 2)).reshape(tok_ctx, heads_dev * HEAD)
    mixed = jnp.dot(attn, out_proj, preferred_element_type=jnp.float32).astype(jnp.bfloat16)
    mixed = lax.all_to_all(mixed, ("yl", "x"), 0, 0, tiled=True).reshape(8, ROWS, width)
    stream = resid.astype(jnp.float32) + jnp.sum(mixed.astype(jnp.float32), axis=0)
    normed = (
        stream * lax.rsqrt(jnp.mean(stream * stream, axis=1, keepdims=True) + 1e-06) * norm_gain
    ).astype(jnp.bfloat16)

    row_parts = gather_chips(normed)
    rows_own, rows_other = pack_rows(place, row_parts, chunk)
    rows_got = swap_cores(rows_other)
    out_own, out_other, hidden = forward(rows_own, rows_got, w_gate, w_up, w_down)
    out_got = swap_cores(out_other)
    sums = merge(place, weight, out_own, out_got, chunk)
    grad_gate, grad_up, grad_down = backward(
        rows_own, rows_got, grads_own, grads_got, w_down, hidden
    )
    combined = scatter_chips(*sums)
    layer_out = (stream + combined).astype(jnp.bfloat16)
    return layer_out, grad_gate, grad_up, grad_down


def solution(mesh):
    split = Mesh(mesh.devices.reshape(SIZES), AXES)
    ctx, tp = ("yh", "z", "k"), ("yl", "x")
    rows, weights = P(ctx + tp, None), P(ctx, tp, None)
    in_specs = (
        P(ctx, tp),
        P(ctx, None),
        P(ctx, None),
        rows,
        P(tp, None),
        P(),
        rows,
        rows,
        weights,
        weights,
        weights,
        rows,
    )
    return jax.shard_map(
        shards,
        mesh=split,
        in_specs=in_specs,
        out_specs=(rows, weights, weights, weights),
        check_vma=False,
    )
```

time: 637 us -> 305 us (0.48)
  the two profiles are of different devices: /device:TPU:39 before, /device:TPU:0 now
where the time goes in v1:
time: 305 us; the launch traced here: 304 us
  waiting for transfers between devices  134 us (44%)
  Pallas kernels  69.3 us (23%)
  starting transfers between devices  60.1 us (20%)
  local copies, waits for them, and re-layouts  22.3 us (7%)
  matrix products  10.4 us (3%)
  other arithmetic  6.84 us (2%)
    ppermute x33, waiting for transfers between devices, send(): return lax.ppermute(array, AXES, shifted(dims, step))  98.9 us
    ppermute x33, starting transfers between devices, send(): return lax.ppermute(array, AXES, shifted(dims, step))  51.6 us
    pallas_call x1, Pallas kernels, backward(): pl.pallas_call(backward_kernel, grid=(experts,), in_specs=[row_block] * 4...  20.1 us
    ppermute x4, waiting for transfers between devices, swap_cores(): return lax.ppermute(array, 'k', [(0, 1), (1, 0)])  19.1 us
    pallas_call x1, Pallas kernels, forward(): pl.pallas_call(forward_kernel, grid=(experts,), in_specs=[row_block, row_...  14.6 us
    all_to_all x1, waiting for transfers between devices, shards(): lax.all_to_all(mixed, ('yl', 'x'), 0, 0, tiled=True).reshape(8, ROWS, width)  13.9 us
    unnamed x61, local copies, waits for them, and re-layouts  13.4 us
    pallas_call x1, Pallas kernels, pack_grads(): pl.pallas_call(pack_grads_kernel, grid=(width // chunk,), in_specs=[pl.Bl...  12.1 us
  transfers between devices with their start and end apart: 39, of which 18 were waited for; matrix products, arithmetic and copies ran while one was open for 9% of the time, Pallas kernels for 11%

profile of v1, /device:TPU:0, one launch (start us, length us, event | category | flops | bytes accessed | tf_op | source)
XLA Modules:
  0.0 304.0 jit_solution(1708194149592271294)
XLA Ops:
  10.6 3.2 %collective-permute-start = (bf16[128,256]{1,0:T(8,128)(2,1)S(1)}, bf16[128,256]{1,0:T(8,128)(2,1)S(1)}, u32[]{:S(2)}, u32[]{:S(2)}) collective-permute-start(bf16[128,256]{1,0:T(8,128)(2,1)S(1)} %get-tuple-element.56), channel_id=1, source_target_pairs={{0,64},{64,0},{1,65},{65,1},{2,66},{66,2},{3,67},{67,3},{4,68},{68... | collective-permute-start | bytes 196616 | tf_op jit(solution)/shard_map/ppermute | solution.py:335
  18.4 2.2 collective-permute-start.2
  34.3 4.3 %fusion.36 = (f32[4,128]{1,0:T(4,128)S(1)}, bf16[4,128,2048]{1,2,0:T(8,128)(2,1)}) fusion(pred[128,2048]{0,1:T(8,128)(4,1)S(1)} %broadcast_compare_fusion, bf16[2048,256]{1,0:T(8,128)(2,1)} %constant_dynamic-update-slice_fusion.5, bf16[128,512]{1,0:T(8,128)(2,1)S(1)} %copy-done), kind=kOutput, calls=%fused_computation.78 | convolution fusion | flops 544212992 | bytes 3934208 | tf_op jit(solution)/shard_map/sub | solution.py:396
  40.9 3.9 %convolution_convert_fusion = bf16[128,4096]{1,0:T(8,128)(2,1)} fusion(bf16[128,512]{0,1:T(8,128)(2,1)S(1)} %bitcast.80, bf16[512,4096]{1,0:T(8,128)(2,1)} %param.16), kind=kOutput, calls=%fused_computation.1 | convolution fusion | flops 537395200 | bytes 5373952 | tf_op jit(solution)/shard_map/dot_general | solution.py:403
  44.8 3.6 %all-to-all-start = ((bf16[8,16,4096]{2,1,0:T(8,128)(2,1)}), bf16[8,16,4096]{2,1,0:T(8,128)(2,1)S(1)}, u32[]{:S(2)}, u32[]{:S(2)}) async-start(bf16[8,16,4096]{2,1,0:T(8,128)(2,1)} %bitcast.79), calls=%async_computation | async-start | bytes 2097152 | tf_op jit(solution)/shard_map/all_to_all | solution.py:404
  50.6 13.9 %all-to-all-done = bf16[8,16,4096]{2,1,0:T(8,128)(2,1)S(1)} async-done(((bf16[8,16,4096]{2,1,0:T(8,128)(2,1)}), bf16[8,16,4096]{2,1,0:T(8,128)(2,1)S(1)}, u32[]{:S(2)}, u32[]{:S(2)}) %all-to-all-start) | async-done | bytes 1048608 | tf_op jit(solution)/shard_map/all_to_all | solution.py:404
  65.9 2.4 collective-permute-start.16
  70.5 2.2 collective-permute-start.12
  75.4 2.7 collective-permute-start.19
  78.5 13.6 %collective-permute-done.18 = bf16[64,4096]{1,0:T(8,128)(2,1)S(1)} collective-permute-done((bf16[64,4096]{1,0:T(8,128)(2,1)S(1)}, bf16[64,4096]{1,0:T(8,128)(2,1)S(1)}, u32[]{:S(2)}, u32[]{:S(2)}) %collective-permute-start.18) | collective-permute-done | bytes 524320 | tf_op jit(solution)/shard_map/ppermute | solution.py:46
  92.2 8.8 %collective-permute-done.20 = bf16[64,4096]{1,0:T(8,128)(2,1)S(1)} collective-permute-done((bf16[64,4096]{1,0:T(8,128)(2,1)S(1)}, bf16[64,4096]{1,0:T(8,128)(2,1)S(1)}, u32[]{:S(2)}, u32[]{:S(2)}) %collective-permute-start.20) | collective-permute-done | bytes 524320 | tf_op jit(solution)/shard_map/ppermute | solution.py:46
  105.7 2.2 collective-permute-start.14
  108.0 20.5 %collective-permute-done.21.refs_1_ = bf16[256,4096]{1,0:T(8,128)(2,1)S(1)} collective-permute-done((bf16[256,4096]{1,0:T(8,128)(2,1)S(1)}, bf16[256,4096]{1,0:T(8,128)(2,1)S(1)}, u32[]{:S(2)}, u32[]{:S(2)}) %collective-permute-start.21) | collective-permute-done | bytes 2097184 | tf_op jit(solution)/shard_map/ppermute | solution.py:46
  131.0 3.0 collective-permute-start.24
  134.0 6.0 %collective-permute-done.13.refs_3_.refs_8_ = bf16[128,4224]{1,0:T(8,128)(2,1)S(1)} collective-permute-done((bf16[128,4224]{1,0:T(8,128)(2,1)S(1)}, bf16[128,4224]{1,0:T(8,128)(2,1)S(1)}, u32[]{:S(2)}, u32[]{:S(2)}) %collective-permute-start.13) | collective-permute-done | bytes 1081376 | tf_op jit(solution)/shard_map/ppermute | solution.py:46
  141.4 12.1 %shard_map.147 = (bf16[2,320,4096]{2,1,0:T(8,128)(2,1)}, bf16[2,320,4096]{2,1,0:T(8,128)(2,1)}, bf16[4,320,256]{2,1,0:T(8,128)(2,1)}, f32[4,320,128]{2,1,0:T(8,128)}) custom-call(s32[1]{0:T(128)} %bitcast.24.me_ref, bf16[256,4224]{1,0:T(8,128)(2,1)} %copy-done.5, bf16[256,4224]{1,0:T(8,128)(2,1)} %copy-done.3, bf16[256,4224]{1,0:T(8,128)(2,1)} %copy-done.4, ...), custom_call_target="tpu_custom_call" | custom-call | tf_op jit(solution)/shard_map/pallas_call | solution.py:199
  154.9 11.6 %shard_map.148 = (bf16[2,320,4096]{2,1,0:T(8,128)(2,1)}, bf16[2,320,4096]{2,1,0:T(8,128)(2,1)}) custom-call(bf16[4,320,256]{2,1,0:T(8,128)(2,1)} %get-tuple-element.21.place_ref, bf16[256,4096]{1,0:T(8,128)(2,1)} %copy-done.13, bf16[256,4096]{1,0:T(8,128)(2,1)} %copy-done.7, bf16[256,4096]{1,0:T(8,128)(2,1)} %copy-done.8, bf16[128,4096]{1,0:T(8,128)(2,1)} %copy-done.18, ...), custom_call_target="tpu_custom_call" | custom-call | tf_op jit(solution)/shard_map/pallas_call | solution.py:224
  167.8 8.5 %collective-permute-done.25.other_ref = bf16[2,320,4096]{2,1,0:T(8,128)(2,1)S(1)} collective-permute-done((bf16[2,320,4096]{2,1,0:T(8,128)(2,1)}, bf16[2,320,4096]{2,1,0:T(8,128)(2,1)S(1)}, u32[]{:S(2)}, u32[]{:S(2)}) %collective-permute-start.25) | collective-permute-done | bytes 5242912 | tf_op jit(solution)/shard_map/ppermute | solution.py:50
  176.3 2.3 copy-done.2
  178.6 14.6 %shard_map.149 = (bf16[2,320,4096]{2,1,0:T(8,128)(2,1)}, bf16[2,320,4096]{2,1,0:T(8,128)(2,1)}, f32[2,2,2,320,192]{4,3,2,1,0:T(8,128)}) custom-call(bf16[2,320,4096]{2,1,0:T(8,128)(2,1)} %get-tuple-element.23.own_ref, bf16[2,320,4096]{2,1,0:T(8,128)(2,1)} %copy-done.2, bf16[2,192,4096]{2,1,0:T(8,128)(2,1)} %wg_ref.1, bf16[2,192,4096]{2,1,0:T(8,128)(2,1)} %wu_ref.1, ...), custom_call_target="tpu_custom_call" | custom-call | tf_op jit(solution)/shard_map/pallas_call | solution.py:280
  193.6 8.5 %collective-permute-done.26.other_ref = bf16[2,320,4096]{2,1,0:T(8,128)(2,1)S(1)} collective-permute-done((bf16[2,320,4096]{2,1,0:T(8,128)(2,1)}, bf16[2,320,4096]{2,1,0:T(8,128)(2,1)S(1)}, u32[]{:S(2)}, u32[]{:S(2)}) %collective-permute-start.26) | collective-permute-done | bytes 5242912 | tf_op jit(solution)/shard_map/ppermute | solution.py:50
  202.1 2.4 copy-done.6
  204.4 10.9 %shard_map.150 = (bf16[256,4096]{1,0:T(8,128)(2,1)}, bf16[256,4096]{1,0:T(8,128)(2,1)}, bf16[256,4096]{1,0:T(8,128)(2,1)}, bf16[128,4096]{1,0:T(8,128)(2,1)}, bf16[128,4096]{1,0:T(8,128)(2,1)}) custom-call(bf16[4,320,256]{2,1,0:T(8,128)(2,1)} %get-tuple-element.21.place_ref, f32[4,320,128]{2,1,0:T(8,128)} %get-tuple-element.22.weight_ref, ...), custom_call_target="tpu_custom_call" | custom-call | tf_op jit(solution)/shard_map/pallas_call | solution.py:239
  217.3 2.8 collective-permute-start.27
  220.1 11.5 %collective-permute-done.29 = bf16[128,4096]{1,0:T(8,128)(2,1)S(1)} collective-permute-done((bf16[128,4096]{1,0:T(8,128)(2,1)}, bf16[128,4096]{1,0:T(8,128)(2,1)S(1)}, u32[]{:S(2)}, u32[]{:S(2)}) %collective-permute-start.29) | collective-permute-done | bytes 1048608 | tf_op jit(solution)/shard_map/ppermute | solution.py:46
  233.3 3.7 %collective-permute-start.28 = (bf16[256,4096]{1,0:T(8,128)(2,1)S(1)}, bf16[256,4096]{1,0:T(8,128)(2,1)S(1)}, u32[]{:S(2)}, u32[]{:S(2)}) collective-permute-start(bf16[256,4096]{1,0:T(8,128)(2,1)S(1)} %pad_maximum_fusion), channel_id=1, source_target_pairs={{0,48},{8,76},{16,0},{24,92},{32,16},{40,108},{48,32},{56,124},{4,... | collective-permute-start | bytes 6291464 | tf_op jit(solution)/shard_map/ppermute | solution.py:46
  236.9 22.5 %collective-permute-done.30 = bf16[256,4096]{1,0:T(8,128)(2,1)S(1)} collective-permute-done((bf16[256,4096]{1,0:T(8,128)(2,1)S(1)}, bf16[256,4096]{1,0:T(8,128)(2,1)S(1)}, u32[]{:S(2)}, u32[]{:S(2)}) %collective-permute-start.30) | collective-permute-done | bytes 2097184 | tf_op jit(solution)/shard_map/ppermute | solution.py:46
  263.2 2.5 collective-permute-start.32
  266.4 6.2 %collective-permute-done.33 = bf16[64,4096]{1,0:T(8,128)(2,1)S(1)} collective-permute-done((bf16[64,4096]{1,0:T(8,128)(2,1)S(1)}, bf16[64,4096]{1,0:T(8,128)(2,1)S(1)}, u32[]{:S(2)}, u32[]{:S(2)}) %collective-permute-start.33) | collective-permute-done | bytes 524320 | tf_op jit(solution)/shard_map/ppermute | solution.py:46
  272.6 5.5 %collective-permute-done.32 = bf16[64,4096]{1,0:T(8,128)(2,1)S(1)} collective-permute-done((bf16[64,4096]{1,0:T(8,128)(2,1)S(1)}, bf16[64,4096]{1,0:T(8,128)(2,1)S(1)}, u32[]{:S(2)}, u32[]{:S(2)}) %collective-permute-start.32) | collective-permute-done | bytes 524320 | tf_op jit(solution)/shard_map/ppermute | solution.py:46
  280.3 2.8 collective-permute-start.34
  283.1 20.1 %shard_map.151 = (bf16[2,192,4096]{2,1,0:T(8,128)(2,1)}, bf16[2,192,4096]{2,1,0:T(8,128)(2,1)}, bf16[2,192,4096]{2,1,0:T(8,128)(2,1)}) custom-call(bf16[2,320,4096]{2,1,0:T(8,128)(2,1)} %get-tuple-element.23.own_ref, bf16[2,320,4096]{2,1,0:T(8,128)(2,1)} %copy-done.2, bf16[2,320,4096]{2,1,0:T(8,128)(2,1)} %get-tuple-element.32.gown_ref, ...), custom_call_target="tpu_custom_call" | custom-call | tf_op jit(solution)/shard_map/pallas_call | solution.py:323
  (155 shorter events, 61.9 us)
Async XLA Ops:
  4.0 17.3 %collective-permute-start.5 = (bf16[16,4224]{1,0:T(8,128)(2,1)S(1)}, bf16[16,4224]{1,0:T(8,128)(2,1)S(1)}, u32[]{:S(2)}, u32[]{:S(2)}) collective-permute-start(bf16[16,4224]{1,0:T(8,128)(2,1)S(1)} %concatenate.41), channel_id=1, source_target_pairs={{0,1},{8,24},{16,17},{24,40},{32,33},{40,56},{48,49},{56,8},{4,5},... | collective-permute-start | bytes 405512 | tf_op jit(solution)/shard_map/ppermute | solution.py:46
  5.6 17.4 %collective-permute-start.6 = (bf16[16,4224]{1,0:T(8,128)(2,1)S(1)}, bf16[16,4224]{1,0:T(8,128)(2,1)S(1)}, u32[]{:S(2)}, u32[]{:S(2)}) collective-permute-start(bf16[16,4224]{1,0:T(8,128)(2,1)S(1)} %concatenate.41), channel_id=1, source_target_pairs={{0,3},{8,56},{16,19},{24,8},{32,35},{40,24},{48,51},{56,40},{4,7},... | collective-permute-start | bytes 405512 | tf_op jit(solution)/shard_map/ppermute | solution.py:46
  7.3 15.8 %collective-permute-start.7 = (bf16[16,4224]{1,0:T(8,128)(2,1)S(1)}, bf16[16,4224]{1,0:T(8,128)(2,1)S(1)}, u32[]{:S(2)}, u32[]{:S(2)}) collective-permute-start(bf16[16,4224]{1,0:T(8,128)(2,1)S(1)} %concatenate.41), channel_id=1, source_target_pairs={{0,2},{8,40},{16,18},{24,56},{32,34},{40,8},{48,50},{56,24},{4,6},... | collective-permute-start | bytes 405512 | tf_op jit(solution)/shard_map/ppermute | solution.py:46
  16.4 10.8 %collective-permute-start.1 = (bf16[256,256]{1,0:T(8,128)(2,1)S(1)}, bf16[256,256]{1,0:T(8,128)(2,1)S(1)}, u32[]{:S(2)}, u32[]{:S(2)}) collective-permute-start(bf16[256,256]{1,0:T(8,128)(2,1)S(1)} %pad_maximum_fusion.4), channel_id=1, source_target_pairs={{0,16},{8,24},{16,32},{24,40},{32,48},{40,56},{48,0},{56,8},{4,20}... | collective-permute-start | bytes 393224 | tf_op jit(solution)/shard_map/ppermute | solution.py:46
  18.4 11.6 %collective-permute-start.2 = (bf16[256,256]{1,0:T(8,128)(2,1)S(1)}, bf16[256,256]{1,0:T(8,128)(2,1)S(1)}, u32[]{:S(2)}, u32[]{:S(2)}) collective-permute-start(bf16[256,256]{1,0:T(8,128)(2,1)S(1)} %pad_maximum_fusion.4), channel_id=1, source_target_pairs={{0,48},{8,56},{16,0},{24,8},{32,16},{40,24},{48,32},{56,40},{4,52}... | collective-permute-start | bytes 393224 | tf_op jit(solution)/shard_map/ppermute | solution.py:46
  23.9 24.5 %collective-permute-start.8 = (bf16[64,4224]{1,0:T(8,128)(2,1)}, bf16[64,4224]{1,0:T(8,128)(2,1)}, u32[]{:S(2)}, u32[]{:S(2)}) collective-permute-start(bf16[64,4224]{1,0:T(8,128)(2,1)} %pad_maximum_fusion.2), channel_id=1, source_target_pairs={{0,4},{8,9},{16,20},{24,25},{32,36},{40,41},{48,52},{56,57},{4,64}... | collective-permute-start | bytes 1622024 | tf_op jit(solution)/shard_map/ppermute | solution.py:46
  25.5 24.1 %collective-permute-start.9 = (bf16[64,4224]{1,0:T(8,128)(2,1)}, bf16[64,4224]{1,0:T(8,128)(2,1)}, u32[]{:S(2)}, u32[]{:S(2)}) collective-permute-start(bf16[64,4224]{1,0:T(8,128)(2,1)} %pad_maximum_fusion.2), channel_id=1, source_target_pairs={{0,68},{8,11},{16,84},{24,27},{32,100},{40,43},{48,116},{56,59},{4... | collective-permute-start | bytes 1622024 | tf_op jit(solution)/shard_map/ppermute | solution.py:46
  27.2 41.1 %collective-permute-start.10 = (bf16[64,4224]{1,0:T(8,128)(2,1)}, bf16[64,4224]{1,0:T(8,128)(2,1)}, u32[]{:S(2)}, u32[]{:S(2)}) collective-permute-start(bf16[64,4224]{1,0:T(8,128)(2,1)} %pad_maximum_fusion.2), channel_id=1, source_target_pairs={{0,64},{8,10},{16,80},{24,26},{32,96},{40,42},{48,112},{56,58},{4,... | collective-permute-start | bytes 1622024 | tf_op jit(solution)/shard_map/ppermute | solution.py:46
  44.8 19.8 %all-to-all-start = ((bf16[8,16,4096]{2,1,0:T(8,128)(2,1)}), bf16[8,16,4096]{2,1,0:T(8,128)(2,1)S(1)}, u32[]{:S(2)}, u32[]{:S(2)}) async-start(bf16[8,16,4096]{2,1,0:T(8,128)(2,1)} %bitcast.79), calls=%async_computation | async-start | bytes 2097152 | tf_op jit(solution)/shard_map/all_to_all | solution.py:404
  69.4 35.0 %collective-permute-start.11 = (bf16[256,4224]{1,0:T(8,128)(2,1)S(1)}, bf16[256,4224]{1,0:T(8,128)(2,1)S(1)}, u32[]{:S(2)}, u32[]{:S(2)}) collective-permute-start(bf16[256,4224]{1,0:T(8,128)(2,1)S(1)} %constant_dynamic-update-slice_fusion.11.refs_0_.refs_5_), channel_id=1, source_target_pairs={{0,16},{8,12},{16,32},{24,28},{32,48},{40,44},{48,0},{56,60},{4,20... | collective-permute-start | bytes 6488072 | tf_op jit(solution)/shard_map/ppermute | solution.py:46
  70.5 34.3 %collective-permute-start.12 = (bf16[256,4224]{1,0:T(8,128)(2,1)S(1)}, bf16[256,4224]{1,0:T(8,128)(2,1)S(1)}, u32[]{:S(2)}, u32[]{:S(2)}) collective-permute-start(bf16[256,4224]{1,0:T(8,128)(2,1)S(1)} %constant_dynamic-update-slice_fusion.11.refs_0_.refs_5_), channel_id=1, source_target_pairs={{0,48},{8,76},{16,0},{24,92},{32,16},{40,108},{48,32},{56,124},{4,... | collective-permute-start | bytes 6488072 | tf_op jit(solution)/shard_map/ppermute | solution.py:46
  74.8 17.3 %collective-permute-start.18 = (bf16[64,4096]{1,0:T(8,128)(2,1)S(1)}, bf16[64,4096]{1,0:T(8,128)(2,1)S(1)}, u32[]{:S(2)}, u32[]{:S(2)}) collective-permute-start(bf16[64,4096]{1,0:T(8,128)(2,1)S(1)} %pad_maximum_fusion.3), channel_id=1, source_target_pairs={{0,4},{8,9},{16,20},{24,25},{32,36},{40,41},{48,52},{56,57},{4,64}... | collective-permute-start | bytes 1572872 | tf_op jit(solution)/shard_map/ppermute | solution.py:46
  75.4 16.7 %collective-permute-start.19 = (bf16[64,4096]{1,0:T(8,128)(2,1)S(1)}, bf16[64,4096]{1,0:T(8,128)(2,1)S(1)}, u32[]{:S(2)}, u32[]{:S(2)}) collective-permute-start(bf16[64,4096]{1,0:T(8,128)(2,1)S(1)} %pad_maximum_fusion.3), channel_id=1, source_target_pairs={{0,68},{8,11},{16,84},{24,27},{32,100},{40,43},{48,116},{56,59},{4... | collective-permute-start | bytes 1572872 | tf_op jit(solution)/shard_map/ppermute | solution.py:46
  78.1 22.9 %collective-permute-start.20 = (bf16[64,4096]{1,0:T(8,128)(2,1)S(1)}, bf16[64,4096]{1,0:T(8,128)(2,1)S(1)}, u32[]{:S(2)}, u32[]{:S(2)}) collective-permute-start(bf16[64,4096]{1,0:T(8,128)(2,1)S(1)} %pad_maximum_fusion.3), channel_id=1, source_target_pairs={{0,64},{8,10},{16,80},{24,26},{32,96},{40,42},{48,112},{56,58},{4,... | collective-permute-start | bytes 1572872 | tf_op jit(solution)/shard_map/ppermute | solution.py:46
  101.1 27.3 %collective-permute-start.21 = (bf16[256,4096]{1,0:T(8,128)(2,1)S(1)}, bf16[256,4096]{1,0:T(8,128)(2,1)S(1)}, u32[]{:S(2)}, u32[]{:S(2)}) collective-permute-start(bf16[256,4096]{1,0:T(8,128)(2,1)S(1)} %constant_dynamic-update-slice_fusion.18.refs_0_), channel_id=1, source_target_pairs={{0,16},{8,12},{16,32},{24,28},{32,48},{40,44},{48,0},{56,60},{4,20... | collective-permute-start | bytes 6291464 | tf_op jit(solution)/shard_map/ppermute | solution.py:46
  102.6 27.2 %collective-permute-start.22 = (bf16[256,4096]{1,0:T(8,128)(2,1)S(1)}, bf16[256,4096]{1,0:T(8,128)(2,1)S(1)}, u32[]{:S(2)}, u32[]{:S(2)}) collective-permute-start(bf16[256,4096]{1,0:T(8,128)(2,1)S(1)} %constant_dynamic-update-slice_fusion.18.refs_0_), channel_id=1, source_target_pairs={{0,48},{8,76},{16,0},{24,92},{32,16},{40,108},{48,32},{56,124},{4,... | collective-permute-start | bytes 6291464 | tf_op jit(solution)/shard_map/ppermute | solution.py:46
  104.5 35.5 %collective-permute-start.13 = (bf16[128,4224]{1,0:T(8,128)(2,1)S(1)}, bf16[128,4224]{1,0:T(8,128)(2,1)S(1)}, u32[]{:S(2)}, u32[]{:S(2)}) collective-permute-start(bf16[128,4224]{1,0:T(8,128)(2,1)S(1)} %slice.82), channel_id=1, source_target_pairs={{0,16},{8,12},{16,32},{24,28},{32,48},{40,44},{48,0},{56,60},{4,20... | collective-permute-start | bytes 3244040 | tf_op jit(solution)/shard_map/ppermute | solution.py:46
  105.7 34.5 %collective-permute-start.14 = (bf16[128,4224]{1,0:T(8,128)(2,1)S(1)}, bf16[128,4224]{1,0:T(8,128)(2,1)S(1)}, u32[]{:S(2)}, u32[]{:S(2)}) collective-permute-start(bf16[128,4224]{1,0:T(8,128)(2,1)S(1)} %slice.83), channel_id=1, source_target_pairs={{0,48},{8,76},{16,0},{24,92},{32,16},{40,108},{48,32},{56,124},{4,... | collective-permute-start | bytes 3244040 | tf_op jit(solution)/shard_map/ppermute | solution.py:46
  129.6 24.0 %collective-permute-start.23 = (bf16[128,4096]{1,0:T(8,128)(2,1)}, bf16[128,4096]{1,0:T(8,128)(2,1)S(1)}, u32[]{:S(2)}, u32[]{:S(2)}) collective-permute-start(bf16[128,4096]{1,0:T(8,128)(2,1)} %slice.84), channel_id=1, source_target_pairs={{0,16},{8,12},{16,32},{24,28},{32,48},{40,44},{48,0},{56,60},{4,20... | collective-permute-start | bytes 3145736 | tf_op jit(solution)/shard_map/ppermute | solution.py:46
  131.0 22.6 %collective-permute-start.24 = (bf16[128,4096]{1,0:T(8,128)(2,1)}, bf16[128,4096]{1,0:T(8,128)(2,1)S(1)}, u32[]{:S(2)}, u32[]{:S(2)}) collective-permute-start(bf16[128,4096]{1,0:T(8,128)(2,1)} %slice.85), channel_id=1, source_target_pairs={{0,48},{8,76},{16,0},{24,92},{32,16},{40,108},{48,32},{56,124},{4,... | collective-permute-start | bytes 3145736 | tf_op jit(solution)/shard_map/ppermute | solution.py:46
  166.4 9.9 %collective-permute-start.25 = (bf16[2,320,4096]{2,1,0:T(8,128)(2,1)}, bf16[2,320,4096]{2,1,0:T(8,128)(2,1)S(1)}, u32[]{:S(2)}, u32[]{:S(2)}) collective-permute-start(bf16[2,320,4096]{2,1,0:T(8,128)(2,1)} %get-tuple-element.24), channel_id=1, source_target_pairs={{0,8},{8,0},{1,9},{9,1},{2,10},{10,2},{3,11},{11,3},{4,12},{12,4},... | collective-permute-start | bytes 15728648 | tf_op jit(solution)/shard_map/ppermute | solution.py:50
  215.3 16.3 %collective-permute-start.29 = (bf16[128,4096]{1,0:T(8,128)(2,1)}, bf16[128,4096]{1,0:T(8,128)(2,1)S(1)}, u32[]{:S(2)}, u32[]{:S(2)}) collective-permute-start(bf16[128,4096]{1,0:T(8,128)(2,1)} %get-tuple-element.31), channel_id=1, source_target_pairs={{0,16},{8,12},{16,32},{24,28},{32,48},{40,44},{48,0},{56,60},{4,20... | collective-permute-start | bytes 3145736 | tf_op jit(solution)/shard_map/ppermute | solution.py:46
  217.3 15.5 %collective-permute-start.27 = (bf16[128,4096]{1,0:T(8,128)(2,1)}, bf16[128,4096]{1,0:T(8,128)(2,1)S(1)}, u32[]{:S(2)}, u32[]{:S(2)}) collective-permute-start(bf16[128,4096]{1,0:T(8,128)(2,1)} %get-tuple-element.29), channel_id=1, source_target_pairs={{0,48},{8,76},{16,0},{24,92},{32,16},{40,108},{48,32},{56,124},{4,... | collective-permute-start | bytes 3145736 | tf_op jit(solution)/shard_map/ppermute | solution.py:46
  232.1 27.3 %collective-permute-start.30 = (bf16[256,4096]{1,0:T(8,128)(2,1)S(1)}, bf16[256,4096]{1,0:T(8,128)(2,1)S(1)}, u32[]{:S(2)}, u32[]{:S(2)}) collective-permute-start(bf16[256,4096]{1,0:T(8,128)(2,1)S(1)} %pad_maximum_fusion.1), channel_id=1, source_target_pairs={{0,16},{8,12},{16,32},{24,28},{32,48},{40,44},{48,0},{56,60},{4,20... | collective-permute-start | bytes 6291464 | tf_op jit(solution)/shard_map/ppermute | solution.py:46
  233.3 27.2 %collective-permute-start.28 = (bf16[256,4096]{1,0:T(8,128)(2,1)S(1)}, bf16[256,4096]{1,0:T(8,128)(2,1)S(1)}, u32[]{:S(2)}, u32[]{:S(2)}) collective-permute-start(bf16[256,4096]{1,0:T(8,128)(2,1)S(1)} %pad_maximum_fusion), channel_id=1, source_target_pairs={{0,48},{8,76},{16,0},{24,92},{32,16},{40,108},{48,32},{56,124},{4,... | collective-permute-start | bytes 6291464 | tf_op jit(solution)/shard_map/ppermute | solution.py:46
  236.9 46.2 %collective-permute-start.37 = (bf16[2,320,4096]{2,1,0:T(8,128)(2,1)S(1)}, bf16[2,320,4096]{2,1,0:T(8,128)(2,1)}, u32[]{:S(2)}, u32[]{:S(2)}) collective-permute-start(bf16[2,320,4096]{2,1,0:T(8,128)(2,1)S(1)} %bitcast.82), channel_id=1, source_target_pairs={{0,8},{8,0},{1,9},{9,1},{2,10},{10,2},{3,11},{11,3},{4,12},{12,4},... | collective-permute-start | bytes 15728648 | tf_op jit(solution)/shard_map/ppermute | solution.py:50
  261.8 10.9 %collective-permute-start.33 = (bf16[64,4096]{1,0:T(8,128)(2,1)S(1)}, bf16[64,4096]{1,0:T(8,128)(2,1)S(1)}, u32[]{:S(2)}, u32[]{:S(2)}) collective-permute-start(bf16[64,4096]{1,0:T(8,128)(2,1)S(1)} %get-tuple-element.41), channel_id=1, source_target_pairs={{0,64},{8,10},{16,80},{24,26},{32,96},{40,42},{48,112},{56,58},{4,... | collective-permute-start | bytes 1572872 | tf_op jit(solution)/shard_map/ppermute | solution.py:46
  263.2 15.0 %collective-permute-start.32 = (bf16[64,4096]{1,0:T(8,128)(2,1)S(1)}, bf16[64,4096]{1,0:T(8,128)(2,1)S(1)}, u32[]{:S(2)}, u32[]{:S(2)}) collective-permute-start(bf16[64,4096]{1,0:T(8,128)(2,1)S(1)} %get-tuple-element.42), channel_id=1, source_target_pairs={{0,4},{8,9},{16,20},{24,25},{32,36},{40,41},{48,52},{56,57},{4,64}... | collective-permute-start | bytes 1572872 | tf_op jit(solution)/shard_map/ppermute | solution.py:46
  265.7 12.8 %collective-permute-start.31 = (bf16[64,4096]{1,0:T(8,128)(2,1)S(1)}, bf16[64,4096]{1,0:T(8,128)(2,1)S(1)}, u32[]{:S(2)}, u32[]{:S(2)}) collective-permute-start(bf16[64,4096]{1,0:T(8,128)(2,1)S(1)} %get-tuple-element.40), channel_id=1, source_target_pairs={{0,68},{8,11},{16,84},{24,27},{32,100},{40,43},{48,116},{56,59},{4... | collective-permute-start | bytes 1572872 | tf_op jit(solution)/shard_map/ppermute | solution.py:46
  278.8 24.4 %collective-permute-start.36 = (bf16[16,4096]{1,0:T(8,128)(2,1)S(1)}, bf16[16,4096]{1,0:T(8,128)(2,1)S(1)}, u32[]{:S(2)}, u32[]{:S(2)}) collective-permute-start(bf16[16,4096]{1,0:T(8,128)(2,1)S(1)} %get-tuple-element.44), channel_id=1, source_target_pairs={{0,2},{8,40},{16,18},{24,56},{32,34},{40,8},{48,50},{56,24},{4,6},... | collective-permute-start | bytes 393224 | tf_op jit(solution)/shard_map/ppermute | solution.py:46
  279.9 23.4 %collective-permute-start.35 = (bf16[16,4096]{1,0:T(8,128)(2,1)S(1)}, bf16[16,4096]{1,0:T(8,128)(2,1)S(1)}, u32[]{:S(2)}, u32[]{:S(2)}) collective-permute-start(bf16[16,4096]{1,0:T(8,128)(2,1)S(1)} %get-tuple-element.45), channel_id=1, source_target_pairs={{0,1},{8,24},{16,17},{24,40},{32,33},{40,56},{48,49},{56,8},{4,5},... | collective-permute-start | bytes 393224 | tf_op jit(solution)/shard_map/ppermute | solution.py:46
  280.3 22.9 %collective-permute-start.34 = (bf16[16,4096]{1,0:T(8,128)(2,1)S(1)}, bf16[16,4096]{1,0:T(8,128)(2,1)S(1)}, u32[]{:S(2)}, u32[]{:S(2)}) collective-permute-start(bf16[16,4096]{1,0:T(8,128)(2,1)S(1)} %get-tuple-element.43), channel_id=1, source_target_pairs={{0,3},{8,56},{16,19},{24,8},{32,35},{40,24},{48,51},{56,40},{4,7},... | collective-permute-start | bytes 393224 | tf_op jit(solution)/shard_map/ppermute | solution.py:46
  (30 other events, 389.2 us)

commit v2 on v1

v2 whole, which is shorter than its diff:
```python
import math

import jax
import jax.numpy as jnp
from jax import lax
from jax.experimental import pallas as pl
from jax.experimental.pallas import tpu as pltpu
from jax.sharding import Mesh
from jax.sharding import PartitionSpec as P

QHEADS = 32
KVHEADS = 2
HEAD = 128
TOPK = 8
CAP = 5
ROWS = 16
META = 128
SIZES = (2, 4, 2, 2, 4)
AXES = ("yh", "z", "k", "yl", "x")


def device_index(yh, z, k, yl, x):
    return (((yh * 4 + z) * 2 + k) * 2 + yl) * 4 + x


def shifted(dims, step):
    pairs = []
    for x in range(4):
        for y in range(4):
            for z in range(4):
                for k in range(2):
                    at = {"x": x, "y": y, "z": z}
                    to = dict(at)
                    to[dims[k]] = (to[dims[k]] + step) % 4
                    pairs.append(
                        (
                            device_index(at["y"] // 2, at["z"], k, at["y"] % 2, at["x"]),
                            device_index(to["y"] // 2, to["z"], k, to["y"] % 2, to["x"]),
                        )
                    )
    return pairs


def send(array, dims, step):
    return lax.ppermute(array, AXES, shifted(dims, step))


def swap_cores(array):
    return lax.ppermute(array, "k", [(0, 1), (1, 0)])


def gather_step(block, dims):
    return [block, send(block, dims, 1), send(block, dims, -1), send(block, dims, 2)]


ORDERS = ("xyz", "zxy")


def stage_dims(stage):
    return (ORDERS[0][stage], ORDERS[1][stage])


def after(array, *others):
    return lax.optimization_barrier((array,) + others)[0]


def after_all(arrays, *others):
    return tuple(after(array, *others) for array in arrays)


def gather_near(block):
    for stage in range(2):
        block = jnp.concatenate(gather_step(block, stage_dims(stage)), 0)
    return block


def gather_sides(block):
    dims = stage_dims(2)
    return send(block, dims, 1), send(block, dims, -1)


def gather_far(left, right):
    dims = stage_dims(2)
    half = left.shape[0] // 2
    return send(left[:half], dims, 1), send(right[half:], dims, -1)


def add(*terms):
    total = terms[0].astype(jnp.float32)
    for term in terms[1:]:
        total = total + term.astype(jnp.float32)
    return total


def scatter_near(total):
    for stage in (1, 0):
        dims = stage_dims(stage)
        parts = total.astype(jnp.bfloat16).reshape(4, -1, total.shape[1])
        total = add(
            parts[0], send(parts[1], dims, -1), send(parts[2], dims, 1), send(parts[3], dims, -2)
        )
    return total


def placement(meta, experts, me):
    rows = meta.shape[0]
    slots = rows // ROWS * CAP
    turned = meta.astype(jnp.float32).T
    ids = turned[0:TOPK]
    gates = turned[TOPK : 2 * TOPK] + turned[2 * TOPK : 3 * TOPK] + turned[3 * TOPK : 4 * TOPK]
    token = lax.broadcasted_iota(jnp.int32, (rows, rows), 0)
    later = lax.broadcasted_iota(jnp.int32, (rows, rows), 1)
    earlier = ((token // ROWS == later // ROWS) & (token < later)).astype(jnp.float32)
    block = (lax.broadcasted_iota(jnp.int32, (1, rows), 1) // ROWS).astype(jnp.float32)
    slot_at = lax.broadcasted_iota(jnp.int32, (slots, rows), 0).astype(jnp.float32)
    places, weights = [], []
    for side in range(2):
        for local in range(experts):
            expert = ((me ^ side) * experts + local).astype(jnp.float32)
            named = ids == expert
            hit = jnp.max(named.astype(jnp.float32), axis=0, keepdims=True)
            gate = jnp.sum(jnp.where(named, gates, 0.0), axis=0, keepdims=True)
            rank = jnp.dot(
                jnp.broadcast_to(hit, (8, rows)), earlier, preferred_element_type=jnp.float32
            )[0:1]
            slot = jnp.where(hit > 0.0, block * CAP + rank, -1.0)
            place = (slot_at == slot).astype(jnp.float32)
            places.append(place)
            weights.append(jnp.sum(place * gate, axis=1, keepdims=True))
    return jnp.concatenate(places, 0), jnp.concatenate(weights, 0)


def cost(flops, *arrays):
    moved = sum(array.size * array.dtype.itemsize for array in arrays)
    return pl.CostEstimate(flops=int(flops), bytes_accessed=int(moved), transcendentals=0)


def call(kernel, grid, ins, in_specs, outs, out_specs, flops, scratch=(), limit=24, told=False):
    return pl.pallas_call(
        kernel,
        grid=grid,
        in_specs=in_specs,
        out_specs=out_specs,
        out_shape=outs,
        scratch_shapes=list(scratch),
        compiler_params=pltpu.CompilerParams(vmem_limit_bytes=limit * 1024 * 1024),
        cost_estimate=cost(flops, *ins, *outs) if told else None,
    )(*ins)


def shape(dims, dtype=jnp.bfloat16):
    return jax.ShapeDtypeStruct(dims, dtype)


def joined(refs):
    return refs[0][...] if len(refs) == 1 else jnp.concatenate([ref[...] for ref in refs], 0)


def store_slots(found, tile, own_ref, other_ref):
    slots = found.shape[0] // 4
    span = pl.ds(tile * slots, slots)
    own_ref[0, span, :] = found[0:slots]
    own_ref[1, span, :] = found[slots : 2 * slots]
    other_ref[0, span, :] = found[2 * slots : 3 * slots]
    other_ref[1, span, :] = found[3 * slots :]


def pack_rows(me, groups, width, chunk):
    parts = [part for group in groups for part in group]
    tile_rows = sum(part.shape[0] for part in groups[0])
    slots = tile_rows // ROWS * CAP
    count, total = len(groups), len(parts)
    meta_at = width // META

    def kernel(me_ref, *refs):
        metas, rows = refs[:total], refs[total : 2 * total]
        own_ref, other_ref, place_ref, weight_ref = refs[2 * total :]

        @pl.when(pl.program_id(0) == 0)
        def _():
            at = 0
            for tile, group in enumerate(groups):
                meta = joined(metas[at : at + len(group)])
                at += len(group)
                place, weight = placement(meta, 2, me_ref[0])
                place_ref[tile] = place.astype(jnp.bfloat16)
                weight_ref[tile] = jnp.broadcast_to(weight, weight_ref.shape[1:])

        at = 0
        for tile, group in enumerate(groups):
            block = joined(rows[at : at + len(group)])
            at += len(group)
            found = jnp.dot(place_ref[tile], block, preferred_element_type=jnp.float32)
            store_slots(found.astype(jnp.bfloat16), tile, own_ref, other_ref)

    out_block = pl.BlockSpec((2, count * slots, chunk), lambda j: (0, 0, j))
    return call(
        kernel,
        (width // chunk,),
        (me, *parts, *parts),
        [pl.BlockSpec(memory_space=pltpu.SMEM)]
        + [pl.BlockSpec((part.shape[0], META), lambda j: (0, meta_at)) for part in parts]
        + [pl.BlockSpec((part.shape[0], chunk), lambda j: (0, j)) for part in parts],
        [shape((2, count * slots, width))] * 2
        + [
            shape((count, 4 * slots, tile_rows)),
            shape((count, 4 * slots, META), jnp.float32),
        ],
        [out_block, out_block]
        + [
            pl.BlockSpec((count, 4 * slots, tile_rows), lambda j: (0, 0, 0)),
            pl.BlockSpec((count, 4 * slots, META), lambda j: (0, 0, 0)),
        ],
        2 * count * 4 * slots * tile_rows * width,
    )


def pack_grads(places, weights, tiles, chunk):
    parts = [part for group in tiles for part in group]
    width = parts[0].shape[1]
    tile_rows = places[0].shape[2]
    slots = places[0].shape[1] // 4
    count = len(places)

    def kernel(*refs):
        place_refs, weight_refs = refs[:count], refs[count : 2 * count]
        rows, (own_ref, other_ref) = refs[2 * count : -2], refs[-2:]
        placed = [ref[t] for ref in place_refs for t in range(ref.shape[0])]
        scales = [ref[t] for ref in weight_refs for t in range(ref.shape[0])]
        at = 0
        for tile, group in enumerate(tiles):
            block = joined(rows[at : at + len(group)])
            at += len(group)
            found = jnp.dot(placed[tile], block, preferred_element_type=jnp.float32)
            found = (found * scales[tile][:, 0:1]).astype(jnp.bfloat16)
            store_slots(found, tile, own_ref, other_ref)

    out_block = pl.BlockSpec((2, len(tiles) * slots, chunk), lambda j: (0, 0, j))
    return call(
        kernel,
        (width // chunk,),
        (*places, *weights, *parts),
        [pl.BlockSpec(a.shape, lambda j: (0, 0, 0)) for a in (*places, *weights)]
        + [pl.BlockSpec((part.shape[0], chunk), lambda j: (0, j)) for part in parts],
        [shape((2, len(tiles) * slots, width))] * 2,
        [out_block, out_block],
        2 * len(tiles) * 4 * slots * tile_rows * width,
        told=True,
    )


def merge(place, weight, own, other, pieces, chunk, into=()):
    width = own.shape[2]
    rows = place.shape[2]
    slots = place.shape[1] // 4
    count = own.shape[1] // slots

    def kernel(place_ref, weight_ref, own_ref, other_ref, *refs):
        outs = refs[len(into) :]
        totals = []
        for tile in range(count):
            span = pl.ds(tile * slots, slots)
            block = jnp.concatenate(
                [ref[e, span, :] for ref in (own_ref, other_ref) for e in range(2)], 0
            )
            scale = weight_ref[tile][:, 0:1]
            scaled = (block.astype(jnp.float32) * scale).astype(jnp.bfloat16)
            totals.append(t_dot(place_ref[tile], scaled).astype(jnp.bfloat16))
        at = 0
        for out, (size, _, _) in zip(outs, pieces):
            out[...] = totals[at // rows][at % rows : at % rows + size]
            at += size

    slot_block = pl.BlockSpec((2, own.shape[1], chunk), lambda j: (0, 0, j))
    return pl.pallas_call(
        kernel,
        grid=(width // chunk,),
        in_specs=[
            pl.BlockSpec(place.shape, lambda j: (0, 0, 0)),
            pl.BlockSpec(weight.shape, lambda j: (0, 0, 0)),
            slot_block,
            slot_block,
        ]
        + [pl.BlockSpec(memory_space=pl.ANY)] * len(into),
        out_specs=[
            pl.BlockSpec((size, chunk), lambda j, at=at: (at, j)) for size, _, at in pieces
        ],
        out_shape=[shape((total, width)) for _, total, _ in pieces],
        input_output_aliases={4 + i: i for i in range(len(into))},
        compiler_params=pltpu.CompilerParams(vmem_limit_bytes=24 * 1024 * 1024),
    )(place, weight, own, other, *into)


def dot_t(a, b):
    return lax.dot_general(a, b, (((1,), (1,)), ((), ())), preferred_element_type=jnp.float32)


def t_dot(a, b):
    return lax.dot_general(a, b, (((0,), (0,)), ((), ())), preferred_element_type=jnp.float32)


def forward(own, other, w_gate, w_up, w_down, chunk):
    experts, rows, width = own.shape
    hidden = w_gate.shape[1]
    steps = width // chunk

    def kernel(own_ref, other_ref, wg_ref, wu_ref, wd_ref, *rest):
        own_out, other_out, hidden_ref, gate_sum, up_sum, active_ref = rest
        step = pl.program_id(1)

        @pl.when(step < steps)
        def _():
            block = jnp.concatenate([own_ref[0], other_ref[0]], 0)
            gate = dot_t(block, wg_ref[0])
            up = dot_t(block, wu_ref[0])

            @pl.when(step == 0)
            def _():
                gate_sum[...] = gate
                up_sum[...] = up

            @pl.when(step > 0)
            def _():
                gate_sum[...] += gate
                up_sum[...] += up

        @pl.when(step == steps)
        def _():
            gate, up = gate_sum[...], up_sum[...]
            hidden_ref[0, 0] = gate
            hidden_ref[0, 1] = up
            active_ref[...] = (gate * jax.nn.sigmoid(gate) * up).astype(jnp.bfloat16)

        @pl.when(step >= steps)
        def _():
            out = jnp.dot(active_ref[...], wd_ref[0], preferred_element_type=jnp.float32)
            out = out.astype(jnp.bfloat16)
            own_out[0] = out[:rows]
            other_out[0] = out[rows:]

    def early(e, s):
        return (e, 0, jnp.minimum(s, steps - 1))

    def late(e, s):
        return (e, 0, jnp.maximum(s - steps, 0))

    row_block = pl.BlockSpec((1, rows, chunk), early)
    weight_block = pl.BlockSpec((1, hidden, chunk), early)
    return call(
        kernel,
        (experts, 2 * steps),
        (own, other, w_gate, w_up, w_down),
        [row_block, row_block, weight_block, weight_block, pl.BlockSpec((1, hidden, chunk), late)],
        [shape(own.shape), shape(own.shape), shape((experts, 2, 2 * rows, hidden), jnp.float32)],
        [
            pl.BlockSpec((1, rows, chunk), late),
            pl.BlockSpec((1, rows, chunk), late),
            pl.BlockSpec((1, 2, 2 * rows, hidden), lambda e, s: (e, 0, 0, 0)),
        ],
        12 * experts * rows * hidden * width,
        [
            pltpu.VMEM((2 * rows, hidden), jnp.float32),
            pltpu.VMEM((2 * rows, hidden), jnp.float32),
            pltpu.VMEM((2 * rows, hidden), jnp.bfloat16),
        ],
    )


def back_act(grads, w_down, chunk):
    experts, rows, width = grads[0].shape
    hidden = w_down.shape[1]

    def kernel(own_ref, other_ref, wd_ref, out_ref):
        block = jnp.concatenate([own_ref[0], other_ref[0]], 0)
        found = dot_t(block, wd_ref[0])

        @pl.when(pl.program_id(1) == 0)
        def _():
            out_ref[0] = found

        @pl.when(pl.program_id(1) > 0)
        def _():
            out_ref[0] += found

    row_block = pl.BlockSpec((1, rows, chunk), lambda e, s: (e, 0, s))
    return call(
        kernel,
        (experts, width // chunk),
        (*grads, w_down),
        [row_block, row_block, pl.BlockSpec((1, hidden, chunk), lambda e, s: (e, 0, s))],
        [shape((experts, 2 * rows, hidden), jnp.float32)],
        [pl.BlockSpec((1, 2 * rows, hidden), lambda e, s: (e, 0, 0))],
        4 * experts * rows * hidden * width,
        told=True,
    )[0]


def hidden_of(refs, which):
    halves = [[], []]
    for ref in refs:
        rows = ref.shape[2] // 2
        for side in range(2):
            halves[side].append(ref[0, which, side * rows : (side + 1) * rows, :])
    return jnp.concatenate(halves[0] + halves[1], 0)


def down_grad(grads, hiddens, chunk):
    experts, rows, width = grads[0].shape
    units = hiddens[0].shape[3]

    def kernel(own_ref, other_ref, *refs):
        hidden_refs, out_ref, active_ref = refs[:-2], refs[-2], refs[-1]

        @pl.when(pl.program_id(1) == 0)
        def _():
            gate, up = hidden_of(hidden_refs, 0), hidden_of(hidden_refs, 1)
            active_ref[...] = (gate * jax.nn.sigmoid(gate) * up).astype(jnp.bfloat16)

        block = jnp.concatenate([own_ref[0], other_ref[0]], 0)
        out_ref[0] = t_dot(active_ref[...], block).astype(jnp.bfloat16)

    row_block = pl.BlockSpec((1, rows, chunk), lambda e, s: (e, 0, s))
    return call(
        kernel,
        (experts, width // chunk),
        (*grads, *hiddens),
        [row_block, row_block]
        + [pl.BlockSpec((1,) + h.shape[1:], lambda e, s: (e, 0, 0, 0)) for h in hiddens],
        [shape((experts, units, width))],
        [pl.BlockSpec((1, units, chunk), lambda e, s: (e, 0, s))],
        4 * experts * rows * units * width,
        [pltpu.VMEM((2 * rows, units), jnp.bfloat16)],
        told=True,
    )[0]


def up_grads(back, groups, hiddens, chunk):
    experts, rows, units = back.shape
    width = groups[0][0].shape[2]
    count = len(groups)

    def kernel(back_ref, *refs):
        row_refs, hidden_refs = refs[: 2 * count], refs[2 * count : 3 * count]
        dg_ref, du_ref, dgate, dup = refs[3 * count :]

        @pl.when(pl.program_id(1) == 0)
        def _():
            gate, up = hidden_of(hidden_refs, 0), hidden_of(hidden_refs, 1)
            sig = jax.nn.sigmoid(gate)
            d_act = back_ref[0]
            dgate[...] = (d_act * up * sig * (1.0 + gate * (1.0 - sig))).astype(jnp.bfloat16)
            dup[...] = (d_act * (gate * sig)).astype(jnp.bfloat16)

        block = jnp.concatenate([ref[0] for ref in row_refs], 0)
        dg_ref[0] = t_dot(dgate[...], block).astype(jnp.bfloat16)
        du_ref[0] = t_dot(dup[...], block).astype(jnp.bfloat16)

    ordered = [group[side] for side in range(2) for group in groups]
    out_block = pl.BlockSpec((1, units, chunk), lambda e, s: (e, 0, s))
    return call(
        kernel,
        (experts, width // chunk),
        (back, *ordered, *hiddens),
        [pl.BlockSpec((1, rows, units), lambda e, s: (e, 0, 0))]
        + [pl.BlockSpec((1, o.shape[1], chunk), lambda e, s: (e, 0, s)) for o in ordered]
        + [pl.BlockSpec((1,) + h.shape[1:], lambda e, s: (e, 0, 0, 0)) for h in hiddens],
        [shape((experts, units, width))] * 2,
        [out_block] * 2,
        4 * experts * rows * units * width,
        [pltpu.VMEM((rows, units), jnp.bfloat16)] * 2,
        told=True,
    )


def attend(base, queries, pairs, out_proj):
    rows, width = queries.shape[0], out_proj.shape[1]
    tokens = pairs.shape[0]
    steps = queries.shape[1] // (2 * HEAD)

    def kernel(base_ref, query_ref, pairs_ref, proj_ref, out_ref, sum_ref):
        both = query_ref[...]
        query = jnp.concatenate([both[:, :HEAD], both[:, HEAD:]], 0)
        pairs = pairs_ref[...]
        scores = dot_t(query, pairs[:, :HEAD]) * (1.0 / math.sqrt(HEAD))
        query_pos = lax.broadcasted_iota(jnp.int32, (2 * rows, 1), 0) % rows + base_ref[0]
        key_pos = lax.broadcasted_iota(jnp.int32, (1, tokens), 1)
        scores = jnp.where(key_pos <= query_pos, scores, -1e30)
        probs = jnp.exp(scores - jnp.max(scores, axis=1, keepdims=True))
        denom = jnp.sum(probs, axis=1, keepdims=True)
        heads = jnp.dot(
            probs.astype(jnp.bfloat16), pairs[:, HEAD:], preferred_element_type=jnp.float32
        )
        heads = (heads / denom).astype(jnp.bfloat16)
        attn = jnp.concatenate([heads[:rows], heads[rows:]], 1)
        part = jnp.dot(attn, proj_ref[...], preferred_element_type=jnp.float32)
        step = pl.program_id(0)

        @pl.when(step == 0)
        def _():
            sum_ref[...] = part

        @pl.when(step > 0)
        def _():
            sum_ref[...] += part

        @pl.when(step == steps - 1)
        def _():
            out_ref[...] = sum_ref[...].astype(jnp.bfloat16)

    return call(
        kernel,
        (steps,),
        (base, queries, pairs, out_proj),
        [
            pl.BlockSpec(memory_space=pltpu.SMEM),
            pl.BlockSpec((rows, 2 * HEAD), lambda h: (0, h)),
            pl.BlockSpec((tokens, 2 * HEAD), lambda h: (0, 0)),
            pl.BlockSpec((2 * HEAD, width), lambda h: (h, 0)),
        ],
        [shape((rows, width))],
        [pl.BlockSpec((rows, width), lambda h: (0, 0))],
        2 * rows * queries.shape[1] * (2 * tokens + width),
        [pltpu.VMEM((rows, width), jnp.float32)],
        limit=32,
    )[0]


def shards(
    queries,
    keys,
    values,
    resid,
    out_proj,
    norm_gain,
    expert_ids,
    gates,
    w_gate,
    w_up,
    w_down,
    cotangent,
):
    width = resid.shape[1]
    chunk = min(512, width)
    yh, z, k, yl = (lax.axis_index(name) for name in ("yh", "z", "k", "yl"))
    ctx = ((yh * 4 + z) * 2 + k).astype(jnp.int32)

    tok_ctx = queries.shape[0]
    key_mine = lax.dynamic_slice_in_dim(keys, yl * HEAD, HEAD, 1)
    value_mine = lax.dynamic_slice_in_dim(values, yl * HEAD, HEAD, 1)
    pair = jnp.concatenate([key_mine, value_mine], 1)
    pairs = lax.all_to_all(
        jnp.broadcast_to(pair, (16,) + pair.shape), ("yh", "z", "k"), 0, 0, tiled=True
    ).reshape(16 * tok_ctx, 2 * HEAD)

    rest = gates
    pieces = [expert_ids.astype(jnp.bfloat16)]
    for _ in range(3):
        piece = lax.reduce_precision(rest, 8, 7)
        pieces.append(piece.astype(jnp.bfloat16))
        rest = rest - piece
    pieces.append(jnp.zeros((ROWS, META - 4 * TOPK), jnp.bfloat16))
    meta = jnp.concatenate(pieces, 1)
    cot_near = jnp.concatenate(gather_step(cotangent, stage_dims(0)), 0)
    cot_near = jnp.concatenate(gather_step(after(cot_near, pairs), stage_dims(1)), 0)
    cot_sides = gather_sides(cot_near)

    base = (ctx * tok_ctx).reshape(1)
    mixed = attend(base, queries, pairs, out_proj)
    mixed = lax.all_to_all(mixed, ("yl", "x"), 0, 0, tiled=True).reshape(8, ROWS, width)
    stream = resid.astype(jnp.float32) + jnp.sum(mixed.astype(jnp.float32), axis=0)
    normed = (
        stream * lax.rsqrt(jnp.mean(stream * stream, axis=1, keepdims=True) + 1e-06) * norm_gain
    ).astype(jnp.bfloat16)

    me = ctx.reshape(1)
    near = jnp.concatenate(
        gather_step(jnp.concatenate([normed, meta], 1), stage_dims(0)), 0
    )
    near = jnp.concatenate(gather_step(after(near, *cot_sides), stage_dims(1)), 0)
    left, right = gather_sides(near)
    half = near.shape[0] // 2
    narrow, wide = 2 * chunk, 4 * chunk

    def run_forward(rows_own, rows_got):
        return forward(rows_own, rows_got, w_gate, w_up, w_down, wide)

    own0, other0, place0, weight0 = pack_rows(me, [[near]], width, narrow)
    got0 = swap_cores(other0)
    out0, back0, hidden0 = run_forward(own0, got0)
    back0 = swap_cores(back0)
    left, right = after(left, out0), after(right, out0)

    far_a, far_b = gather_far(left, right)
    own1, other1, place1, weight1 = pack_rows(me, [[left], [right]], width, narrow)
    got1 = swap_cores(other1)
    (sum0,) = merge(place0, weight0, after(out0, other1), back0, [(2 * half, 2 * half, 0)], narrow)
    out1, back1, hidden1 = run_forward(after(own1, sum0), got1)
    back1 = swap_cores(back1)

    far_got = far_a
    far_a, far_b = after(far_a, out1), after(far_b, out1)
    own2, other2, place2, weight2 = pack_rows(me, [[far_a, far_b]], width, narrow)
    got2 = swap_cores(other2)
    out2, back2, hidden2 = run_forward(own2, got2)
    back2 = swap_cores(back2)

    dims = stage_dims(2)
    left_a, minus, plus, right_b = merge(
        place1,
        weight1,
        after(out1, out2),
        back1,
        [(half, half, 0), (half, 2 * half, 1), (half, 2 * half, 0), (half, half, 0)],
        narrow,
    )
    minus, plus = merge(
        place2,
        weight2,
        after(out2, left_a),
        back2,
        [(half, 2 * half, 0), (half, 2 * half, 1)],
        narrow,
        (minus, plus),
    )
    got_minus, got_plus = send(minus, dims, -1), send(plus, dims, 1)

    cot_left, cot_right = (after(side, far_got) for side in cot_sides)
    cot_far = gather_far(cot_left, cot_right)
    cot_tiles = [[after(cot_near, minus)], [cot_left], [cot_right], list(cot_far)]
    places, weights = (place0, place1, place2), (weight0, weight1, weight2)
    grads_own, grads_other = pack_grads(places, weights, cot_tiles, chunk)
    grads = (grads_own, swap_cores(grads_other))
    hiddens = [hidden0, hidden1, hidden2]

    left_a = add(after(left_a, grads_other), got_minus[:half]).astype(jnp.bfloat16)
    right_b = add(after(right_b, grads_other), got_plus[half:]).astype(jnp.bfloat16)
    got_left_a, got_right_b = send(left_a, dims, -1), send(right_b, dims, 1)
    back = back_act(grads, w_down, wide)
    sum0 = after(sum0, back)
    total = jnp.concatenate(
        [
            add(sum0[:half], got_left_a, got_plus[:half]),
            add(sum0[half:], got_minus[half:], got_right_b),
        ],
        0,
    )
    groups = [(own0, got0), (own1, got1), (own2, got2)]
    grad_down = down_grad(after_all(grads, back), hiddens, narrow)
    grad_gate, grad_up = up_grads(back, groups, hiddens, narrow)
    combined = scatter_near(total)
    layer_out = (stream + combined).astype(jnp.bfloat16)
    return layer_out, grad_gate, grad_up, grad_down


def solution(mesh):
    split = Mesh(mesh.devices.reshape(SIZES), AXES)
    ctx, tp = ("yh", "z", "k"), ("yl", "x")
    rows, weights = P(ctx + tp, None), P(ctx, tp, None)
    in_specs = (
        P(ctx, tp),
        P(ctx, None),
        P(ctx, None),
        rows,
        P(tp, None),
        P(),
        rows,
        rows,
        weights,
        weights,
        weights,
        rows,
    )
    return jax.shard_map(
        shards,
        mesh=split,
        in_specs=in_specs,
        out_specs=(rows, weights, weights, weights),
        check_vma=False,
    )
```

time: 305 us -> 264 us (0.87)
  waiting for transfers between devices: 134 us -> 121 us
  matrix products: 10.4 us -> 0 us
  local copies, waits for them, and re-layouts: 22.3 us -> 14.6 us
  starting transfers between devices: 60.1 us -> 54.4 us
    ppermute x33 -> x30, starting transfers between devices: 51.6 us -> 38.8 us  [send(): return lax.ppermute(array, AXES, shifted(dims, step))]
    all_to_all x0 -> x1, starting transfers between devices: none -> 8.26 us  [shards(): lax.all_to_all(jnp.broadcast_to(pair, (16,) + pair.shape), ('yh', 'z', 'k...]
    ppermute x4 -> x7, waiting for transfers between devices: 19.1 us -> 10.9 us  [swap_cores(): return lax.ppermute(array, 'k', [(0, 1), (1, 0)])]
    all_to_all x0 -> x1, waiting for transfers between devices: none -> 7.91 us  [shards(): lax.all_to_all(jnp.broadcast_to(pair, (16,) + pair.shape), ('yh', 'z', 'k...]
    dot_general x2 -> x0, matrix products: 6.08 us -> none  [the longest x1 3.91 us: shards(): jnp.dot(attn, out_proj, preferred_element_type=jnp.float32)]
    ppermute x33 -> x30, waiting for transfers between devices: 98.9 us -> 93.4 us  [send(): return lax.ppermute(array, AXES, shifted(dims, step))]
    all_to_all x1, waiting for transfers between devices: 13.9 us -> 8.88 us  [shards(): lax.all_to_all(mixed, ('yl', 'x'), 0, 0, tiled=True).reshape(8, ROWS, width)]
    unnamed x61 -> x63, local copies, waits for them, and re-layouts: 13.4 us -> 8.38 us
  transfers between devices with their start and end apart: 39 -> 39, of which waited for: 18 -> 22; matrix products, arithmetic and copies ran while one was open for 9% -> 4% of each run, Pallas kernels for 11% -> 22%
where the time goes in v2:
time: 264 us; the launch traced here: 263 us
  waiting for transfers between devices  121 us (46%)
  Pallas kernels  67.6 us (26%)
  starting transfers between devices  54.4 us (21%)
  local copies, waits for them, and re-layouts  14.6 us (6%)
  other arithmetic  3.88 us (1%)
    ppermute x30, waiting for transfers between devices, send(): return lax.ppermute(array, AXES, shifted(dims, step))  93.4 us
    pallas_call x11, Pallas kernels, call(): pl.pallas_call(kernel, grid=grid, in_specs=in_specs, out_specs=out_specs,...  58.7 us
    ppermute x30, starting transfers between devices, send(): return lax.ppermute(array, AXES, shifted(dims, step))  38.8 us
    ppermute x7, waiting for transfers between devices, swap_cores(): return lax.ppermute(array, 'k', [(0, 1), (1, 0)])  10.9 us
    all_to_all x1, waiting for transfers between devices, shards(): lax.all_to_all(mixed, ('yl', 'x'), 0, 0, tiled=True).reshape(8, ROWS, width)  8.88 us
    pallas_call x3, Pallas kernels, merge(): pl.pallas_call(kernel, grid=(width // chunk,), in_specs=[pl.BlockSpec(pla...  8.84 us
    unnamed x63, local copies, waits for them, and re-layouts  8.38 us
    all_to_all x1, starting transfers between devices, shards(): lax.all_to_all(jnp.broadcast_to(pair, (16,) + pair.shape), ('yh', 'z', 'k...  8.26 us
  transfers between devices with their start and end apart: 39, of which 22 were waited for; matrix products, arithmetic and copies ran while one was open for 4% of the time, Pallas kernels for 22%

profile of v2, /device:TPU:0, one launch (start us, length us, event | category | flops | bytes accessed | tf_op | source)
XLA Modules:
  0.0 262.8 jit_solution(6578644749718969039)
XLA Ops:
  2.6 8.3 %all-to-all-start = ((bf16[16,128,256]{2,1,0:T(8,128)(2,1)}), bf16[16,128,256]{2,1,0:T(8,128)(2,1)S(1)}, u32[]{:S(2)}, u32[]{:S(2)}) async-start(bf16[16,128,256]{2,1,0:T(8,128)(2,1)} %broadcast_in_dim.8), calls=%async_computation | async-start | bytes 2097152 | tf_op jit(solution)/shard_map/all_to_all | solution.py:551
  10.9 2.8 %collective-permute-start.4 = (bf16[16,4096]{1,0:T(8,128)(2,1)S(1)}, bf16[16,4096]{1,0:T(8,128)(2,1)S(1)}, u32[]{:S(2)}, u32[]{:S(2)}) collective-permute-start(bf16[16,4096]{1,0:T(8,128)(2,1)S(1)} %copy-done.25), channel_id=1, source_target_pairs={{0,3},{8,56},{16,19},{24,8},{32,35},{40,24},{48,51},{56,40},{4,7},... | collective-permute-start | bytes 393224 | tf_op jit(solution)/shard_map/ppermute | solution.py:45
  16.2 5.1 %collective-permute-done.3 = bf16[16,4096]{1,0:T(8,128)(2,1)S(1)} collective-permute-done((bf16[16,4096]{1,0:T(8,128)(2,1)S(1)}, bf16[16,4096]{1,0:T(8,128)(2,1)S(1)}, u32[]{:S(2)}, u32[]{:S(2)}) %collective-permute-start.3) | collective-permute-done | bytes 131104 | tf_op jit(solution)/shard_map/ppermute | solution.py:45
  21.3 7.9 %all-to-all-done = bf16[16,128,256]{2,1,0:T(8,128)(2,1)S(1)} async-done(((bf16[16,128,256]{2,1,0:T(8,128)(2,1)}), bf16[16,128,256]{2,1,0:T(8,128)(2,1)S(1)}, u32[]{:S(2)}, u32[]{:S(2)}) %all-to-all-start) | async-done | bytes 1048608 | tf_op jit(solution)/shard_map/all_to_all | solution.py:551
  35.8 4.7 %shard_map.147 = bf16[128,4096]{1,0:T(8,128)(2,1)} custom-call(s32[1]{0:T(128)} %bitcast.base_ref, bf16[128,512]{1,0:T(8,128)(2,1)S(1)} %copy-done.23, bf16[2048,256]{1,0:T(8,128)(2,1)S(1)} %bitcast.4, bf16[512,4096]{1,0:T(8,128)(2,1)S(1)} %copy-done.3), custom_call_target="tpu_custom_call" | custom-call | tf_op jit(solution)/shard_map/pallas_call | solution.py:139
  40.5 4.4 %all-to-all-start.1 = ((bf16[8,16,4096]{2,1,0:T(8,128)(2,1)}), bf16[8,16,4096]{2,1,0:T(8,128)(2,1)S(1)}, u32[]{:S(2)}, u32[]{:S(2)}) async-start(bf16[8,16,4096]{2,1,0:T(8,128)(2,1)} %bitcast.2), calls=%async_computation.1 | async-start | bytes 2097152 | tf_op jit(solution)/shard_map/all_to_all | solution.py:569
  53.0 8.9 %all-to-all-done.1 = bf16[8,16,4096]{2,1,0:T(8,128)(2,1)S(1)} async-done(((bf16[8,16,4096]{2,1,0:T(8,128)(2,1)}), bf16[8,16,4096]{2,1,0:T(8,128)(2,1)S(1)}, u32[]{:S(2)}, u32[]{:S(2)}) %all-to-all-start.1) | async-done | bytes 1048608 | tf_op jit(solution)/shard_map/all_to_all | solution.py:569
  63.9 2.7 %collective-permute-start.1 = (bf16[16,4224]{1,0:T(8,128)(2,1)S(1)}, bf16[16,4224]{1,0:T(8,128)(2,1)S(1)}, u32[]{:S(2)}, u32[]{:S(2)}) collective-permute-start(bf16[16,4224]{1,0:T(8,128)(2,1)S(1)} %concatenate.21), channel_id=1, source_target_pairs={{0,3},{8,56},{16,19},{24,8},{32,35},{40,24},{48,51},{56,40},{4,7},... | collective-permute-start | bytes 405512 | tf_op jit(solution)/shard_map/ppermute | solution.py:45
  66.6 3.0 %collective-permute-done.2 = bf16[16,4224]{1,0:T(8,128)(2,1)S(1)} collective-permute-done((bf16[16,4224]{1,0:T(8,128)(2,1)S(1)}, bf16[16,4224]{1,0:T(8,128)(2,1)S(1)}, u32[]{:S(2)}, u32[]{:S(2)}) %collective-permute-start.2) | collective-permute-done | bytes 135200 | tf_op jit(solution)/shard_map/ppermute | solution.py:45
  69.7 3.2 %collective-permute-done = bf16[16,4224]{1,0:T(8,128)(2,1)S(1)} collective-permute-done((bf16[16,4224]{1,0:T(8,128)(2,1)S(1)}, bf16[16,4224]{1,0:T(8,128)(2,1)S(1)}, u32[]{:S(2)}, u32[]{:S(2)}) %collective-permute-start) | collective-permute-done | bytes 135200 | tf_op jit(solution)/shard_map/ppermute | solution.py:45
  72.9 7.2 %collective-permute-done.10.refs_8_ = bf16[256,4096]{1,0:T(8,128)(2,1)S(1)} collective-permute-done((bf16[256,4096]{1,0:T(8,128)(2,1)}, bf16[256,4096]{1,0:T(8,128)(2,1)S(1)}, u32[]{:S(2)}, u32[]{:S(2)}) %collective-permute-start.10) | collective-permute-done | bytes 2097184 | tf_op jit(solution)/shard_map/ppermute | solution.py:45
  80.1 3.0 %collective-permute-done.9.refs_7_ = bf16[256,4096]{1,0:T(8,128)(2,1)} collective-permute-done((bf16[256,4096]{1,0:T(8,128)(2,1)}, bf16[256,4096]{1,0:T(8,128)(2,1)}, u32[]{:S(2)}, u32[]{:S(2)}) %collective-permute-start.9) | collective-permute-done | bytes 2097184 | tf_op jit(solution)/shard_map/ppermute | solution.py:45
  87.4 12.3 %collective-permute-done.11 = bf16[64,4224]{1,0:T(8,128)(2,1)S(1)} collective-permute-done((bf16[64,4224]{1,0:T(8,128)(2,1)S(1)}, bf16[64,4224]{1,0:T(8,128)(2,1)S(1)}, u32[]{:S(2)}, u32[]{:S(2)}) %collective-permute-start.11) | collective-permute-done | bytes 540704 | tf_op jit(solution)/shard_map/ppermute | solution.py:45
  104.7 3.0 %collective-permute-done.14.other_ref.refs_3_ = bf16[2,80,4096]{2,1,0:T(8,128)(2,1)S(1)} collective-permute-done((bf16[2,80,4096]{2,1,0:T(8,128)(2,1)S(1)}, bf16[2,80,4096]{2,1,0:T(8,128)(2,1)S(1)}, u32[]{:S(2)}, u32[]{:S(2)}) %collective-permute-start.14) | collective-permute-done | bytes 1310752 | tf_op jit(solution)/shard_map/ppermute | solution.py:49
  107.7 5.5 %shard_map.149 = (bf16[2,80,4096]{2,1,0:T(8,128)(2,1)S(1)}, bf16[2,80,4096]{2,1,0:T(8,128)(2,1)S(1)}, f32[2,2,160,192]{3,2,1,0:T(8,128)S(1)}) custom-call(bf16[2,80,4096]{2,1,0:T(8,128)(2,1)S(1)} %get-tuple-element.57.own_ref.refs_0_, bf16[2,80,4096]{2,1,0:T(8,128)(2,1)S(1)} %collective-permute-done.14.other_ref.refs_3_, ...), custom_call_target="tpu_custom_call" | custom-call | tf_op jit(solution)/shard_map/pallas_call | solution.py:139
  113.3 13.6 %collective-permute-done.16.refs_1_.refs_3_ = bf16[256,4224]{1,0:T(8,128)(2,1)S(1)} collective-permute-done((bf16[256,4224]{1,0:T(8,128)(2,1)S(1)}, bf16[256,4224]{1,0:T(8,128)(2,1)S(1)}, u32[]{:S(2)}, u32[]{:S(2)}) %collective-permute-start.16) | collective-permute-done | bytes 2162720 | tf_op jit(solution)/shard_map/ppermute | solution.py:45
  128.2 3.5 %shard_map.150 = (bf16[2,160,4096]{2,1,0:T(8,128)(2,1)S(1)}, bf16[2,160,4096]{2,1,0:T(8,128)(2,1)S(1)}, bf16[2,320,256]{2,1,0:T(8,128)(2,1)S(1)}, f32[2,320,128]{2,1,0:T(8,128)S(1)}) custom-call(s32[1]{0:T(128)} %bitcast.3.me_ref, bf16[256,4224]{1,0:T(8,128)(2,1)S(1)} %collective-permute-done.15.refs_0_.refs_2_, ...), custom_call_target="tpu_custom_call" | custom-call | tf_op jit(solution)/shard_map/pallas_call | solution.py:139
  134.6 4.0 %collective-permute-done.17.other_ref = bf16[2,80,4096]{2,1,0:T(8,128)(2,1)S(1)} collective-permute-done((bf16[2,80,4096]{2,1,0:T(8,128)(2,1)S(1)}, bf16[2,80,4096]{2,1,0:T(8,128)(2,1)S(1)}, u32[]{:S(2)}, u32[]{:S(2)}) %collective-permute-start.17) | collective-permute-done | bytes 1310752 | tf_op jit(solution)/shard_map/ppermute | solution.py:49
  141.0 7.6 %shard_map.152 = (bf16[2,160,4096]{2,1,0:T(8,128)(2,1)S(1)}, bf16[2,160,4096]{2,1,0:T(8,128)(2,1)S(1)}, f32[2,2,320,192]{3,2,1,0:T(8,128)S(1)}) custom-call(bf16[2,160,4096]{2,1,0:T(8,128)(2,1)S(1)} %get-tuple-element.67.own_ref.refs_1_, bf16[2,160,4096]{2,1,0:T(8,128)(2,1)S(1)} %collective-permute-done.19.other_ref.refs_4_, ...), custom_call_target="tpu_custom_call" | custom-call | tf_op jit(solution)/shard_map/pallas_call | solution.py:139
  152.7 3.9 %collective-permute-done.21.other_ref.refs_5_ = bf16[2,80,4096]{2,1,0:T(8,128)(2,1)S(1)} collective-permute-done((bf16[2,80,4096]{2,1,0:T(8,128)(2,1)S(1)}, bf16[2,80,4096]{2,1,0:T(8,128)(2,1)S(1)}, u32[]{:S(2)}, u32[]{:S(2)}) %collective-permute-start.21) | collective-permute-done | bytes 1310752 | tf_op jit(solution)/shard_map/ppermute | solution.py:49
  156.6 5.5 %shard_map.154 = (bf16[2,80,4096]{2,1,0:T(8,128)(2,1)S(1)}, bf16[2,80,4096]{2,1,0:T(8,128)(2,1)S(1)}, f32[2,2,160,192]{3,2,1,0:T(8,128)S(1)}) custom-call(bf16[2,80,4096]{2,1,0:T(8,128)(2,1)S(1)} %get-tuple-element.74.own_ref.refs_2_, bf16[2,80,4096]{2,1,0:T(8,128)(2,1)S(1)} %collective-permute-done.21.other_ref.refs_5_, ...), custom_call_target="tpu_custom_call" | custom-call | tf_op jit(solution)/shard_map/pallas_call | solution.py:139
  166.6 4.0 %shard_map.155 = (bf16[128,4096]{1,0:T(8,128)(2,1)S(1)}, bf16[256,4096]{1,0:T(8,128)(2,1)S(1)}, bf16[256,4096]{1,0:T(8,128)(2,1)S(1)}, bf16[128,4096]{1,0:T(8,128)(2,1)S(1)}) custom-call(bf16[2,320,256]{2,1,0:T(8,128)(2,1)S(1)} %get-tuple-element.65.place_ref.refs_1_, f32[2,320,128]{2,1,0:T(8,128)S(1)} %get-tuple-element.72.weight_ref.refs_4_, ...), custom_call_target="tpu_custom_call" | custom-call | tf_op jit(solution)/shard_map/pallas_call | solution.py:275
  174.4 5.0 %collective-permute-done.25.refs_10_ = bf16[128,4096]{1,0:T(8,128)(2,1)S(1)} collective-permute-done((bf16[128,4096]{1,0:T(8,128)(2,1)S(1)}, bf16[128,4096]{1,0:T(8,128)(2,1)S(1)}, u32[]{:S(2)}, u32[]{:S(2)}) %collective-permute-start.25) | collective-permute-done | bytes 1048608 | tf_op jit(solution)/shard_map/ppermute | solution.py:45
  180.7 7.4 %shard_map.157 = (bf16[2,320,4096]{2,1,0:T(8,128)(2,1)S(1)}, bf16[2,320,4096]{2,1,0:T(8,128)(2,1)S(1)}) custom-call(bf16[1,320,256]{2,1,0:T(8,128)(2,1)S(1)} %get-tuple-element.55.place_ref.refs_0_, bf16[2,320,256]{2,1,0:T(8,128)(2,1)S(1)} %get-tuple-element.65.place_ref.refs_1_, bf16[1,320,256]{2,1,0:T(8,128)(2,1)S(1)} %get-tuple-element.71.place_ref.refs_2_, ...), custom_call_target="tpu_custom_call" | custom-call | flops 2684354560 | bytes 20185088 | tf_op jit(solution)/shard_map/pallas_call | solution.py:139
  191.8 24.0 %collective-permute-done.29 = bf16[256,4096]{1,0:T(8,128)(2,1)S(1)} collective-permute-done((bf16[256,4096]{1,0:T(8,128)(2,1)S(1)}, bf16[256,4096]{1,0:T(8,128)(2,1)S(1)}, u32[]{:S(2)}, u32[]{:S(2)}) %collective-permute-start.29) | collective-permute-done | bytes 2097184 | tf_op jit(solution)/shard_map/ppermute | solution.py:45
  216.4 3.3 %collective-permute-start.28 = (bf16[128,4096]{1,0:T(8,128)(2,1)S(1)}, bf16[128,4096]{1,0:T(8,128)(2,1)S(1)}, u32[]{:S(2)}, u32[]{:S(2)}) collective-permute-start(bf16[128,4096]{1,0:T(8,128)(2,1)S(1)} %add_convert_fusion.3), channel_id=1, source_target_pairs={{0,48},{8,76},{16,0},{24,92},{32,16},{40,108},{48,32},{56,124},{4,... | collective-permute-start | bytes 3145736 | tf_op jit(solution)/shard_map/ppermute | solution.py:45
  219.7 4.7 %shard_map.158.back_ref = f32[2,640,192]{2,1,0:T(8,128)S(1)} custom-call(bf16[2,320,4096]{2,1,0:T(8,128)(2,1)S(1)} %get-tuple-element.100.own_ref, bf16[2,320,4096]{2,1,0:T(8,128)(2,1)S(1)} %collective-permute-done.26.other_ref, bf16[2,192,4096]{2,1,0:T(8,128)(2,1)S(1)} %copy-done), custom_call_target="tpu_custom_call" | custom-call | flops 2013265920 | bytes 14614528 | tf_op jit(solution)/shard_map/pallas_call | solution.py:139
  224.3 7.8 %collective-permute-done.31 = bf16[128,4096]{1,0:T(8,128)(2,1)S(1)} collective-permute-done((bf16[128,4096]{1,0:T(8,128)(2,1)S(1)}, bf16[128,4096]{1,0:T(8,128)(2,1)S(1)}, u32[]{:S(2)}, u32[]{:S(2)}) %collective-permute-start.31) | collective-permute-done | bytes 1048608 | tf_op jit(solution)/shard_map/ppermute | solution.py:45
  236.6 8.9 %shard_map.159 = (bf16[2,192,4096]{2,1,0:T(8,128)(2,1)}, bf16[2,192,4096]{2,1,0:T(8,128)(2,1)}) custom-call(f32[2,640,192]{2,1,0:T(8,128)S(1)} %shard_map.158.back_ref, bf16[2,80,4096]{2,1,0:T(8,128)(2,1)S(1)} %copy-done.7, bf16[2,160,4096]{2,1,0:T(8,128)(2,1)S(1)} %get-tuple-element.67.own_ref.refs_1_, bf16[2,80,4096]{2,1,0:T(8,128)(2,1)S(1)} %copy-done.11, ...), custom_call_target="tpu_custom_call" | custom-call | flops 4026531840 | bytes 19726336 | tf_op jit(solution)/shard_map/pallas_call | solution.py:139
  245.5 5.5 %collective-permute-done.32 = bf16[64,4096]{1,0:T(8,128)(2,1)S(1)} collective-permute-done((bf16[64,4096]{1,0:T(8,128)(2,1)S(1)}, bf16[64,4096]{1,0:T(8,128)(2,1)S(1)}, u32[]{:S(2)}, u32[]{:S(2)}) %collective-permute-start.32) | collective-permute-done | bytes 524320 | tf_op jit(solution)/shard_map/ppermute | solution.py:45
  251.3 2.7 %collective-permute-start.34 = (bf16[16,4096]{1,0:T(8,128)(2,1)S(1)}, bf16[16,4096]{1,0:T(8,128)(2,1)S(1)}, u32[]{:S(2)}, u32[]{:S(2)}) collective-permute-start(bf16[16,4096]{1,0:T(8,128)(2,1)S(1)} %get-tuple-element.106), channel_id=1, source_target_pairs={{0,3},{8,56},{16,19},{24,8},{32,35},{40,24},{48,51},{56,40},{4,7},... | collective-permute-start | bytes 393224 | tf_op jit(solution)/shard_map/ppermute | solution.py:45
  255.8 6.2 %shard_map.160 = bf16[2,192,4096]{2,1,0:T(8,128)(2,1)} custom-call(bf16[2,320,4096]{2,1,0:T(8,128)(2,1)S(1)} %get-tuple-element.100.own_ref, bf16[2,320,4096]{2,1,0:T(8,128)(2,1)S(1)} %collective-permute-done.26.other_ref, f32[2,2,160,192]{3,2,1,0:T(8,128)S(1)} %get-tuple-element.95.refs_6_.refs_0_, f32[2,2,320,192]{3,2,1,0:T(8,128)S(1)} %copy-done.15, ...), custom_call_target="tpu_custom_call" | custom-call | flops 2013265920 | bytes 15597568 | tf_op jit(solution)/shard_map/pallas_call | solution.py:139
  (153 shorter events, 61.8 us)
Async XLA Ops:
  2.6 26.6 %all-to-all-start = ((bf16[16,128,256]{2,1,0:T(8,128)(2,1)}), bf16[16,128,256]{2,1,0:T(8,128)(2,1)S(1)}, u32[]{:S(2)}, u32[]{:S(2)}) async-start(bf16[16,128,256]{2,1,0:T(8,128)(2,1)} %broadcast_in_dim.8), calls=%async_computation | async-start | bytes 2097152 | tf_op jit(solution)/shard_map/all_to_all | solution.py:551
  13.7 7.6 %collective-permute-start.3 = (bf16[16,4096]{1,0:T(8,128)(2,1)S(1)}, bf16[16,4096]{1,0:T(8,128)(2,1)S(1)}, u32[]{:S(2)}, u32[]{:S(2)}) collective-permute-start(bf16[16,4096]{1,0:T(8,128)(2,1)S(1)} %copy-done.25), channel_id=1, source_target_pairs={{0,1},{8,24},{16,17},{24,40},{32,33},{40,56},{48,49},{56,8},{4,5},... | collective-permute-start | bytes 393224 | tf_op jit(solution)/shard_map/ppermute | solution.py:45
  13.7 7.6 %collective-permute-start.5 = (bf16[16,4096]{1,0:T(8,128)(2,1)S(1)}, bf16[16,4096]{1,0:T(8,128)(2,1)S(1)}, u32[]{:S(2)}, u32[]{:S(2)}) collective-permute-start(bf16[16,4096]{1,0:T(8,128)(2,1)S(1)} %copy-done.25), channel_id=1, source_target_pairs={{0,2},{8,40},{16,18},{24,56},{32,34},{40,8},{48,50},{56,24},{4,6},... | collective-permute-start | bytes 393224 | tf_op jit(solution)/shard_map/ppermute | solution.py:45
  29.2 16.1 %collective-permute-start.6 = (bf16[64,4096]{1,0:T(8,128)(2,1)S(1)}, bf16[64,4096]{1,0:T(8,128)(2,1)}, u32[]{:S(2)}, u32[]{:S(2)}) collective-permute-start(bf16[64,4096]{1,0:T(8,128)(2,1)S(1)} %pad_maximum_fusion.1), channel_id=1, source_target_pairs={{0,4},{8,9},{16,20},{24,25},{32,36},{40,41},{48,52},{56,57},{4,64}... | collective-permute-start | bytes 1572872 | tf_op jit(solution)/shard_map/ppermute | solution.py:45
  30.1 19.0 %collective-permute-start.8 = (bf16[64,4096]{1,0:T(8,128)(2,1)S(1)}, bf16[64,4096]{1,0:T(8,128)(2,1)}, u32[]{:S(2)}, u32[]{:S(2)}) collective-permute-start(bf16[64,4096]{1,0:T(8,128)(2,1)S(1)} %pad_maximum_fusion.1), channel_id=1, source_target_pairs={{0,64},{8,10},{16,80},{24,26},{32,96},{40,42},{48,112},{56,58},{4,... | collective-permute-start | bytes 1572872 | tf_op jit(solution)/shard_map/ppermute | solution.py:45
  30.8 16.4 %collective-permute-start.7 = (bf16[64,4096]{1,0:T(8,128)(2,1)S(1)}, bf16[64,4096]{1,0:T(8,128)(2,1)}, u32[]{:S(2)}, u32[]{:S(2)}) collective-permute-start(bf16[64,4096]{1,0:T(8,128)(2,1)S(1)} %pad_maximum_fusion.1), channel_id=1, source_target_pairs={{0,68},{8,11},{16,84},{24,27},{32,100},{40,43},{48,116},{56,59},{4... | collective-permute-start | bytes 1572872 | tf_op jit(solution)/shard_map/ppermute | solution.py:45
  40.5 21.4 %all-to-all-start.1 = ((bf16[8,16,4096]{2,1,0:T(8,128)(2,1)}), bf16[8,16,4096]{2,1,0:T(8,128)(2,1)S(1)}, u32[]{:S(2)}, u32[]{:S(2)}) async-start(bf16[8,16,4096]{2,1,0:T(8,128)(2,1)} %bitcast.2), calls=%async_computation.1 | async-start | bytes 2097152 | tf_op jit(solution)/shard_map/all_to_all | solution.py:569
  51.0 29.1 %collective-permute-start.10 = (bf16[256,4096]{1,0:T(8,128)(2,1)}, bf16[256,4096]{1,0:T(8,128)(2,1)S(1)}, u32[]{:S(2)}, u32[]{:S(2)}) collective-permute-start(bf16[256,4096]{1,0:T(8,128)(2,1)} %constant_dynamic-update-slice_fusion.refs_6_), channel_id=1, source_target_pairs={{0,48},{8,76},{16,0},{24,92},{32,16},{40,108},{48,32},{56,124},{4,... | collective-permute-start | bytes 6291464 | tf_op jit(solution)/shard_map/ppermute | solution.py:45
  52.7 30.5 %collective-permute-start.9 = (bf16[256,4096]{1,0:T(8,128)(2,1)}, bf16[256,4096]{1,0:T(8,128)(2,1)}, u32[]{:S(2)}, u32[]{:S(2)}) collective-permute-start(bf16[256,4096]{1,0:T(8,128)(2,1)} %constant_dynamic-update-slice_fusion.refs_6_), channel_id=1, source_target_pairs={{0,16},{8,12},{16,32},{24,28},{32,48},{40,44},{48,0},{56,60},{4,20... | collective-permute-start | bytes 6291464 | tf_op jit(solution)/shard_map/ppermute | solution.py:45
  83.1 16.8 %collective-permute-start.13 = (bf16[64,4224]{1,0:T(8,128)(2,1)S(1)}, bf16[64,4224]{1,0:T(8,128)(2,1)S(1)}, u32[]{:S(2)}, u32[]{:S(2)}) collective-permute-start(bf16[64,4224]{1,0:T(8,128)(2,1)S(1)} %pad_maximum_fusion), channel_id=1, source_target_pairs={{0,64},{8,10},{16,80},{24,26},{32,96},{40,42},{48,112},{56,58},{4,... | collective-permute-start | bytes 1622024 | tf_op jit(solution)/shard_map/ppermute | solution.py:45
  85.3 14.6 %collective-permute-start.12 = (bf16[64,4224]{1,0:T(8,128)(2,1)S(1)}, bf16[64,4224]{1,0:T(8,128)(2,1)S(1)}, u32[]{:S(2)}, u32[]{:S(2)}) collective-permute-start(bf16[64,4224]{1,0:T(8,128)(2,1)S(1)} %pad_maximum_fusion), channel_id=1, source_target_pairs={{0,68},{8,11},{16,84},{24,27},{32,100},{40,43},{48,116},{56,59},{4... | collective-permute-start | bytes 1622024 | tf_op jit(solution)/shard_map/ppermute | solution.py:45
  87.4 12.4 %collective-permute-start.11 = (bf16[64,4224]{1,0:T(8,128)(2,1)S(1)}, bf16[64,4224]{1,0:T(8,128)(2,1)S(1)}, u32[]{:S(2)}, u32[]{:S(2)}) collective-permute-start(bf16[64,4224]{1,0:T(8,128)(2,1)S(1)} %pad_maximum_fusion), channel_id=1, source_target_pairs={{0,4},{8,9},{16,20},{24,25},{32,36},{40,41},{48,52},{56,57},{4,64}... | collective-permute-start | bytes 1622024 | tf_op jit(solution)/shard_map/ppermute | solution.py:45
  100.1 26.8 %collective-permute-start.16 = (bf16[256,4224]{1,0:T(8,128)(2,1)S(1)}, bf16[256,4224]{1,0:T(8,128)(2,1)S(1)}, u32[]{:S(2)}, u32[]{:S(2)}) collective-permute-start(bf16[256,4224]{1,0:T(8,128)(2,1)S(1)} %constant_dynamic-update-slice_fusion.4.refs_0_.refs_1_), channel_id=1, source_target_pairs={{0,48},{8,76},{16,0},{24,92},{32,16},{40,108},{48,32},{56,124},{4,... | collective-permute-start | bytes 6488072 | tf_op jit(solution)/shard_map/ppermute | solution.py:45
  100.1 28.0 %collective-permute-start.15 = (bf16[256,4224]{1,0:T(8,128)(2,1)S(1)}, bf16[256,4224]{1,0:T(8,128)(2,1)S(1)}, u32[]{:S(2)}, u32[]{:S(2)}) collective-permute-start(bf16[256,4224]{1,0:T(8,128)(2,1)S(1)} %constant_dynamic-update-slice_fusion.4.refs_0_.refs_1_), channel_id=1, source_target_pairs={{0,16},{8,12},{16,32},{24,28},{32,48},{40,44},{48,0},{56,60},{4,20... | collective-permute-start | bytes 6488072 | tf_op jit(solution)/shard_map/ppermute | solution.py:45
  131.7 9.3 %collective-permute-start.19 = (bf16[2,160,4096]{2,1,0:T(8,128)(2,1)S(1)}, bf16[2,160,4096]{2,1,0:T(8,128)(2,1)S(1)}, u32[]{:S(2)}, u32[]{:S(2)}) collective-permute-start(bf16[2,160,4096]{2,1,0:T(8,128)(2,1)S(1)} %get-tuple-element.62), channel_id=1, source_target_pairs={{0,8},{8,0},{1,9},{9,1},{2,10},{10,2},{3,11},{11,3},{4,12},{12,4},... | collective-permute-start | bytes 7864328 | tf_op jit(solution)/shard_map/ppermute | solution.py:49
  132.3 16.3 %collective-permute-start.20 = (bf16[128,4224]{1,0:T(8,128)(2,1)S(1)}, bf16[128,4224]{1,0:T(8,128)(2,1)S(1)}, u32[]{:S(2)}, u32[]{:S(2)}) collective-permute-start(bf16[128,4224]{1,0:T(8,128)(2,1)S(1)} %slice.67), channel_id=1, source_target_pairs={{0,48},{8,76},{16,0},{24,92},{32,16},{40,108},{48,32},{56,124},{4,... | collective-permute-start | bytes 3244040 | tf_op jit(solution)/shard_map/ppermute | solution.py:45
  132.7 16.4 %collective-permute-start.18 = (bf16[128,4224]{1,0:T(8,128)(2,1)S(1)}, bf16[128,4224]{1,0:T(8,128)(2,1)S(1)}, u32[]{:S(2)}, u32[]{:S(2)}) collective-permute-start(bf16[128,4224]{1,0:T(8,128)(2,1)S(1)} %slice.66), channel_id=1, source_target_pairs={{0,16},{8,12},{16,32},{24,28},{32,48},{40,44},{48,0},{56,60},{4,20... | collective-permute-start | bytes 3244040 | tf_op jit(solution)/shard_map/ppermute | solution.py:45
  149.1 17.5 %collective-permute-start.22 = (bf16[2,160,4096]{2,1,0:T(8,128)(2,1)S(1)}, bf16[2,160,4096]{2,1,0:T(8,128)(2,1)S(1)}, u32[]{:S(2)}, u32[]{:S(2)}) collective-permute-start(bf16[2,160,4096]{2,1,0:T(8,128)(2,1)S(1)} %get-tuple-element.78), channel_id=1, source_target_pairs={{0,8},{8,0},{1,9},{9,1},{2,10},{10,2},{3,11},{11,3},{4,12},{12,4},... | collective-permute-start | bytes 7864328 | tf_op jit(solution)/shard_map/ppermute | solution.py:49
  162.2 8.4 %collective-permute-start.23 = (bf16[2,80,4096]{2,1,0:T(8,128)(2,1)S(1)}, bf16[2,80,4096]{2,1,0:T(8,128)(2,1)S(1)}, u32[]{:S(2)}, u32[]{:S(2)}) collective-permute-start(bf16[2,80,4096]{2,1,0:T(8,128)(2,1)S(1)} %get-tuple-element.81), channel_id=1, source_target_pairs={{0,8},{8,0},{1,9},{9,1},{2,10},{10,2},{3,11},{11,3},{4,12},{12,4},... | collective-permute-start | bytes 3932168 | tf_op jit(solution)/shard_map/ppermute | solution.py:49
  164.5 14.9 %collective-permute-start.25 = (bf16[128,4096]{1,0:T(8,128)(2,1)S(1)}, bf16[128,4096]{1,0:T(8,128)(2,1)S(1)}, u32[]{:S(2)}, u32[]{:S(2)}) collective-permute-start(bf16[128,4096]{1,0:T(8,128)(2,1)S(1)} %slice.69), channel_id=1, source_target_pairs={{0,48},{8,76},{16,0},{24,92},{32,16},{40,108},{48,32},{56,124},{4,... | collective-permute-start | bytes 3145736 | tf_op jit(solution)/shard_map/ppermute | solution.py:45
  164.6 16.1 %collective-permute-start.24 = (bf16[128,4096]{1,0:T(8,128)(2,1)S(1)}, bf16[128,4096]{1,0:T(8,128)(2,1)S(1)}, u32[]{:S(2)}, u32[]{:S(2)}) collective-permute-start(bf16[128,4096]{1,0:T(8,128)(2,1)S(1)} %slice.68), channel_id=1, source_target_pairs={{0,16},{8,12},{16,32},{24,28},{32,48},{40,44},{48,0},{56,60},{4,20... | collective-permute-start | bytes 3145736 | tf_op jit(solution)/shard_map/ppermute | solution.py:45
  188.1 31.6 %collective-permute-start.26 = (bf16[2,320,4096]{2,1,0:T(8,128)(2,1)S(1)}, bf16[2,320,4096]{2,1,0:T(8,128)(2,1)S(1)}, u32[]{:S(2)}, u32[]{:S(2)}) collective-permute-start(bf16[2,320,4096]{2,1,0:T(8,128)(2,1)S(1)} %get-tuple-element.89), channel_id=1, source_target_pairs={{0,8},{8,0},{1,9},{9,1},{2,10},{10,2},{3,11},{11,3},{4,12},{12,4},... | collective-permute-start | bytes 15728648 | tf_op jit(solution)/shard_map/ppermute | solution.py:49
  188.5 27.2 %collective-permute-start.29 = (bf16[256,4096]{1,0:T(8,128)(2,1)S(1)}, bf16[256,4096]{1,0:T(8,128)(2,1)S(1)}, u32[]{:S(2)}, u32[]{:S(2)}) collective-permute-start(bf16[256,4096]{1,0:T(8,128)(2,1)S(1)} %copy-done.5), channel_id=1, source_target_pairs={{0,16},{8,12},{16,32},{24,28},{32,48},{40,44},{48,0},{56,60},{4,20... | collective-permute-start | bytes 6291464 | tf_op jit(solution)/shard_map/ppermute | solution.py:45
  189.4 26.7 %collective-permute-start.27 = (bf16[256,4096]{1,0:T(8,128)(2,1)S(1)}, bf16[256,4096]{1,0:T(8,128)(2,1)S(1)}, u32[]{:S(2)}, u32[]{:S(2)}) collective-permute-start(bf16[256,4096]{1,0:T(8,128)(2,1)S(1)} %get-tuple-element.84), channel_id=1, source_target_pairs={{0,48},{8,76},{16,0},{24,92},{32,16},{40,108},{48,32},{56,124},{4,... | collective-permute-start | bytes 6291464 | tf_op jit(solution)/shard_map/ppermute | solution.py:45
  216.0 16.1 %collective-permute-start.31 = (bf16[128,4096]{1,0:T(8,128)(2,1)S(1)}, bf16[128,4096]{1,0:T(8,128)(2,1)S(1)}, u32[]{:S(2)}, u32[]{:S(2)}) collective-permute-start(bf16[128,4096]{1,0:T(8,128)(2,1)S(1)} %add_convert_fusion.1), channel_id=1, source_target_pairs={{0,16},{8,12},{16,32},{24,28},{32,48},{40,44},{48,0},{56,60},{4,20... | collective-permute-start | bytes 3145736 | tf_op jit(solution)/shard_map/ppermute | solution.py:45
  216.4 15.7 %collective-permute-start.28 = (bf16[128,4096]{1,0:T(8,128)(2,1)S(1)}, bf16[128,4096]{1,0:T(8,128)(2,1)S(1)}, u32[]{:S(2)}, u32[]{:S(2)}) collective-permute-start(bf16[128,4096]{1,0:T(8,128)(2,1)S(1)} %add_convert_fusion.3), channel_id=1, source_target_pairs={{0,48},{8,76},{16,0},{24,92},{32,16},{40,108},{48,32},{56,124},{4,... | collective-permute-start | bytes 3145736 | tf_op jit(solution)/shard_map/ppermute | solution.py:45
  233.4 12.0 %collective-permute-start.30 = (bf16[64,4096]{1,0:T(8,128)(2,1)S(1)}, bf16[64,4096]{1,0:T(8,128)(2,1)S(1)}, u32[]{:S(2)}, u32[]{:S(2)}) collective-permute-start(bf16[64,4096]{1,0:T(8,128)(2,1)S(1)} %slice.87), channel_id=1, source_target_pairs={{0,68},{8,11},{16,84},{24,27},{32,100},{40,43},{48,116},{56,59},{4... | collective-permute-start | bytes 1572872 | tf_op jit(solution)/shard_map/ppermute | solution.py:45
  235.0 16.0 %collective-permute-start.32 = (bf16[64,4096]{1,0:T(8,128)(2,1)S(1)}, bf16[64,4096]{1,0:T(8,128)(2,1)S(1)}, u32[]{:S(2)}, u32[]{:S(2)}) collective-permute-start(bf16[64,4096]{1,0:T(8,128)(2,1)S(1)} %get-tuple-element.104), channel_id=1, source_target_pairs={{0,4},{8,9},{16,20},{24,25},{32,36},{40,41},{48,52},{56,57},{4,64}... | collective-permute-start | bytes 1572872 | tf_op jit(solution)/shard_map/ppermute | solution.py:45
  235.5 15.5 %collective-permute-start.33 = (bf16[64,4096]{1,0:T(8,128)(2,1)S(1)}, bf16[64,4096]{1,0:T(8,128)(2,1)S(1)}, u32[]{:S(2)}, u32[]{:S(2)}) collective-permute-start(bf16[64,4096]{1,0:T(8,128)(2,1)S(1)} %get-tuple-element.105), channel_id=1, source_target_pairs={{0,64},{8,10},{16,80},{24,26},{32,96},{40,42},{48,112},{56,58},{4,... | collective-permute-start | bytes 1572872 | tf_op jit(solution)/shard_map/ppermute | solution.py:45
  251.3 10.7 %collective-permute-start.34 = (bf16[16,4096]{1,0:T(8,128)(2,1)S(1)}, bf16[16,4096]{1,0:T(8,128)(2,1)S(1)}, u32[]{:S(2)}, u32[]{:S(2)}) collective-permute-start(bf16[16,4096]{1,0:T(8,128)(2,1)S(1)} %get-tuple-element.106), channel_id=1, source_target_pairs={{0,3},{8,56},{16,19},{24,8},{32,35},{40,24},{48,51},{56,40},{4,7},... | collective-permute-start | bytes 393224 | tf_op jit(solution)/shard_map/ppermute | solution.py:45
  254.0 8.0 %collective-permute-start.36 = (bf16[16,4096]{1,0:T(8,128)(2,1)S(1)}, bf16[16,4096]{1,0:T(8,128)(2,1)S(1)}, u32[]{:S(2)}, u32[]{:S(2)}) collective-permute-start(bf16[16,4096]{1,0:T(8,128)(2,1)S(1)} %get-tuple-element.107), channel_id=1, source_target_pairs={{0,2},{8,40},{16,18},{24,56},{32,34},{40,8},{48,50},{56,24},{4,6},... | collective-permute-start | bytes 393224 | tf_op jit(solution)/shard_map/ppermute | solution.py:45
  254.9 7.1 %collective-permute-start.35 = (bf16[16,4096]{1,0:T(8,128)(2,1)S(1)}, bf16[16,4096]{1,0:T(8,128)(2,1)S(1)}, u32[]{:S(2)}, u32[]{:S(2)}) collective-permute-start(bf16[16,4096]{1,0:T(8,128)(2,1)S(1)} %get-tuple-element.108), channel_id=1, source_target_pairs={{0,1},{8,24},{16,17},{24,40},{32,33},{40,56},{48,49},{56,8},{4,5},... | collective-permute-start | bytes 393224 | tf_op jit(solution)/shard_map/ppermute | solution.py:45
  (35 other events, 342.4 us)

commit v3 on v2

--- a/solution.py
+++ b/solution.py
@@ -45,8 +45,8 @@
     return lax.ppermute(array, AXES, shifted(dims, step))
 
 
-def swap_cores(array):
-    return lax.ppermute(array, "k", [(0, 1), (1, 0)])
+def swap_cores(arrays):
+    return [lax.ppermute(array, "k", [(0, 1), (1, 0)]) for array in arrays]
 
 
 def gather_step(block, dims):
@@ -156,16 +156,18 @@
     return refs[0][...] if len(refs) == 1 else jnp.concatenate([ref[...] for ref in refs], 0)
 
 
-def store_slots(found, tile, own_ref, other_ref):
-    slots = found.shape[0] // 4
-    span = pl.ds(tile * slots, slots)
-    own_ref[0, span, :] = found[0:slots]
-    own_ref[1, span, :] = found[slots : 2 * slots]
-    other_ref[0, span, :] = found[2 * slots : 3 * slots]
-    other_ref[1, span, :] = found[3 * slots :]
-
-
-def pack_rows(me, groups, width, chunk):
+def store_slots(found, own_ref, other_refs):
+    slots = found[0].shape[0] // 4
+    for e in range(2):
+        own_ref[e] = jnp.concatenate([tile[e * slots : (e + 1) * slots] for tile in found], 0)
+        rows = jnp.concatenate([tile[(e + 2) * slots : (e + 3) * slots] for tile in found], 0)
+        at = 0
+        for ref in other_refs:
+            ref[e] = rows[at : at + ref.shape[1]]
+            at += ref.shape[1]
+
+
+def pack_rows(me, groups, cuts, width, chunk):
     parts = [part for group in groups for part in group]
     tile_rows = sum(part.shape[0] for part in groups[0])
     slots = tile_rows // ROWS * CAP
@@ -174,7 +176,7 @@
 
     def kernel(me_ref, *refs):
         metas, rows = refs[:total], refs[total : 2 * total]
-        own_ref, other_ref, place_ref, weight_ref = refs[2 * total :]
+        own_ref, *other_refs, place_ref, weight_ref = refs[2 * total :]
 
         @pl.when(pl.program_id(0) == 0)
         def _():
@@ -186,33 +188,36 @@
                 place_ref[tile] = place.astype(jnp.bfloat16)
                 weight_ref[tile] = jnp.broadcast_to(weight, weight_ref.shape[1:])
 
-        at = 0
+        at, found = 0, []
         for tile, group in enumerate(groups):
             block = joined(rows[at : at + len(group)])
             at += len(group)
-            found = jnp.dot(place_ref[tile], block, preferred_element_type=jnp.float32)
-            store_slots(found.astype(jnp.bfloat16), tile, own_ref, other_ref)
-
-    out_block = pl.BlockSpec((2, count * slots, chunk), lambda j: (0, 0, j))
-    return call(
+            rows_of = jnp.dot(place_ref[tile], block, preferred_element_type=jnp.float32)
+            found.append(rows_of.astype(jnp.bfloat16))
+        store_slots(found, own_ref, other_refs)
+
+    own, *others, place, weight = call(
         kernel,
         (width // chunk,),
         (me, *parts, *parts),
         [pl.BlockSpec(memory_space=pltpu.SMEM)]
         + [pl.BlockSpec((part.shape[0], META), lambda j: (0, meta_at)) for part in parts]
         + [pl.BlockSpec((part.shape[0], chunk), lambda j: (0, j)) for part in parts],
-        [shape((2, count * slots, width))] * 2
+        [shape((2, count * slots, width))]
+        + [shape((2, cut, width)) for cut in cuts]
         + [
             shape((count, 4 * slots, tile_rows)),
             shape((count, 4 * slots, META), jnp.float32),
         ],
-        [out_block, out_block]
+        [pl.BlockSpec((2, count * slots, chunk), lambda j: (0, 0, j))]
+        + [pl.BlockSpec((2, cut, chunk), lambda j: (0, 0, j)) for cut in cuts]
         + [
             pl.BlockSpec((count, 4 * slots, tile_rows), lambda j: (0, 0, 0)),
             pl.BlockSpec((count, 4 * slots, META), lambda j: (0, 0, 0)),
         ],
         2 * count * 4 * slots * tile_rows * width,
     )
+    return own, others, place, weight
 
 
 def pack_grads(places, weights, tiles, chunk):
@@ -224,44 +229,51 @@
 
     def kernel(*refs):
         place_refs, weight_refs = refs[:count], refs[count : 2 * count]
-        rows, (own_ref, other_ref) = refs[2 * count : -2], refs[-2:]
+        rows = refs[2 * count : 2 * count + len(parts)]
+        own_ref, *other_refs = refs[2 * count + len(parts) :]
         placed = [ref[t] for ref in place_refs for t in range(ref.shape[0])]
         scales = [ref[t] for ref in weight_refs for t in range(ref.shape[0])]
-        at = 0
+        at, found = 0, []
         for tile, group in enumerate(tiles):
             block = joined(rows[at : at + len(group)])
             at += len(group)
-            found = jnp.dot(placed[tile], block, preferred_element_type=jnp.float32)
-            found = (found * scales[tile][:, 0:1]).astype(jnp.bfloat16)
-            store_slots(found, tile, own_ref, other_ref)
-
-    out_block = pl.BlockSpec((2, len(tiles) * slots, chunk), lambda j: (0, 0, j))
-    return call(
+            rows_of = jnp.dot(placed[tile], block, preferred_element_type=jnp.float32)
+            found.append((rows_of * scales[tile][:, 0:1]).astype(jnp.bfloat16))
+        store_slots(found, own_ref, other_refs)
+
+    own, *others = call(
         kernel,
         (width // chunk,),
         (*places, *weights, *parts),
         [pl.BlockSpec(a.shape, lambda j: (0, 0, 0)) for a in (*places, *weights)]
         + [pl.BlockSpec((part.shape[0], chunk), lambda j: (0, j)) for part in parts],
-        [shape((2, len(tiles) * slots, width))] * 2,
-        [out_block, out_block],
+        [shape((2, len(tiles) * slots, width))] + [shape((2, slots, width))] * len(tiles),
+        [pl.BlockSpec((2, len(tiles) * slots, chunk), lambda j: (0, 0, j))]
+        + [pl.BlockSpec((2, slots, chunk), lambda j: (0, 0, j))] * len(tiles),
         2 * len(tiles) * 4 * slots * tile_rows * width,
         told=True,
     )
-
-
-def merge(place, weight, own, other, pieces, chunk, into=()):
+    return own, others
+
+
+def merge(place, weight, own, others, pieces, chunk, into=()):
     width = own.shape[2]
     rows = place.shape[2]
     slots = place.shape[1] // 4
     count = own.shape[1] // slots
 
-    def kernel(place_ref, weight_ref, own_ref, other_ref, *refs):
-        outs = refs[len(into) :]
+    def kernel(place_ref, weight_ref, own_ref, *refs):
+        outs = refs[len(others) + len(into) :]
+        other_rows = [
+            jnp.concatenate([ref[e] for ref in refs[: len(others)]], 0) for e in range(2)
+        ]
         totals = []
         for tile in range(count):
             span = pl.ds(tile * slots, slots)
             block = jnp.concatenate(
-                [ref[e, span, :] for ref in (own_ref, other_ref) for e in range(2)], 0
+                [own_ref[e, span, :] for e in range(2)]
+                + [rows_of[tile * slots : (tile + 1) * slots] for rows_of in other_rows],
+                0,
             )
             scale = weight_ref[tile][:, 0:1]
             scaled = (block.astype(jnp.float32) * scale).astype(jnp.bfloat16)
@@ -271,24 +283,23 @@
             out[...] = totals[at // rows][at % rows : at % rows + size]
             at += size
 
-    slot_block = pl.BlockSpec((2, own.shape[1], chunk), lambda j: (0, 0, j))
     return pl.pallas_call(
         kernel,
         grid=(width // chunk,),
         in_specs=[
             pl.BlockSpec(place.shape, lambda j: (0, 0, 0)),
             pl.BlockSpec(weight.shape, lambda j: (0, 0, 0)),
-            slot_block,
-            slot_block,
+            pl.BlockSpec((2, own.shape[1], chunk), lambda j: (0, 0, j)),
         ]
+        + [pl.BlockSpec((2, other.shape[1], chunk), lambda j: (0, 0, j)) for other in others]
         + [pl.BlockSpec(memory_space=pl.ANY)] * len(into),
         out_specs=[
             pl.BlockSpec((size, chunk), lambda j, at=at: (at, j)) for size, _, at in pieces
         ],
         out_shape=[shape((total, width)) for _, total, _ in pieces],
-        input_output_aliases={4 + i: i for i in range(len(into))},
+        input_output_aliases={3 + len(others) + i: i for i in range(len(into))},
         compiler_params=pltpu.CompilerParams(vmem_limit_bytes=24 * 1024 * 1024),
-    )(place, weight, own, other, *into)
+    )(place, weight, own, *others, *into)
 
 
 def dot_t(a, b):
@@ -299,18 +310,20 @@
     return lax.dot_general(a, b, (((0,), (0,)), ((), ())), preferred_element_type=jnp.float32)
 
 
-def forward(own, other, w_gate, w_up, w_down, chunk):
+def forward(own, others, backs_cuts, w_gate, w_up, w_down, chunk):
     experts, rows, width = own.shape
     hidden = w_gate.shape[1]
     steps = width // chunk
-
-    def kernel(own_ref, other_ref, wg_ref, wu_ref, wd_ref, *rest):
-        own_out, other_out, hidden_ref, gate_sum, up_sum, active_ref = rest
+    count = len(others)
+
+    def kernel(own_ref, *refs):
+        other_refs, (wg_ref, wu_ref, wd_ref) = refs[:count], refs[count : count + 3]
+        own_out, *other_outs, hidden_ref, gate_sum, up_sum, active_ref = refs[count + 3 :]
         step = pl.program_id(1)
 
         @pl.when(step < steps)
         def _():
-            block = jnp.concatenate([own_ref[0], other_ref[0]], 0)
+            block = jnp.concatenate([own_ref[0]] + [ref[0] for ref in other_refs], 0)
             gate = dot_t(block, wg_ref[0])
             up = dot_t(block, wu_ref[0])
 
@@ -336,7 +349,10 @@
             out = jnp.dot(active_ref[...], wd_ref[0], preferred_element_type=jnp.float32)
             out = out.astype(jnp.bfloat16)
             own_out[0] = out[:rows]
-            other_out[0] = out[rows:]
+            at = rows
+            for other_out in other_outs:
+                other_out[0] = out[at : at + other_out.shape[1]]
+                at += other_out.shape[1]
 
     def early(e, s):
         return (e, 0, jnp.minimum(s, steps - 1))
@@ -346,15 +362,18 @@
 
     row_block = pl.BlockSpec((1, rows, chunk), early)
     weight_block = pl.BlockSpec((1, hidden, chunk), early)
-    return call(
+    out, *backs, values = call(
         kernel,
         (experts, 2 * steps),
-        (own, other, w_gate, w_up, w_down),
-        [row_block, row_block, weight_block, weight_block, pl.BlockSpec((1, hidden, chunk), late)],
-        [shape(own.shape), shape(own.shape), shape((experts, 2, 2 * rows, hidden), jnp.float32)],
+        (own, *others, w_gate, w_up, w_down),
+        [row_block]
+        + [pl.BlockSpec((1, other.shape[1], chunk), early) for other in others]
+        + [weight_block, weight_block, pl.BlockSpec((1, hidden, chunk), late)],
+        [shape(own.shape)] + [shape((experts, cut, width)) for cut in backs_cuts]
+        + [shape((experts, 2, 2 * rows, hidden), jnp.float32)],
         [
             pl.BlockSpec((1, rows, chunk), late),
-            pl.BlockSpec((1, rows, chunk), late),
+            *[pl.BlockSpec((1, cut, chunk), late) for cut in backs_cuts],
             pl.BlockSpec((1, 2, 2 * rows, hidden), lambda e, s: (e, 0, 0, 0)),
         ],
         12 * experts * rows * hidden * width,
@@ -364,15 +383,17 @@
             pltpu.VMEM((2 * rows, hidden), jnp.bfloat16),
         ],
     )
+    return out, backs, values
 
 
 def back_act(grads, w_down, chunk):
-    experts, rows, width = grads[0].shape
+    experts, _, width = grads[0].shape
+    rows = sum(part.shape[1] for part in grads)
     hidden = w_down.shape[1]
 
-    def kernel(own_ref, other_ref, wd_ref, out_ref):
-        block = jnp.concatenate([own_ref[0], other_ref[0]], 0)
-        found = dot_t(block, wd_ref[0])
+    def kernel(*refs):
+        wd_ref, out_ref = refs[-2:]
+        found = dot_t(jnp.concatenate([ref[0] for ref in refs[:-2]], 0), wd_ref[0])
 
         @pl.when(pl.program_id(1) == 0)
         def _():
@@ -382,15 +403,15 @@
         def _():
             out_ref[0] += found
 
-    row_block = pl.BlockSpec((1, rows, chunk), lambda e, s: (e, 0, s))
     return call(
         kernel,
         (experts, width // chunk),
         (*grads, w_down),
-        [row_block, row_block, pl.BlockSpec((1, hidden, chunk), lambda e, s: (e, 0, s))],
-        [shape((experts, 2 * rows, hidden), jnp.float32)],
-        [pl.BlockSpec((1, 2 * rows, hidden), lambda e, s: (e, 0, 0))],
-        4 * experts * rows * hidden * width,
+        [pl.BlockSpec((1, part.shape[1], chunk), lambda e, s: (e, 0, s)) for part in grads]
+        + [pl.BlockSpec((1, hidden, chunk), lambda e, s: (e, 0, s))],
+        [shape((experts, rows, hidden), jnp.float32)],
+        [pl.BlockSpec((1, rows, hidden), lambda e, s: (e, 0, 0))],
+        2 * experts * rows * hidden * width,
         told=True,
     )[0]
 
@@ -405,43 +426,44 @@
 
 
 def down_grad(grads, hiddens, chunk):
-    experts, rows, width = grads[0].shape
+    experts, _, width = grads[0].shape
+    rows = sum(part.shape[1] for part in grads)
     units = hiddens[0].shape[3]
-
-    def kernel(own_ref, other_ref, *refs):
-        hidden_refs, out_ref, active_ref = refs[:-2], refs[-2], refs[-1]
+    count = len(grads)
+
+    def kernel(*refs):
+        hidden_refs, out_ref, active_ref = refs[count:-2], refs[-2], refs[-1]
 
         @pl.when(pl.program_id(1) == 0)
         def _():
             gate, up = hidden_of(hidden_refs, 0), hidden_of(hidden_refs, 1)
             active_ref[...] = (gate * jax.nn.sigmoid(gate) * up).astype(jnp.bfloat16)
 
-        block = jnp.concatenate([own_ref[0], other_ref[0]], 0)
+        block = jnp.concatenate([ref[0] for ref in refs[:count]], 0)
         out_ref[0] = t_dot(active_ref[...], block).astype(jnp.bfloat16)
 
-    row_block = pl.BlockSpec((1, rows, chunk), lambda e, s: (e, 0, s))
     return call(
         kernel,
         (experts, width // chunk),
         (*grads, *hiddens),
-        [row_block, row_block]
+        [pl.BlockSpec((1, part.shape[1], chunk), lambda e, s: (e, 0, s)) for part in grads]
         + [pl.BlockSpec((1,) + h.shape[1:], lambda e, s: (e, 0, 0, 0)) for h in hiddens],
         [shape((experts, units, width))],
         [pl.BlockSpec((1, units, chunk), lambda e, s: (e, 0, s))],
-        4 * experts * rows * units * width,
-        [pltpu.VMEM((2 * rows, units), jnp.bfloat16)],
+        2 * experts * rows * units * width,
+        [pltpu.VMEM((rows, units), jnp.bfloat16)],
         told=True,
     )[0]
 
 
-def up_grads(back, groups, hiddens, chunk):
+def up_grads(back, ordered, hiddens, chunk):
     experts, rows, units = back.shape
-    width = groups[0][0].shape[2]
-    count = len(groups)
+    width = ordered[0].shape[2]
+    count = len(ordered)
 
     def kernel(back_ref, *refs):
-        row_refs, hidden_refs = refs[: 2 * count], refs[2 * count : 3 * count]
-        dg_ref, du_ref, dgate, dup = refs[3 * count :]
+        row_refs, hidden_refs = refs[:count], refs[count:-4]
+        dg_ref, du_ref, dgate, dup = refs[-4:]
 
         @pl.when(pl.program_id(1) == 0)
         def _():
@@ -455,7 +477,6 @@
         dg_ref[0] = t_dot(dgate[...], block).astype(jnp.bfloat16)
         du_ref[0] = t_dot(dup[...], block).astype(jnp.bfloat16)
 
-    ordered = [group[side] for side in range(2) for group in groups]
     out_block = pl.BlockSpec((1, units, chunk), lambda e, s: (e, 0, s))
     return call(
         kernel,
@@ -521,7 +542,7 @@
         [pl.BlockSpec((rows, width), lambda h: (0, 0))],
         2 * rows * queries.shape[1] * (2 * tokens + width),
         [pltpu.VMEM((rows, width), jnp.float32)],
-        limit=32,
+        limit=56,
     )[0]
 
 
@@ -576,32 +597,37 @@
     near = jnp.concatenate(
         gather_step(jnp.concatenate([normed, meta], 1), stage_dims(0)), 0
     )
-    near = jnp.concatenate(gather_step(after(near, *cot_sides), stage_dims(1)), 0)
+    near = after(jnp.concatenate(gather_step(near, stage_dims(1)), 0), *cot_sides)
     left, right = gather_sides(near)
     half = near.shape[0] // 2
     narrow, wide = 2 * chunk, 4 * chunk
 
-    def run_forward(rows_own, rows_got):
-        return forward(rows_own, rows_got, w_gate, w_up, w_down, wide)
-
-    own0, other0, place0, weight0 = pack_rows(me, [[near]], width, narrow)
+    slots = near.shape[0] // ROWS * CAP
+    cuts = [slots // 32 * 16 + 16, slots // 32 * 16]
+    thirds = [cuts[0], 2 * cuts[1], cuts[0]]
+
+    def run_forward(rows_own, rows_got, backs):
+        return forward(rows_own, rows_got, backs, w_gate, w_up, w_down, wide)
+
+    own0, other0, place0, weight0 = pack_rows(me, [[near]], [slots], width, narrow)
     got0 = swap_cores(other0)
-    out0, back0, hidden0 = run_forward(own0, got0)
+    out0, back0, hidden0 = run_forward(own0, got0, [slots])
     back0 = swap_cores(back0)
     left, right = after(left, out0), after(right, out0)
 
     far_a, far_b = gather_far(left, right)
-    own1, other1, place1, weight1 = pack_rows(me, [[left], [right]], width, narrow)
+    own1, other1, place1, weight1 = pack_rows(me, [[left], [right]], thirds, width, narrow)
     got1 = swap_cores(other1)
-    (sum0,) = merge(place0, weight0, after(out0, other1), back0, [(2 * half, 2 * half, 0)], narrow)
-    out1, back1, hidden1 = run_forward(after(own1, sum0), got1)
+    (sum0,) = merge(place0, weight0, after(out0, *other1), back0, [(2 * half, 2 * half, 0)], narrow)
+    out1, back1, hidden1 = run_forward(after(own1, sum0), got1, [2 * slots])
     back1 = swap_cores(back1)
 
-    far_got = far_a
+    cot_left, cot_right = (after(side, far_a) for side in cot_sides)
+    cot_far = gather_far(cot_left, cot_right)
     far_a, far_b = after(far_a, out1), after(far_b, out1)
-    own2, other2, place2, weight2 = pack_rows(me, [[far_a, far_b]], width, narrow)
+    own2, other2, place2, weight2 = pack_rows(me, [[far_a, far_b]], cuts, width, narrow)
     got2 = swap_cores(other2)
-    out2, back2, hidden2 = run_forward(own2, got2)
+    out2, back2, hidden2 = run_forward(own2, got2, cuts)
     back2 = swap_cores(back2)
 
     dims = stage_dims(2)
@@ -616,7 +642,7 @@
     minus, plus = merge(
         place2,
         weight2,
-        after(out2, left_a),
+        after(out2, left_a, *cot_far),
         back2,
         [(half, 2 * half, 0), (half, 2 * half, 1)],
         narrow,
@@ -624,16 +650,14 @@
     )
     got_minus, got_plus = send(minus, dims, -1), send(plus, dims, 1)
 
-    cot_left, cot_right = (after(side, far_got) for side in cot_sides)
-    cot_far = gather_far(cot_left, cot_right)
-    cot_tiles = [[after(cot_near, minus)], [cot_left], [cot_right], list(cot_far)]
+    cot_tiles = [[cot_near], [cot_left], [cot_right], list(cot_far)]
     places, weights = (place0, place1, place2), (weight0, weight1, weight2)
     grads_own, grads_other = pack_grads(places, weights, cot_tiles, chunk)
-    grads = (grads_own, swap_cores(grads_other))
+    grads = [grads_own] + swap_cores(grads_other)
     hiddens = [hidden0, hidden1, hidden2]
 
-    left_a = add(after(left_a, grads_other), got_minus[:half]).astype(jnp.bfloat16)
-    right_b = add(after(right_b, grads_other), got_plus[half:]).astype(jnp.bfloat16)
+    left_a = add(left_a, got_minus[:half]).astype(jnp.bfloat16)
+    right_b = add(right_b, got_plus[half:]).astype(jnp.bfloat16)
     got_left_a, got_right_b = send(left_a, dims, -1), send(right_b, dims, 1)
     back = back_act(grads, w_down, wide)
     sum0 = after(sum0, back)
@@ -644,9 +668,9 @@
         ],
         0,
     )
-    groups = [(own0, got0), (own1, got1), (own2, got2)]
     grad_down = down_grad(after_all(grads, back), hiddens, narrow)
-    grad_gate, grad_up = up_grads(back, groups, hiddens, narrow)
+    rows = [own0, own1, own2] + got0 + got1 + got2
+    grad_gate, grad_up = up_grads(back, rows, hiddens, narrow)
     combined = scatter_near(total)
     layer_out = (stream + combined).astype(jnp.bfloat16)
     return layer_out, grad_gate, grad_up, grad_down

time: 264 us -> 249 us (0.943)
  waiting for transfers between devices: 121 us -> 95.8 us
  starting transfers between devices: 54.4 us -> 62.1 us
  local copies, waits for them, and re-layouts: 14.6 us -> 10.5 us
  Pallas kernels: 67.6 us -> 71.2 us
    ppermute x30, waiting for transfers between devices: 93.4 us -> 76.3 us  [send(): return lax.ppermute(array, AXES, shifted(dims, step))]
    ppermute x7 -> x14, waiting for transfers between devices: 10.9 us -> 3.06 us  [swap_cores(): return [lax.ppermute(array, 'k', [(0, 1), (1, 0)]) for array in arrays]]
    ppermute x7 -> x14, starting transfers between devices: 2.92 us -> 8.44 us  [swap_cores(): return [lax.ppermute(array, 'k', [(0, 1), (1, 0)]) for array in arrays]]
    unnamed x63 -> x64, local copies, waits for them, and re-layouts: 8.38 us -> 4.69 us
    pallas_call x11, Pallas kernels: 58.7 us -> 62.4 us  [call(): pl.pallas_call(kernel, grid=grid, in_specs=in_specs, out_specs=out_specs,...]
  transfers between devices with their start and end apart: 39 -> 46, of which waited for: 22 -> 24; matrix products, arithmetic and copies ran while one was open for 4% -> 4% of each run, Pallas kernels for 22% -> 28%
where the time goes in v3:
time: 249 us; the launch traced here: 247 us
  waiting for transfers between devices  95.8 us (38%)
  Pallas kernels  71.2 us (29%)
  starting transfers between devices  62.1 us (25%)
  local copies, waits for them, and re-layouts  10.5 us (4%)
  other arithmetic  6.48 us (3%)
    ppermute x30, waiting for transfers between devices, send(): return lax.ppermute(array, AXES, shifted(dims, step))  76.3 us
    pallas_call x11, Pallas kernels, call(): pl.pallas_call(kernel, grid=grid, in_specs=in_specs, out_specs=out_specs,...  62.4 us
    ppermute x30, starting transfers between devices, send(): return lax.ppermute(array, AXES, shifted(dims, step))  40.9 us
    pallas_call x3, Pallas kernels, merge(): pl.pallas_call(kernel, grid=(width // chunk,), in_specs=[pl.BlockSpec(pla...  8.84 us
    all_to_all x1, waiting for transfers between devices, shards(): lax.all_to_all(jnp.broadcast_to(pair, (16,) + pair.shape), ('yh', 'z', 'k...  8.55 us
    ppermute x14, starting transfers between devices, swap_cores(): return [lax.ppermute(array, 'k', [(0, 1), (1, 0)]) for array in arrays]  8.44 us
    all_to_all x1, starting transfers between devices, shards(): lax.all_to_all(jnp.broadcast_to(pair, (16,) + pair.shape), ('yh', 'z', 'k...  8.13 us
    all_to_all x1, waiting for transfers between devices, shards(): lax.all_to_all(mixed, ('yl', 'x'), 0, 0, tiled=True).reshape(8, ROWS, width)  7.9 us
  transfers between devices with their start and end apart: 46, of which 24 were waited for; matrix products, arithmetic and copies ran while one was open for 4% of the time, Pallas kernels for 28%

profile of v3, /device:TPU:0, one launch (start us, length us, event | category | flops | bytes accessed | tf_op | source)
XLA Modules:
  0.0 247.3 jit_solution(6553451780416596093)
XLA Ops:
  2.6 8.1 %all-to-all-start = ((bf16[16,128,256]{2,1,0:T(8,128)(2,1)}), bf16[16,128,256]{2,1,0:T(8,128)(2,1)S(1)}, u32[]{:S(2)}, u32[]{:S(2)}) async-start(bf16[16,128,256]{2,1,0:T(8,128)(2,1)} %broadcast_in_dim.8), calls=%async_computation | async-start | bytes 2097152 | tf_op jit(solution)/shard_map/all_to_all | solution.py:572
  17.3 3.2 %collective-permute-done.8 = bf16[16,4096]{1,0:T(8,128)(2,1)S(1)} collective-permute-done((bf16[16,4096]{1,0:T(8,128)(2,1)S(1)}, bf16[16,4096]{1,0:T(8,128)(2,1)S(1)}, u32[]{:S(2)}, u32[]{:S(2)}) %collective-permute-start.8) | collective-permute-done | bytes 131104 | tf_op jit(solution)/shard_map/ppermute | solution.py:45
  20.6 8.6 %all-to-all-done = bf16[16,128,256]{2,1,0:T(8,128)(2,1)S(1)} async-done(((bf16[16,128,256]{2,1,0:T(8,128)(2,1)}), bf16[16,128,256]{2,1,0:T(8,128)(2,1)S(1)}, u32[]{:S(2)}, u32[]{:S(2)}) %all-to-all-start) | async-done | bytes 1048608 | tf_op jit(solution)/shard_map/all_to_all | solution.py:572
  29.9 2.5 %collective-permute-start.10 = (bf16[64,4096]{1,0:T(8,128)(2,1)S(1)}, bf16[64,4096]{1,0:T(8,128)(2,1)}, u32[]{:S(2)}, u32[]{:S(2)}) collective-permute-start(bf16[64,4096]{1,0:T(8,128)(2,1)S(1)} %pad_maximum_fusion.1), channel_id=1, source_target_pairs={{0,68},{8,11},{16,84},{24,27},{32,100},{40,43},{48,116},{56,59},{4... | collective-permute-start | bytes 1572872 | tf_op jit(solution)/shard_map/ppermute | solution.py:45
  33.3 6.6 %shard_map.147 = bf16[128,4096]{1,0:T(8,128)(2,1)} custom-call(s32[1]{0:T(128)} %bitcast.base_ref, bf16[128,512]{1,0:T(8,128)(2,1)} %query_ref.1, bf16[2048,256]{1,0:T(8,128)(2,1)} %bitcast.4, bf16[512,4096]{1,0:T(8,128)(2,1)} %proj_ref.1), custom_call_target="tpu_custom_call" | custom-call | tf_op jit(solution)/shard_map/pallas_call | solution.py:139
  39.8 4.6 %all-to-all-start.1 = ((bf16[8,16,4096]{2,1,0:T(8,128)(2,1)}), bf16[8,16,4096]{2,1,0:T(8,128)(2,1)S(1)}, u32[]{:S(2)}, u32[]{:S(2)}) async-start(bf16[8,16,4096]{2,1,0:T(8,128)(2,1)} %bitcast.5), calls=%async_computation.1 | async-start | bytes 2097152 | tf_op jit(solution)/shard_map/all_to_all | solution.py:590
  49.7 3.2 %collective-permute-start.13 = (bf16[256,4096]{1,0:T(8,128)(2,1)}, bf16[256,4096]{1,0:T(8,128)(2,1)}, u32[]{:S(2)}, u32[]{:S(2)}) collective-permute-start(bf16[256,4096]{1,0:T(8,128)(2,1)} %constant_dynamic-update-slice_fusion.7.refs_6_), channel_id=1, source_target_pairs={{0,48},{8,76},{16,0},{24,92},{32,16},{40,108},{48,32},{56,124},{4,... | collective-permute-start | bytes 6291464 | tf_op jit(solution)/shard_map/ppermute | solution.py:45
  52.9 7.9 %all-to-all-done.1 = bf16[8,16,4096]{2,1,0:T(8,128)(2,1)S(1)} async-done(((bf16[8,16,4096]{2,1,0:T(8,128)(2,1)}), bf16[8,16,4096]{2,1,0:T(8,128)(2,1)S(1)}, u32[]{:S(2)}, u32[]{:S(2)}) %all-to-all-start.1) | async-done | bytes 1048608 | tf_op jit(solution)/shard_map/all_to_all | solution.py:590
  65.4 3.0 %collective-permute-done = bf16[16,4224]{1,0:T(8,128)(2,1)S(1)} collective-permute-done((bf16[16,4224]{1,0:T(8,128)(2,1)S(1)}, bf16[16,4224]{1,0:T(8,128)(2,1)S(1)}, u32[]{:S(2)}, u32[]{:S(2)}) %collective-permute-start) | collective-permute-done | bytes 135200 | tf_op jit(solution)/shard_map/ppermute | solution.py:45
  72.5 2.7 %collective-permute-start.4 = (bf16[64,4224]{1,0:T(8,128)(2,1)S(1)}, bf16[64,4224]{1,0:T(8,128)(2,1)S(1)}, u32[]{:S(2)}, u32[]{:S(2)}) collective-permute-start(bf16[64,4224]{1,0:T(8,128)(2,1)S(1)} %pad_maximum_fusion), channel_id=1, source_target_pairs={{0,68},{8,11},{16,84},{24,27},{32,100},{40,43},{48,116},{56,59},{4... | collective-permute-start | bytes 1622024 | tf_op jit(solution)/shard_map/ppermute | solution.py:45
  77.1 8.2 %collective-permute-done.3 = bf16[64,4224]{1,0:T(8,128)(2,1)S(1)} collective-permute-done((bf16[64,4224]{1,0:T(8,128)(2,1)S(1)}, bf16[64,4224]{1,0:T(8,128)(2,1)S(1)}, u32[]{:S(2)}, u32[]{:S(2)}) %collective-permute-start.3) | collective-permute-done | bytes 540704 | tf_op jit(solution)/shard_map/ppermute | solution.py:45
  87.8 9.0 %collective-permute-done.5 = bf16[64,4224]{1,0:T(8,128)(2,1)S(1)} collective-permute-done((bf16[64,4224]{1,0:T(8,128)(2,1)S(1)}, bf16[64,4224]{1,0:T(8,128)(2,1)S(1)}, u32[]{:S(2)}, u32[]{:S(2)}) %collective-permute-start.5) | collective-permute-done | bytes 540704 | tf_op jit(solution)/shard_map/ppermute | solution.py:45
  101.3 3.0 %collective-permute-done.14.refs_0_.refs_3_ = bf16[2,80,4096]{2,1,0:T(8,128)(2,1)S(1)} collective-permute-done((bf16[2,80,4096]{2,1,0:T(8,128)(2,1)S(1)}, bf16[2,80,4096]{2,1,0:T(8,128)(2,1)S(1)}, u32[]{:S(2)}, u32[]{:S(2)}) %collective-permute-start.14) | collective-permute-done | bytes 1310752 | tf_op jit(solution)/shard_map/ppermute | solution.py:49
  104.3 5.6 %shard_map.149 = (bf16[2,80,4096]{2,1,0:T(8,128)(2,1)S(1)}, bf16[2,80,4096]{2,1,0:T(8,128)(2,1)S(1)}, f32[2,2,160,192]{3,2,1,0:T(8,128)S(1)}) custom-call(bf16[2,80,4096]{2,1,0:T(8,128)(2,1)S(1)} %get-tuple-element.64.own_ref.refs_0_, bf16[2,80,4096]{2,1,0:T(8,128)(2,1)S(1)} %collective-permute-done.14.refs_0_.refs_3_, bf16[2,192,4096]{2,1,0:T(8,128)(2,1)S(1)} %copy-done.1, ...), custom_call_target="tpu_custom_call" | custom-call | tf_op jit(solution)/shard_map/pallas_call | solution.py:139
  110.3 13.4 %collective-permute-done.16.refs_1_.refs_3_ = bf16[256,4224]{1,0:T(8,128)(2,1)S(1)} collective-permute-done((bf16[256,4224]{1,0:T(8,128)(2,1)S(1)}, bf16[256,4224]{1,0:T(8,128)(2,1)S(1)}, u32[]{:S(2)}, u32[]{:S(2)}) %collective-permute-start.16) | collective-permute-done | bytes 2162720 | tf_op jit(solution)/shard_map/ppermute | solution.py:45
  125.3 3.6 %shard_map.150 = (bf16[2,160,4096]{2,1,0:T(8,128)(2,1)S(1)}, bf16[2,48,4096]{2,1,0:T(8,128)(2,1)S(1)}, bf16[2,64,4096]{2,1,0:T(8,128)(2,1)S(1)}, bf16[2,48,4096]...) custom-call(s32[1]{0:T(128)} %bitcast.3.me_ref, ...), custom_call_target="tpu_custom_call" | custom-call | tf_op jit(solution)/shard_map/pallas_call | solution.py:139
  134.3 7.7 %shard_map.152 = (bf16[2,160,4096]{2,1,0:T(8,128)(2,1)S(1)}, bf16[2,160,4096]{2,1,0:T(8,128)(2,1)S(1)}, f32[2,2,320,192]{3,2,1,0:T(8,128)S(1)}) custom-call(bf16[2,160,4096]{2,1,0:T(8,128)(2,1)S(1)} %get-tuple-element.76.own_ref.refs_1_, bf16[2,48,4096]{2,1,0:T(8,128)(2,1)S(1)} %collective-permute-done.19.refs_0_.refs_4_, ...), custom_call_target="tpu_custom_call" | custom-call | tf_op jit(solution)/shard_map/pallas_call | solution.py:139
  142.1 2.7 %collective-permute-start.31 = (bf16[2,160,4096]{2,1,0:T(8,128)(2,1)S(1)}, bf16[2,160,4096]{2,1,0:T(8,128)(2,1)S(1)}, u32[]{:S(2)}, u32[]{:S(2)}) collective-permute-start(bf16[2,160,4096]{2,1,0:T(8,128)(2,1)S(1)} %get-tuple-element.96), channel_id=1, source_target_pairs={{0,8},{8,0},{1,9},{9,1},{2,10},{10,2},{3,11},{11,3},{4,12},{12,4},... | collective-permute-start | bytes 7864328 | tf_op jit(solution)/shard_map/ppermute | solution.py:49
  148.6 3.5 %collective-permute-start.29 = (bf16[2,48,4096]{2,1,0:T(8,128)(2,1)S(1)}, bf16[2,48,4096]{2,1,0:T(8,128)(2,1)S(1)}, u32[]{:S(2)}, u32[]{:S(2)}) collective-permute-start(bf16[2,48,4096]{2,1,0:T(8,128)(2,1)S(1)} %get-tuple-element.92), channel_id=1, source_target_pairs={{0,8},{8,0},{1,9},{9,1},{2,10},{10,2},{3,11},{11,3},{4,12},{12,4},... | collective-permute-start | bytes 2359304 | tf_op jit(solution)/shard_map/ppermute | solution.py:49
  153.7 3.3 %collective-permute-start.24 = (bf16[128,4096]{1,0:T(8,128)(2,1)S(1)}, bf16[128,4096]{1,0:T(8,128)(2,1)S(1)}, u32[]{:S(2)}, u32[]{:S(2)}) collective-permute-start(bf16[128,4096]{1,0:T(8,128)(2,1)S(1)} %slice.69), channel_id=1, source_target_pairs={{0,48},{8,76},{16,0},{24,92},{32,16},{40,108},{48,32},{56,124},{4,... | collective-permute-start | bytes 3145736 | tf_op jit(solution)/shard_map/ppermute | solution.py:45
  157.0 5.6 %shard_map.156 = (bf16[2,80,4096]{2,1,0:T(8,128)(2,1)S(1)}, bf16[2,48,4096]{2,1,0:T(8,128)(2,1)S(1)}, bf16[2,32,4096]{2,1,0:T(8,128)(2,1)S(1)}, f32[2,2,160,192]{3,2,1,0:T(8,128)S(1)}) custom-call(bf16[2,80,4096]{2,1,0:T(8,128)(2,1)S(1)} %get-tuple-element.91.own_ref.refs_2_, bf16[2,48,4096]{2,1,0:T(8,128)(2,1)S(1)} %collective-permute-done.29.refs_0_.refs_7_, ...), custom_call_target="tpu_custom_call" | custom-call | tf_op jit(solution)/shard_map/pallas_call | solution.py:139
  164.0 4.0 %shard_map.157 = (bf16[128,4096]{1,0:T(8,128)(2,1)S(1)}, bf16[256,4096]{1,0:T(8,128)(2,1)S(1)}, bf16[256,4096]{1,0:T(8,128)(2,1)S(1)}, bf16[128,4096]{1,0:T(8,128)(2,1)S(1)}) custom-call(bf16[2,320,256]{2,1,0:T(8,128)(2,1)S(1)} %get-tuple-element.74.refs_1_.place_ref, f32[2,320,128]{2,1,0:T(8,128)S(1)} %get-tuple-element.81.refs_4_.weight_ref, ...), custom_call_target="tpu_custom_call" | custom-call | tf_op jit(solution)/shard_map/pallas_call | solution.py:286
  171.9 3.8 %collective-permute-start.34 = (bf16[256,4096]{1,0:T(8,128)(2,1)S(1)}, bf16[256,4096]{1,0:T(8,128)(2,1)}, u32[]{:S(2)}, u32[]{:S(2)}) collective-permute-start(bf16[256,4096]{1,0:T(8,128)(2,1)S(1)} %get-tuple-element.103), channel_id=1, source_target_pairs={{0,48},{8,76},{16,0},{24,92},{32,16},{40,108},{48,32},{56,124},{4,... | collective-permute-start | bytes 6291464 | tf_op jit(solution)/shard_map/ppermute | solution.py:45
  175.6 8.6 %shard_map.154 = (bf16[2,320,4096]{2,1,0:T(8,128)(2,1)S(1)}, bf16[2,80,4096]{2,1,0:T(8,128)(2,1)}, bf16[2,80,4096]{2,1,0:T(8,128)(2,1)}, bf16[2,80,4096]{2,1,0:T(8,128)(2,1)}, bf16[2,80,4096]{2,1,0:T(8,128)(2,1)S(1)}) custom-call(bf16[1,320,256]{2,1,0:T(8,128)(2,1)S(1)} %get-tuple-element.62.place_ref.refs_0_, ...), custom_call_target="tpu_custom_call" | custom-call | flops 2684354560 | bytes 20185088 | tf_op jit(solution)/shard_map/pallas_call | solution.py:139
  184.8 14.8 %collective-permute-done.36 = bf16[256,4096]{1,0:T(8,128)(2,1)S(1)} collective-permute-done((bf16[256,4096]{1,0:T(8,128)(2,1)S(1)}, bf16[256,4096]{1,0:T(8,128)(2,1)S(1)}, u32[]{:S(2)}, u32[]{:S(2)}) %collective-permute-start.36) | collective-permute-done | bytes 2097184 | tf_op jit(solution)/shard_map/ppermute | solution.py:45
  204.7 4.7 %shard_map.155.back_ref = f32[2,640,192]{2,1,0:T(8,128)S(1)} custom-call(bf16[2,320,4096]{2,1,0:T(8,128)(2,1)S(1)} %get-tuple-element.111.refs_0_, bf16[2,80,4096]{2,1,0:T(8,128)(2,1)S(1)} %collective-permute-done.25.refs_1_, bf16[2,80,4096]{2,1,0:T(8,128)(2,1)S(1)} %collective-permute-done.26.refs_2_, ...), custom_call_target="tpu_custom_call" | custom-call | flops 2013265920 | bytes 14614528 | tf_op jit(solution)/shard_map/pallas_call | solution.py:139
  209.5 6.5 %collective-permute-done.38 = bf16[128,4096]{1,0:T(8,128)(2,1)S(1)} collective-permute-done((bf16[128,4096]{1,0:T(8,128)(2,1)S(1)}, bf16[128,4096]{1,0:T(8,128)(2,1)S(1)}, u32[]{:S(2)}, u32[]{:S(2)}) %collective-permute-start.38) | collective-permute-done | bytes 1048608 | tf_op jit(solution)/shard_map/ppermute | solution.py:45
  217.5 2.5 %add_convert_fusion.2 = (bf16[128,4096]{1,0:T(8,128)(2,1)S(1)}, bf16[128,4096]{1,0:T(8,128)(2,1)S(1)}) fusion(bf16[128,4096]{1,0:T(8,128)(2,1)S(1)} %collective-permute-done.35, bf16[256,4096]{1,0:T(8,128)(2,1)S(1)} %collective-permute-done.36, bf16[256,4096]{1,0:T(8,128)(2,1)S(1)} %shard_map.151, bf16[128,4096]{1,0:T(8,128)(2,1)S(1)} %collective-permute-done.38, ...), kind=kLoop, calls=%fused_computation.2 | loop fusion | flops 6291456 | bytes 8388608 | tf_op jit(solution)/shard_map/convert
  220.2 2.9 %collective-permute-start.40 = (bf16[64,4096]{1,0:T(8,128)(2,1)S(1)}, bf16[64,4096]{1,0:T(8,128)(2,1)S(1)}, u32[]{:S(2)}, u32[]{:S(2)}) collective-permute-start(bf16[64,4096]{1,0:T(8,128)(2,1)S(1)} %get-tuple-element.119), channel_id=1, source_target_pairs={{0,64},{8,10},{16,80},{24,26},{32,96},{40,42},{48,112},{56,58},{4,... | collective-permute-start | bytes 1572872 | tf_op jit(solution)/shard_map/ppermute | solution.py:45
  223.6 9.1 %shard_map.159 = (bf16[2,192,4096]{2,1,0:T(8,128)(2,1)}, bf16[2,192,4096]{2,1,0:T(8,128)(2,1)}) custom-call(f32[2,640,192]{2,1,0:T(8,128)S(1)} %shard_map.155.back_ref, bf16[2,80,4096]{2,1,0:T(8,128)(2,1)S(1)} %get-tuple-element.64.own_ref.refs_0_, bf16[2,160,4096]{2,1,0:T(8,128)(2,1)S(1)} %get-tuple-element.76.own_ref.refs_1_, ...), custom_call_target="tpu_custom_call" | custom-call | flops 4026531840 | bytes 19726336 | tf_op jit(solution)/shard_map/pallas_call | solution.py:139
  232.7 3.5 %collective-permute-done.39 = bf16[64,4096]{1,0:T(8,128)(2,1)S(1)} collective-permute-done((bf16[64,4096]{1,0:T(8,128)(2,1)S(1)}, bf16[64,4096]{1,0:T(8,128)(2,1)S(1)}, u32[]{:S(2)}, u32[]{:S(2)}) %collective-permute-start.39) | collective-permute-done | bytes 524320 | tf_op jit(solution)/shard_map/ppermute | solution.py:45
  240.2 6.3 %shard_map.160 = bf16[2,192,4096]{2,1,0:T(8,128)(2,1)} custom-call(bf16[2,320,4096]{2,1,0:T(8,128)(2,1)S(1)} %get-tuple-element.111.refs_0_, bf16[2,80,4096]{2,1,0:T(8,128)(2,1)S(1)} %collective-permute-done.25.refs_1_, bf16[2,80,4096]{2,1,0:T(8,128)(2,1)S(1)} %collective-permute-done.26.refs_2_, bf16[2,80,4096]{2,1,0:T(8,128)(2,1)S(1)} %collective-permute-done.27.refs_3_, ...), custom_call_target="tpu_custom_call" | custom-call | flops 2013265920 | bytes 15597568 | tf_op jit(solution)/shard_map/pallas_call | solution.py:139
  (168 shorter events, 63.6 us)
Async XLA Ops:
  2.6 26.5 %all-to-all-start = ((bf16[16,128,256]{2,1,0:T(8,128)(2,1)}), bf16[16,128,256]{2,1,0:T(8,128)(2,1)S(1)}, u32[]{:S(2)}, u32[]{:S(2)}) async-start(bf16[16,128,256]{2,1,0:T(8,128)(2,1)} %broadcast_in_dim.8), calls=%async_computation | async-start | bytes 2097152 | tf_op jit(solution)/shard_map/all_to_all | solution.py:572
  29.1 16.0 %collective-permute-start.9 = (bf16[64,4096]{1,0:T(8,128)(2,1)S(1)}, bf16[64,4096]{1,0:T(8,128)(2,1)S(1)}, u32[]{:S(2)}, u32[]{:S(2)}) collective-permute-start(bf16[64,4096]{1,0:T(8,128)(2,1)S(1)} %pad_maximum_fusion.1), channel_id=1, source_target_pairs={{0,4},{8,9},{16,20},{24,25},{32,36},{40,41},{48,52},{56,57},{4,64}... | collective-permute-start | bytes 1572872 | tf_op jit(solution)/shard_map/ppermute | solution.py:45
  29.9 16.0 %collective-permute-start.10 = (bf16[64,4096]{1,0:T(8,128)(2,1)S(1)}, bf16[64,4096]{1,0:T(8,128)(2,1)}, u32[]{:S(2)}, u32[]{:S(2)}) collective-permute-start(bf16[64,4096]{1,0:T(8,128)(2,1)S(1)} %pad_maximum_fusion.1), channel_id=1, source_target_pairs={{0,68},{8,11},{16,84},{24,27},{32,100},{40,43},{48,116},{56,59},{4... | collective-permute-start | bytes 1572872 | tf_op jit(solution)/shard_map/ppermute | solution.py:45
  33.3 14.5 %collective-permute-start.11 = (bf16[64,4096]{1,0:T(8,128)(2,1)S(1)}, bf16[64,4096]{1,0:T(8,128)(2,1)}, u32[]{:S(2)}, u32[]{:S(2)}) collective-permute-start(bf16[64,4096]{1,0:T(8,128)(2,1)S(1)} %pad_maximum_fusion.1), channel_id=1, source_target_pairs={{0,64},{8,10},{16,80},{24,26},{32,96},{40,42},{48,112},{56,58},{4,... | collective-permute-start | bytes 1572872 | tf_op jit(solution)/shard_map/ppermute | solution.py:45
  39.8 21.0 %all-to-all-start.1 = ((bf16[8,16,4096]{2,1,0:T(8,128)(2,1)}), bf16[8,16,4096]{2,1,0:T(8,128)(2,1)S(1)}, u32[]{:S(2)}, u32[]{:S(2)}) async-start(bf16[8,16,4096]{2,1,0:T(8,128)(2,1)} %bitcast.5), calls=%async_computation.1 | async-start | bytes 2097152 | tf_op jit(solution)/shard_map/all_to_all | solution.py:590
  49.7 47.1 %collective-permute-start.12 = (bf16[256,4096]{1,0:T(8,128)(2,1)}, bf16[256,4096]{1,0:T(8,128)(2,1)S(1)}, u32[]{:S(2)}, u32[]{:S(2)}) collective-permute-start(bf16[256,4096]{1,0:T(8,128)(2,1)} %constant_dynamic-update-slice_fusion.7.refs_6_), channel_id=1, source_target_pairs={{0,16},{8,12},{16,32},{24,28},{32,48},{40,44},{48,0},{56,60},{4,20... | collective-permute-start | bytes 6291464 | tf_op jit(solution)/shard_map/ppermute | solution.py:45
  49.7 47.2 %collective-permute-start.13 = (bf16[256,4096]{1,0:T(8,128)(2,1)}, bf16[256,4096]{1,0:T(8,128)(2,1)}, u32[]{:S(2)}, u32[]{:S(2)}) collective-permute-start(bf16[256,4096]{1,0:T(8,128)(2,1)} %constant_dynamic-update-slice_fusion.7.refs_6_), channel_id=1, source_target_pairs={{0,48},{8,76},{16,0},{24,92},{32,16},{40,108},{48,32},{56,124},{4,... | collective-permute-start | bytes 6291464 | tf_op jit(solution)/shard_map/ppermute | solution.py:45
  71.9 13.3 %collective-permute-start.3 = (bf16[64,4224]{1,0:T(8,128)(2,1)S(1)}, bf16[64,4224]{1,0:T(8,128)(2,1)S(1)}, u32[]{:S(2)}, u32[]{:S(2)}) collective-permute-start(bf16[64,4224]{1,0:T(8,128)(2,1)S(1)} %pad_maximum_fusion), channel_id=1, source_target_pairs={{0,4},{8,9},{16,20},{24,25},{32,36},{40,41},{48,52},{56,57},{4,64}... | collective-permute-start | bytes 1622024 | tf_op jit(solution)/shard_map/ppermute | solution.py:45
  72.5 15.2 %collective-permute-start.4 = (bf16[64,4224]{1,0:T(8,128)(2,1)S(1)}, bf16[64,4224]{1,0:T(8,128)(2,1)S(1)}, u32[]{:S(2)}, u32[]{:S(2)}) collective-permute-start(bf16[64,4224]{1,0:T(8,128)(2,1)S(1)} %pad_maximum_fusion), channel_id=1, source_target_pairs={{0,68},{8,11},{16,84},{24,27},{32,100},{40,43},{48,116},{56,59},{4... | collective-permute-start | bytes 1622024 | tf_op jit(solution)/shard_map/ppermute | solution.py:45
  75.2 21.6 %collective-permute-start.5 = (bf16[64,4224]{1,0:T(8,128)(2,1)S(1)}, bf16[64,4224]{1,0:T(8,128)(2,1)S(1)}, u32[]{:S(2)}, u32[]{:S(2)}) collective-permute-start(bf16[64,4224]{1,0:T(8,128)(2,1)S(1)} %pad_maximum_fusion), channel_id=1, source_target_pairs={{0,64},{8,10},{16,80},{24,26},{32,96},{40,42},{48,112},{56,58},{4,... | collective-permute-start | bytes 1622024 | tf_op jit(solution)/shard_map/ppermute | solution.py:45
  96.9 26.8 %collective-permute-start.16 = (bf16[256,4224]{1,0:T(8,128)(2,1)S(1)}, bf16[256,4224]{1,0:T(8,128)(2,1)S(1)}, u32[]{:S(2)}, u32[]{:S(2)}) collective-permute-start(bf16[256,4224]{1,0:T(8,128)(2,1)S(1)} %constant_dynamic-update-slice_fusion.refs_0_.refs_1_), channel_id=1, source_target_pairs={{0,48},{8,76},{16,0},{24,92},{32,16},{40,108},{48,32},{56,124},{4,... | collective-permute-start | bytes 6488072 | tf_op jit(solution)/shard_map/ppermute | solution.py:45
  97.3 27.9 %collective-permute-start.15 = (bf16[256,4224]{1,0:T(8,128)(2,1)S(1)}, bf16[256,4224]{1,0:T(8,128)(2,1)S(1)}, u32[]{:S(2)}, u32[]{:S(2)}) collective-permute-start(bf16[256,4224]{1,0:T(8,128)(2,1)S(1)} %constant_dynamic-update-slice_fusion.refs_0_.refs_1_), channel_id=1, source_target_pairs={{0,16},{8,12},{16,32},{24,28},{32,48},{40,44},{48,0},{56,60},{4,20... | collective-permute-start | bytes 6488072 | tf_op jit(solution)/shard_map/ppermute | solution.py:45
  109.9 19.8 %collective-permute-start.17 = (bf16[2,80,4096]{2,1,0:T(8,128)(2,1)S(1)}, bf16[2,80,4096]{2,1,0:T(8,128)(2,1)S(1)}, u32[]{:S(2)}, u32[]{:S(2)}) collective-permute-start(bf16[2,80,4096]{2,1,0:T(8,128)(2,1)S(1)} %get-tuple-element.73), channel_id=1, source_target_pairs={{0,8},{8,0},{1,9},{9,1},{2,10},{10,2},{3,11},{11,3},{4,12},{12,4},... | collective-permute-start | bytes 3932168 | tf_op jit(solution)/shard_map/ppermute | solution.py:49
  129.6 15.2 %collective-permute-start.22 = (bf16[128,4224]{1,0:T(8,128)(2,1)S(1)}, bf16[128,4224]{1,0:T(8,128)(2,1)S(1)}, u32[]{:S(2)}, u32[]{:S(2)}) collective-permute-start(bf16[128,4224]{1,0:T(8,128)(2,1)S(1)} %slice.67), channel_id=1, source_target_pairs={{0,48},{8,76},{16,0},{24,92},{32,16},{40,108},{48,32},{56,124},{4,... | collective-permute-start | bytes 3244040 | tf_op jit(solution)/shard_map/ppermute | solution.py:45
  129.8 16.4 %collective-permute-start.18 = (bf16[128,4224]{1,0:T(8,128)(2,1)S(1)}, bf16[128,4224]{1,0:T(8,128)(2,1)S(1)}, u32[]{:S(2)}, u32[]{:S(2)}) collective-permute-start(bf16[128,4224]{1,0:T(8,128)(2,1)S(1)} %slice.66), channel_id=1, source_target_pairs={{0,16},{8,12},{16,32},{24,28},{32,48},{40,44},{48,0},{56,60},{4,20... | collective-permute-start | bytes 3244040 | tf_op jit(solution)/shard_map/ppermute | solution.py:45
  142.1 22.0 %collective-permute-start.31 = (bf16[2,160,4096]{2,1,0:T(8,128)(2,1)S(1)}, bf16[2,160,4096]{2,1,0:T(8,128)(2,1)S(1)}, u32[]{:S(2)}, u32[]{:S(2)}) collective-permute-start(bf16[2,160,4096]{2,1,0:T(8,128)(2,1)S(1)} %get-tuple-element.96), channel_id=1, source_target_pairs={{0,8},{8,0},{1,9},{9,1},{2,10},{10,2},{3,11},{11,3},{4,12},{12,4},... | collective-permute-start | bytes 7864328 | tf_op jit(solution)/shard_map/ppermute | solution.py:49
  148.6 8.4 %collective-permute-start.29 = (bf16[2,48,4096]{2,1,0:T(8,128)(2,1)S(1)}, bf16[2,48,4096]{2,1,0:T(8,128)(2,1)S(1)}, u32[]{:S(2)}, u32[]{:S(2)}) collective-permute-start(bf16[2,48,4096]{2,1,0:T(8,128)(2,1)S(1)} %get-tuple-element.92), channel_id=1, source_target_pairs={{0,8},{8,0},{1,9},{9,1},{2,10},{10,2},{3,11},{11,3},{4,12},{12,4},... | collective-permute-start | bytes 2359304 | tf_op jit(solution)/shard_map/ppermute | solution.py:49
  152.3 16.1 %collective-permute-start.23 = (bf16[128,4096]{1,0:T(8,128)(2,1)S(1)}, bf16[128,4096]{1,0:T(8,128)(2,1)S(1)}, u32[]{:S(2)}, u32[]{:S(2)}) collective-permute-start(bf16[128,4096]{1,0:T(8,128)(2,1)S(1)} %slice.68), channel_id=1, source_target_pairs={{0,16},{8,12},{16,32},{24,28},{32,48},{40,44},{48,0},{56,60},{4,20... | collective-permute-start | bytes 3145736 | tf_op jit(solution)/shard_map/ppermute | solution.py:45
  153.7 15.6 %collective-permute-start.24 = (bf16[128,4096]{1,0:T(8,128)(2,1)S(1)}, bf16[128,4096]{1,0:T(8,128)(2,1)S(1)}, u32[]{:S(2)}, u32[]{:S(2)}) collective-permute-start(bf16[128,4096]{1,0:T(8,128)(2,1)S(1)} %slice.69), channel_id=1, source_target_pairs={{0,48},{8,76},{16,0},{24,92},{32,16},{40,108},{48,32},{56,124},{4,... | collective-permute-start | bytes 3145736 | tf_op jit(solution)/shard_map/ppermute | solution.py:45
  171.8 27.8 %collective-permute-start.36 = (bf16[256,4096]{1,0:T(8,128)(2,1)S(1)}, bf16[256,4096]{1,0:T(8,128)(2,1)S(1)}, u32[]{:S(2)}, u32[]{:S(2)}) collective-permute-start(bf16[256,4096]{1,0:T(8,128)(2,1)S(1)} %get-tuple-element.104), channel_id=1, source_target_pairs={{0,16},{8,12},{16,32},{24,28},{32,48},{40,44},{48,0},{56,60},{4,20... | collective-permute-start | bytes 6291464 | tf_op jit(solution)/shard_map/ppermute | solution.py:45
  171.9 28.0 %collective-permute-start.34 = (bf16[256,4096]{1,0:T(8,128)(2,1)S(1)}, bf16[256,4096]{1,0:T(8,128)(2,1)}, u32[]{:S(2)}, u32[]{:S(2)}) collective-permute-start(bf16[256,4096]{1,0:T(8,128)(2,1)S(1)} %get-tuple-element.103), channel_id=1, source_target_pairs={{0,48},{8,76},{16,0},{24,92},{32,16},{40,108},{48,32},{56,124},{4,... | collective-permute-start | bytes 6291464 | tf_op jit(solution)/shard_map/ppermute | solution.py:45
  184.2 18.4 %collective-permute-start.25 = (bf16[2,80,4096]{2,1,0:T(8,128)(2,1)}, bf16[2,80,4096]{2,1,0:T(8,128)(2,1)S(1)}, u32[]{:S(2)}, u32[]{:S(2)}) collective-permute-start(bf16[2,80,4096]{2,1,0:T(8,128)(2,1)} %get-tuple-element.86), channel_id=1, source_target_pairs={{0,8},{8,0},{1,9},{9,1},{2,10},{10,2},{3,11},{11,3},{4,12},{12,4},... | collective-permute-start | bytes 3932168 | tf_op jit(solution)/shard_map/ppermute | solution.py:49
  184.2 20.5 %collective-permute-start.26 = (bf16[2,80,4096]{2,1,0:T(8,128)(2,1)}, bf16[2,80,4096]{2,1,0:T(8,128)(2,1)S(1)}, u32[]{:S(2)}, u32[]{:S(2)}) collective-permute-start(bf16[2,80,4096]{2,1,0:T(8,128)(2,1)} %get-tuple-element.87), channel_id=1, source_target_pairs={{0,8},{8,0},{1,9},{9,1},{2,10},{10,2},{3,11},{11,3},{4,12},{12,4},... | collective-permute-start | bytes 3932168 | tf_op jit(solution)/shard_map/ppermute | solution.py:49
  184.7 20.0 %collective-permute-start.27 = (bf16[2,80,4096]{2,1,0:T(8,128)(2,1)}, bf16[2,80,4096]{2,1,0:T(8,128)(2,1)S(1)}, u32[]{:S(2)}, u32[]{:S(2)}) collective-permute-start(bf16[2,80,4096]{2,1,0:T(8,128)(2,1)} %get-tuple-element.88), channel_id=1, source_target_pairs={{0,8},{8,0},{1,9},{9,1},{2,10},{10,2},{3,11},{11,3},{4,12},{12,4},... | collective-permute-start | bytes 3932168 | tf_op jit(solution)/shard_map/ppermute | solution.py:49
  199.8 16.1 %collective-permute-start.38 = (bf16[128,4096]{1,0:T(8,128)(2,1)S(1)}, bf16[128,4096]{1,0:T(8,128)(2,1)S(1)}, u32[]{:S(2)}, u32[]{:S(2)}) collective-permute-start(bf16[128,4096]{1,0:T(8,128)(2,1)S(1)} %add_convert_fusion.1), channel_id=1, source_target_pairs={{0,16},{8,12},{16,32},{24,28},{32,48},{40,44},{48,0},{56,60},{4,20... | collective-permute-start | bytes 3145736 | tf_op jit(solution)/shard_map/ppermute | solution.py:45
  202.6 14.9 %collective-permute-start.35 = (bf16[128,4096]{1,0:T(8,128)(2,1)S(1)}, bf16[128,4096]{1,0:T(8,128)(2,1)S(1)}, u32[]{:S(2)}, u32[]{:S(2)}) collective-permute-start(bf16[128,4096]{1,0:T(8,128)(2,1)S(1)} %add_convert_fusion.3), channel_id=1, source_target_pairs={{0,48},{8,76},{16,0},{24,92},{32,16},{40,108},{48,32},{56,124},{4,... | collective-permute-start | bytes 3145736 | tf_op jit(solution)/shard_map/ppermute | solution.py:45
  220.1 16.1 %collective-permute-start.39 = (bf16[64,4096]{1,0:T(8,128)(2,1)S(1)}, bf16[64,4096]{1,0:T(8,128)(2,1)S(1)}, u32[]{:S(2)}, u32[]{:S(2)}) collective-permute-start(bf16[64,4096]{1,0:T(8,128)(2,1)S(1)} %get-tuple-element.118), channel_id=1, source_target_pairs={{0,4},{8,9},{16,20},{24,25},{32,36},{40,41},{48,52},{56,57},{4,64}... | collective-permute-start | bytes 1572872 | tf_op jit(solution)/shard_map/ppermute | solution.py:45
  220.2 16.0 %collective-permute-start.40 = (bf16[64,4096]{1,0:T(8,128)(2,1)S(1)}, bf16[64,4096]{1,0:T(8,128)(2,1)S(1)}, u32[]{:S(2)}, u32[]{:S(2)}) collective-permute-start(bf16[64,4096]{1,0:T(8,128)(2,1)S(1)} %get-tuple-element.119), channel_id=1, source_target_pairs={{0,64},{8,10},{16,80},{24,26},{32,96},{40,42},{48,112},{56,58},{4,... | collective-permute-start | bytes 1572872 | tf_op jit(solution)/shard_map/ppermute | solution.py:45
  223.2 14.0 %collective-permute-start.37 = (bf16[64,4096]{1,0:T(8,128)(2,1)S(1)}, bf16[64,4096]{1,0:T(8,128)(2,1)S(1)}, u32[]{:S(2)}, u32[]{:S(2)}) collective-permute-start(bf16[64,4096]{1,0:T(8,128)(2,1)S(1)} %slice.87), channel_id=1, source_target_pairs={{0,68},{8,11},{16,84},{24,27},{32,100},{40,43},{48,116},{56,59},{4... | collective-permute-start | bytes 1572872 | tf_op jit(solution)/shard_map/ppermute | solution.py:45
  237.4 9.1 %collective-permute-start.41 = (bf16[16,4096]{1,0:T(8,128)(2,1)S(1)}, bf16[16,4096]{1,0:T(8,128)(2,1)S(1)}, u32[]{:S(2)}, u32[]{:S(2)}) collective-permute-start(bf16[16,4096]{1,0:T(8,128)(2,1)S(1)} %get-tuple-element.120), channel_id=1, source_target_pairs={{0,3},{8,56},{16,19},{24,8},{32,35},{40,24},{48,51},{56,40},{4,7},... | collective-permute-start | bytes 393224 | tf_op jit(solution)/shard_map/ppermute | solution.py:45
  238.6 7.9 %collective-permute-start.42 = (bf16[16,4096]{1,0:T(8,128)(2,1)S(1)}, bf16[16,4096]{1,0:T(8,128)(2,1)S(1)}, u32[]{:S(2)}, u32[]{:S(2)}) collective-permute-start(bf16[16,4096]{1,0:T(8,128)(2,1)S(1)} %get-tuple-element.122), channel_id=1, source_target_pairs={{0,1},{8,24},{16,17},{24,40},{32,33},{40,56},{48,49},{56,8},{4,5},... | collective-permute-start | bytes 393224 | tf_op jit(solution)/shard_map/ppermute | solution.py:45
  239.5 7.0 %collective-permute-start.43 = (bf16[16,4096]{1,0:T(8,128)(2,1)S(1)}, bf16[16,4096]{1,0:T(8,128)(2,1)S(1)}, u32[]{:S(2)}, u32[]{:S(2)}) collective-permute-start(bf16[16,4096]{1,0:T(8,128)(2,1)S(1)} %get-tuple-element.121), channel_id=1, source_target_pairs={{0,2},{8,40},{16,18},{24,56},{32,34},{40,8},{48,50},{56,24},{4,6},... | collective-permute-start | bytes 393224 | tf_op jit(solution)/shard_map/ppermute | solution.py:45
  (41 other events, 311.4 us)

commit v4 on v3

--- a/solution.py
+++ b/solution.py
@@ -631,40 +631,28 @@
     back2 = swap_cores(back2)
 
     dims = stage_dims(2)
-    left_a, minus, plus, right_b = merge(
-        place1,
-        weight1,
-        after(out1, out2),
-        back1,
-        [(half, half, 0), (half, 2 * half, 1), (half, 2 * half, 0), (half, half, 0)],
-        narrow,
-    )
-    minus, plus = merge(
-        place2,
-        weight2,
-        after(out2, left_a, *cot_far),
-        back2,
-        [(half, 2 * half, 0), (half, 2 * half, 1)],
-        narrow,
-        (minus, plus),
-    )
-    got_minus, got_plus = send(minus, dims, -1), send(plus, dims, 1)
+    left_a, left_b, right_a, right_b = merge(
+        place1, weight1, after(out1, out2), back1, [(half, half, 0)] * 4, narrow
+    )
+    out2 = after(out2, left_a, *cot_far)
+    far_a, far_b = merge(place2, weight2, out2, back2, [(half, half, 0)] * 2, narrow)
+    got_far_a, got_far_b = send(far_a, dims, -1), send(far_b, dims, 1)
+    got_left_b, got_right_a = send(left_b, dims, -1), send(right_a, dims, 1)
 
     cot_tiles = [[cot_near], [cot_left], [cot_right], list(cot_far)]
     places, weights = (place0, place1, place2), (weight0, weight1, weight2)
     grads_own, grads_other = pack_grads(places, weights, cot_tiles, chunk)
-    grads = [grads_own] + swap_cores(grads_other)
+    grads = [grads_own] + swap_cores(after_all(grads_other, got_left_b, got_right_a))
     hiddens = [hidden0, hidden1, hidden2]
 
-    left_a = add(left_a, got_minus[:half]).astype(jnp.bfloat16)
-    right_b = add(right_b, got_plus[half:]).astype(jnp.bfloat16)
+    left_a = add(left_a, got_far_a).astype(jnp.bfloat16)
+    right_b = add(right_b, got_far_b).astype(jnp.bfloat16)
     got_left_a, got_right_b = send(left_a, dims, -1), send(right_b, dims, 1)
     back = back_act(grads, w_down, wide)
-    sum0 = after(sum0, back)
     total = jnp.concatenate(
         [
-            add(sum0[:half], got_left_a, got_plus[:half]),
-            add(sum0[half:], got_minus[half:], got_right_b),
+            add(sum0[:half], got_left_a, got_right_a),
+            add(sum0[half:], got_left_b, got_right_b),
         ],
         0,
     )

time: 249 us -> 245 us (0.984)
  waiting for transfers between devices: 95.8 us -> 91.5 us
    ppermute x30 -> x32, starting transfers between devices: 40.9 us -> 47.7 us  [send(): return lax.ppermute(array, AXES, shifted(dims, step))]
    ppermute x14, starting transfers between devices: 8.44 us -> 2.79 us  [swap_cores(): return [lax.ppermute(array, 'k', [(0, 1), (1, 0)]) for array in arrays]]
    ppermute x30 -> x32, waiting for transfers between devices: 76.3 us -> 73 us  [send(): return lax.ppermute(array, AXES, shifted(dims, step))]
    unnamed x64 -> x72, local copies, waits for them, and re-layouts: 4.69 us -> 5.89 us
  transfers between devices with their start and end apart: 46 -> 48, of which waited for: 24 -> 21; matrix products, arithmetic and copies ran while one was open for 4% -> 5% of each run, Pallas kernels for 28% -> 28%
where the time goes in v4:
time: 245 us; the launch traced here: 244 us
  waiting for transfers between devices  91.5 us (37%)
  Pallas kernels  70.9 us (29%)
  starting transfers between devices  63.3 us (26%)
  local copies, waits for them, and re-layouts  11.7 us (5%)
  other arithmetic  5.42 us (2%)
    ppermute x32, waiting for transfers between devices, send(): return lax.ppermute(array, AXES, shifted(dims, step))  73 us
    pallas_call x11, Pallas kernels, call(): pl.pallas_call(kernel, grid=grid, in_specs=in_specs, out_specs=out_specs,...  62.1 us
    ppermute x32, starting transfers between devices, send(): return lax.ppermute(array, AXES, shifted(dims, step))  47.7 us
    pallas_call x3, Pallas kernels, merge(): pl.pallas_call(kernel, grid=(width // chunk,), in_specs=[pl.BlockSpec(pla...  8.84 us
    all_to_all x1, starting transfers between devices, shards(): lax.all_to_all(jnp.broadcast_to(pair, (16,) + pair.shape), ('yh', 'z', 'k...  8.13 us
    all_to_all x1, waiting for transfers between devices, shards(): lax.all_to_all(mixed, ('yl', 'x'), 0, 0, tiled=True).reshape(8, ROWS, width)  7.89 us
    all_to_all x1, waiting for transfers between devices, shards(): lax.all_to_all(jnp.broadcast_to(pair, (16,) + pair.shape), ('yh', 'z', 'k...  7.61 us
    unnamed x72, local copies, waits for them, and re-layouts  5.89 us
  transfers between devices with their start and end apart: 48, of which 21 were waited for; matrix products, arithmetic and copies ran while one was open for 5% of the time, Pallas kernels for 28%

profile of v4, /device:TPU:0, one launch (start us, length us, event | category | flops | bytes accessed | tf_op | source)
XLA Modules:
  0.0 244.1 jit_solution(3098074084453149412)
XLA Ops:
  2.6 8.1 %all-to-all-start = ((bf16[16,128,256]{2,1,0:T(8,128)(2,1)}), bf16[16,128,256]{2,1,0:T(8,128)(2,1)S(1)}, u32[]{:S(2)}, u32[]{:S(2)}) async-start(bf16[16,128,256]{2,1,0:T(8,128)(2,1)} %broadcast_in_dim.8), calls=%async_computation | async-start | bytes 2097152 | tf_op jit(solution)/shard_map/all_to_all | solution.py:572
  10.7 3.1 %collective-permute-start.8 = (bf16[16,4096]{1,0:T(8,128)(2,1)S(1)}, bf16[16,4096]{1,0:T(8,128)(2,1)S(1)}, u32[]{:S(2)}, u32[]{:S(2)}) collective-permute-start(bf16[16,4096]{1,0:T(8,128)(2,1)S(1)} %copy-done.28), channel_id=1, source_target_pairs={{0,2},{8,40},{16,18},{24,56},{32,34},{40,8},{48,50},{56,24},{4,6},... | collective-permute-start | bytes 393224 | tf_op jit(solution)/shard_map/ppermute | solution.py:45
  21.2 7.6 %all-to-all-done = bf16[16,128,256]{2,1,0:T(8,128)(2,1)S(1)} async-done(((bf16[16,128,256]{2,1,0:T(8,128)(2,1)}), bf16[16,128,256]{2,1,0:T(8,128)(2,1)S(1)}, u32[]{:S(2)}, u32[]{:S(2)}) %all-to-all-start) | async-done | bytes 1048608 | tf_op jit(solution)/shard_map/all_to_all | solution.py:572
  29.6 2.5 %collective-permute-start.10 = (bf16[64,4096]{1,0:T(8,128)(2,1)S(1)}, bf16[64,4096]{1,0:T(8,128)(2,1)}, u32[]{:S(2)}, u32[]{:S(2)}) collective-permute-start(bf16[64,4096]{1,0:T(8,128)(2,1)S(1)} %pad_maximum_fusion.1), channel_id=1, source_target_pairs={{0,68},{8,11},{16,84},{24,27},{32,100},{40,43},{48,116},{56,59},{4... | collective-permute-start | bytes 1572872 | tf_op jit(solution)/shard_map/ppermute | solution.py:45
  33.0 6.6 %shard_map.147 = bf16[128,4096]{1,0:T(8,128)(2,1)} custom-call(s32[1]{0:T(128)} %bitcast.base_ref, bf16[128,512]{1,0:T(8,128)(2,1)} %query_ref.1, bf16[2048,256]{1,0:T(8,128)(2,1)} %bitcast.4, bf16[512,4096]{1,0:T(8,128)(2,1)} %proj_ref.1), custom_call_target="tpu_custom_call" | custom-call | tf_op jit(solution)/shard_map/pallas_call | solution.py:139
  39.6 4.6 %all-to-all-start.1 = ((bf16[8,16,4096]{2,1,0:T(8,128)(2,1)}), bf16[8,16,4096]{2,1,0:T(8,128)(2,1)S(1)}, u32[]{:S(2)}, u32[]{:S(2)}) async-start(bf16[8,16,4096]{2,1,0:T(8,128)(2,1)} %bitcast.5), calls=%async_computation.1 | async-start | bytes 2097152 | tf_op jit(solution)/shard_map/all_to_all | solution.py:590
  49.4 3.2 %collective-permute-start.13 = (bf16[256,4096]{1,0:T(8,128)(2,1)}, bf16[256,4096]{1,0:T(8,128)(2,1)}, u32[]{:S(2)}, u32[]{:S(2)}) collective-permute-start(bf16[256,4096]{1,0:T(8,128)(2,1)} %constant_dynamic-update-slice_fusion.7.refs_6_), channel_id=1, source_target_pairs={{0,48},{8,76},{16,0},{24,92},{32,16},{40,108},{48,32},{56,124},{4,... | collective-permute-start | bytes 6291464 | tf_op jit(solution)/shard_map/ppermute | solution.py:45
  52.6 7.9 %all-to-all-done.1 = bf16[8,16,4096]{2,1,0:T(8,128)(2,1)S(1)} async-done(((bf16[8,16,4096]{2,1,0:T(8,128)(2,1)}), bf16[8,16,4096]{2,1,0:T(8,128)(2,1)S(1)}, u32[]{:S(2)}, u32[]{:S(2)}) %all-to-all-start.1) | async-done | bytes 1048608 | tf_op jit(solution)/shard_map/all_to_all | solution.py:590
  65.1 3.0 %collective-permute-done = bf16[16,4224]{1,0:T(8,128)(2,1)S(1)} collective-permute-done((bf16[16,4224]{1,0:T(8,128)(2,1)S(1)}, bf16[16,4224]{1,0:T(8,128)(2,1)S(1)}, u32[]{:S(2)}, u32[]{:S(2)}) %collective-permute-start) | collective-permute-done | bytes 135200 | tf_op jit(solution)/shard_map/ppermute | solution.py:45
  72.2 2.7 %collective-permute-start.4 = (bf16[64,4224]{1,0:T(8,128)(2,1)S(1)}, bf16[64,4224]{1,0:T(8,128)(2,1)S(1)}, u32[]{:S(2)}, u32[]{:S(2)}) collective-permute-start(bf16[64,4224]{1,0:T(8,128)(2,1)S(1)} %pad_maximum_fusion), channel_id=1, source_target_pairs={{0,68},{8,11},{16,84},{24,27},{32,100},{40,43},{48,116},{56,59},{4... | collective-permute-start | bytes 1622024 | tf_op jit(solution)/shard_map/ppermute | solution.py:45
  76.7 8.2 %collective-permute-done.3 = bf16[64,4224]{1,0:T(8,128)(2,1)S(1)} collective-permute-done((bf16[64,4224]{1,0:T(8,128)(2,1)S(1)}, bf16[64,4224]{1,0:T(8,128)(2,1)S(1)}, u32[]{:S(2)}, u32[]{:S(2)}) %collective-permute-start.3) | collective-permute-done | bytes 540704 | tf_op jit(solution)/shard_map/ppermute | solution.py:45
  87.5 10.0 %collective-permute-done.5 = bf16[64,4224]{1,0:T(8,128)(2,1)S(1)} collective-permute-done((bf16[64,4224]{1,0:T(8,128)(2,1)S(1)}, bf16[64,4224]{1,0:T(8,128)(2,1)S(1)}, u32[]{:S(2)}, u32[]{:S(2)}) %collective-permute-start.5) | collective-permute-done | bytes 540704 | tf_op jit(solution)/shard_map/ppermute | solution.py:45
  97.6 3.2 %collective-permute-start.16 = (bf16[256,4224]{1,0:T(8,128)(2,1)S(1)}, bf16[256,4224]{1,0:T(8,128)(2,1)S(1)}, u32[]{:S(2)}, u32[]{:S(2)}) collective-permute-start(bf16[256,4224]{1,0:T(8,128)(2,1)S(1)} %constant_dynamic-update-slice_fusion.refs_0_.refs_1_), channel_id=1, source_target_pairs={{0,48},{8,76},{16,0},{24,92},{32,16},{40,108},{48,32},{56,124},{4,... | collective-permute-start | bytes 6488072 | tf_op jit(solution)/shard_map/ppermute | solution.py:45
  103.2 3.0 %collective-permute-done.14.refs_0_.refs_3_ = bf16[2,80,4096]{2,1,0:T(8,128)(2,1)S(1)} collective-permute-done((bf16[2,80,4096]{2,1,0:T(8,128)(2,1)S(1)}, bf16[2,80,4096]{2,1,0:T(8,128)(2,1)S(1)}, u32[]{:S(2)}, u32[]{:S(2)}) %collective-permute-start.14) | collective-permute-done | bytes 1310752 | tf_op jit(solution)/shard_map/ppermute | solution.py:49
  106.2 5.6 %shard_map.149 = (bf16[2,80,4096]{2,1,0:T(8,128)(2,1)S(1)}, bf16[2,80,4096]{2,1,0:T(8,128)(2,1)S(1)}, f32[2,2,160,192]{3,2,1,0:T(8,128)S(1)}) custom-call(bf16[2,80,4096]{2,1,0:T(8,128)(2,1)S(1)} %get-tuple-element.67.own_ref.refs_0_, bf16[2,80,4096]{2,1,0:T(8,128)(2,1)S(1)} %collective-permute-done.14.refs_0_.refs_3_, bf16[2,192,4096]{2,1,0:T(8,128)(2,1)S(1)} %copy-done.1, ...), custom_call_target="tpu_custom_call" | custom-call | tf_op jit(solution)/shard_map/pallas_call | solution.py:139
  112.2 13.4 %collective-permute-done.15.refs_0_.refs_2_ = bf16[256,4224]{1,0:T(8,128)(2,1)S(1)} collective-permute-done((bf16[256,4224]{1,0:T(8,128)(2,1)S(1)}, bf16[256,4224]{1,0:T(8,128)(2,1)S(1)}, u32[]{:S(2)}, u32[]{:S(2)}) %collective-permute-start.15) | collective-permute-done | bytes 2162720 | tf_op jit(solution)/shard_map/ppermute | solution.py:45
  125.6 3.6 %shard_map.150 = (bf16[2,160,4096]{2,1,0:T(8,128)(2,1)S(1)}, bf16[2,48,4096]{2,1,0:T(8,128)(2,1)S(1)}, bf16[2,64,4096]{2,1,0:T(8,128)(2,1)S(1)}, bf16[2,48,4096]...) custom-call(s32[1]{0:T(128)} %bitcast.3.me_ref, ...), custom_call_target="tpu_custom_call" | custom-call | tf_op jit(solution)/shard_map/pallas_call | solution.py:139
  130.1 3.3 %collective-permute-start.22 = (bf16[128,4224]{1,0:T(8,128)(2,1)S(1)}, bf16[128,4224]{1,0:T(8,128)(2,1)S(1)}, u32[]{:S(2)}, u32[]{:S(2)}) collective-permute-start(bf16[128,4224]{1,0:T(8,128)(2,1)S(1)} %slice.56), channel_id=1, source_target_pairs={{0,48},{8,76},{16,0},{24,92},{32,16},{40,108},{48,32},{56,124},{4,... | collective-permute-start | bytes 3244040 | tf_op jit(solution)/shard_map/ppermute | solution.py:45
  135.9 8.4 %shard_map.152 = (bf16[2,160,4096]{2,1,0:T(8,128)(2,1)S(1)}, bf16[2,160,4096]{2,1,0:T(8,128)(2,1)}, f32[2,2,320,192]{3,2,1,0:T(8,128)S(1)}) custom-call(bf16[2,160,4096]{2,1,0:T(8,128)(2,1)S(1)} %get-tuple-element.80.own_ref.refs_1_, bf16[2,48,4096]{2,1,0:T(8,128)(2,1)S(1)} %collective-permute-done.18.refs_0_.refs_4_, ...), custom_call_target="tpu_custom_call" | custom-call | tf_op jit(solution)/shard_map/pallas_call | solution.py:139
  154.4 5.7 %shard_map.154 = (bf16[2,80,4096]{2,1,0:T(8,128)(2,1)S(1)}, bf16[2,48,4096]{2,1,0:T(8,128)(2,1)S(1)}, bf16[2,32,4096]{2,1,0:T(8,128)(2,1)S(1)}, f32[2,2,160,192]{3,2,1,0:T(8,128)S(1)}) custom-call(bf16[2,80,4096]{2,1,0:T(8,128)(2,1)S(1)} %get-tuple-element.84.own_ref.refs_2_, bf16[2,48,4096]{2,1,0:T(8,128)(2,1)S(1)} %collective-permute-done.23.refs_0_.refs_7_, ...), custom_call_target="tpu_custom_call" | custom-call | tf_op jit(solution)/shard_map/pallas_call | solution.py:139
  160.7 4.0 %shard_map.155 = (bf16[128,4096]{1,0:T(8,128)(2,1)S(1)}, bf16[128,4096]{1,0:T(8,128)(2,1)S(1)}, bf16[128,4096]{1,0:T(8,128)(2,1)S(1)}, bf16[128,4096]{1,0:T(8,128)(2,1)S(1)}) custom-call(bf16[2,320,256]{2,1,0:T(8,128)(2,1)S(1)} %get-tuple-element.77.place_ref.refs_1_, f32[2,320,128]{2,1,0:T(8,128)S(1)} %get-tuple-element.78.weight_ref.refs_4_, ...), custom_call_target="tpu_custom_call" | custom-call | tf_op jit(solution)/shard_map/pallas_call | solution.py:286
  170.8 3.1 %collective-permute-start.30 = (bf16[128,4096]{1,0:T(8,128)(2,1)S(1)}, bf16[128,4096]{1,0:T(8,128)(2,1)S(1)}, u32[]{:S(2)}, u32[]{:S(2)}) collective-permute-start(bf16[128,4096]{1,0:T(8,128)(2,1)S(1)} %get-tuple-element.98), channel_id=1, source_target_pairs={{0,48},{8,76},{16,0},{24,92},{32,16},{40,108},{48,32},{56,124},{4,... | collective-permute-start | bytes 3145736 | tf_op jit(solution)/shard_map/ppermute | solution.py:45
  177.2 9.0 %collective-permute-done.30 = bf16[128,4096]{1,0:T(8,128)(2,1)S(1)} collective-permute-done((bf16[128,4096]{1,0:T(8,128)(2,1)S(1)}, bf16[128,4096]{1,0:T(8,128)(2,1)S(1)}, u32[]{:S(2)}, u32[]{:S(2)}) %collective-permute-start.30) | collective-permute-done | bytes 1048608 | tf_op jit(solution)/shard_map/ppermute | solution.py:45
  186.6 3.8 %collective-permute-start.31 = (bf16[128,4096]{1,0:T(8,128)(2,1)S(1)}, bf16[128,4096]{1,0:T(8,128)(2,1)}, u32[]{:S(2)}, u32[]{:S(2)}) collective-permute-start(bf16[128,4096]{1,0:T(8,128)(2,1)S(1)} %add_convert_fusion.3), channel_id=1, source_target_pairs={{0,48},{8,76},{16,0},{24,92},{32,16},{40,108},{48,32},{56,124},{4,... | collective-permute-start | bytes 3145736 | tf_op jit(solution)/shard_map/ppermute | solution.py:45
  190.7 7.5 %shard_map.157 = (bf16[2,320,4096]{2,1,0:T(8,128)(2,1)S(1)}, bf16[2,80,4096]{2,1,0:T(8,128)(2,1)S(1)}, bf16[2,80,4096]{2,1,0:T(8,128)(2,1)S(1)}, bf16[2,80,4096]...) custom-call(bf16[1,320,256]{2,1,0:T(8,128)(2,1)S(1)} %get-tuple-element.65.place_ref.refs_0_, ...), custom_call_target="tpu_custom_call" | custom-call | flops 2684354560 | bytes 20185088 | tf_op jit(solution)/shard_map/pallas_call | solution.py:139
  198.2 3.0 %collective-permute-done.32 = bf16[128,4096]{1,0:T(8,128)(2,1)S(1)} collective-permute-done((bf16[128,4096]{1,0:T(8,128)(2,1)S(1)}, bf16[128,4096]{1,0:T(8,128)(2,1)S(1)}, u32[]{:S(2)}, u32[]{:S(2)}) %collective-permute-start.32) | collective-permute-done | bytes 1048608 | tf_op jit(solution)/shard_map/ppermute | solution.py:45
  201.7 7.0 %collective-permute-done.31 = bf16[128,4096]{1,0:T(8,128)(2,1)} collective-permute-done((bf16[128,4096]{1,0:T(8,128)(2,1)S(1)}, bf16[128,4096]{1,0:T(8,128)(2,1)}, u32[]{:S(2)}, u32[]{:S(2)}) %collective-permute-start.31) | collective-permute-done | bytes 1048608 | tf_op jit(solution)/shard_map/ppermute | solution.py:45
  208.7 3.8 %collective-permute-done.36 = bf16[128,4096]{1,0:T(8,128)(2,1)} collective-permute-done((bf16[128,4096]{1,0:T(8,128)(2,1)S(1)}, bf16[128,4096]{1,0:T(8,128)(2,1)}, u32[]{:S(2)}, u32[]{:S(2)}) %collective-permute-start.36) | collective-permute-done | bytes 1048608 | tf_op jit(solution)/shard_map/ppermute | solution.py:45
  212.5 2.7 %add_convert_fusion.2 = (bf16[128,4096]{1,0:T(8,128)(2,1)S(1)}, bf16[128,4096]{1,0:T(8,128)(2,1)S(1)}) fusion(bf16[128,4096]{1,0:T(8,128)(2,1)S(1)} %collective-permute-done.32, bf16[128,4096]{1,0:T(8,128)(2,1)} %collective-permute-done.31, bf16[256,4096]{1,0:T(8,128)(2,1)S(1)} %shard_map.151, bf16[128,4096]{1,0:T(8,128)(2,1)} %collective-permute-done.36, ...), kind=kLoop, calls=%fused_computation.2 | loop fusion | flops 6291456 | bytes 8388608 | tf_op jit(solution)/shard_map/convert
  219.4 4.7 %shard_map.158.back_ref = f32[2,640,192]{2,1,0:T(8,128)S(1)} custom-call(bf16[2,320,4096]{2,1,0:T(8,128)(2,1)S(1)} %get-tuple-element.117.refs_0_, bf16[2,80,4096]{2,1,0:T(8,128)(2,1)S(1)} %collective-permute-done.42.refs_1_, bf16[2,80,4096]{2,1,0:T(8,128)(2,1)S(1)} %collective-permute-done.43.refs_2_, ...), custom_call_target="tpu_custom_call" | custom-call | flops 2013265920 | bytes 14614528 | tf_op jit(solution)/shard_map/pallas_call | solution.py:139
  224.2 9.1 %shard_map.159 = (bf16[2,192,4096]{2,1,0:T(8,128)(2,1)}, bf16[2,192,4096]{2,1,0:T(8,128)(2,1)}) custom-call(f32[2,640,192]{2,1,0:T(8,128)S(1)} %shard_map.158.back_ref, bf16[2,80,4096]{2,1,0:T(8,128)(2,1)S(1)} %get-tuple-element.67.own_ref.refs_0_, bf16[2,160,4096]{2,1,0:T(8,128)(2,1)S(1)} %get-tuple-element.80.own_ref.refs_1_, ...), custom_call_target="tpu_custom_call" | custom-call | flops 4026531840 | bytes 19726336 | tf_op jit(solution)/shard_map/pallas_call | solution.py:139
  237.0 6.3 %shard_map.160 = bf16[2,192,4096]{2,1,0:T(8,128)(2,1)} custom-call(bf16[2,320,4096]{2,1,0:T(8,128)(2,1)S(1)} %get-tuple-element.117.refs_0_, bf16[2,80,4096]{2,1,0:T(8,128)(2,1)S(1)} %collective-permute-done.42.refs_1_, bf16[2,80,4096]{2,1,0:T(8,128)(2,1)S(1)} %collective-permute-done.43.refs_2_, bf16[2,80,4096]{2,1,0:T(8,128)(2,1)S(1)} %collective-permute-done.44.refs_3_, ...), custom_call_target="tpu_custom_call" | custom-call | flops 2013265920 | bytes 15597568 | tf_op jit(solution)/shard_map/pallas_call | solution.py:139
  (180 shorter events, 65.1 us)
Async XLA Ops:
  2.6 26.2 %all-to-all-start = ((bf16[16,128,256]{2,1,0:T(8,128)(2,1)}), bf16[16,128,256]{2,1,0:T(8,128)(2,1)S(1)}, u32[]{:S(2)}, u32[]{:S(2)}) async-start(bf16[16,128,256]{2,1,0:T(8,128)(2,1)} %broadcast_in_dim.8), calls=%async_computation | async-start | bytes 2097152 | tf_op jit(solution)/shard_map/all_to_all | solution.py:572
  28.8 16.0 %collective-permute-start.9 = (bf16[64,4096]{1,0:T(8,128)(2,1)S(1)}, bf16[64,4096]{1,0:T(8,128)(2,1)S(1)}, u32[]{:S(2)}, u32[]{:S(2)}) collective-permute-start(bf16[64,4096]{1,0:T(8,128)(2,1)S(1)} %pad_maximum_fusion.1), channel_id=1, source_target_pairs={{0,4},{8,9},{16,20},{24,25},{32,36},{40,41},{48,52},{56,57},{4,64}... | collective-permute-start | bytes 1572872 | tf_op jit(solution)/shard_map/ppermute | solution.py:45
  29.6 16.0 %collective-permute-start.10 = (bf16[64,4096]{1,0:T(8,128)(2,1)S(1)}, bf16[64,4096]{1,0:T(8,128)(2,1)}, u32[]{:S(2)}, u32[]{:S(2)}) collective-permute-start(bf16[64,4096]{1,0:T(8,128)(2,1)S(1)} %pad_maximum_fusion.1), channel_id=1, source_target_pairs={{0,68},{8,11},{16,84},{24,27},{32,100},{40,43},{48,116},{56,59},{4... | collective-permute-start | bytes 1572872 | tf_op jit(solution)/shard_map/ppermute | solution.py:45
  33.0 14.5 %collective-permute-start.11 = (bf16[64,4096]{1,0:T(8,128)(2,1)S(1)}, bf16[64,4096]{1,0:T(8,128)(2,1)}, u32[]{:S(2)}, u32[]{:S(2)}) collective-permute-start(bf16[64,4096]{1,0:T(8,128)(2,1)S(1)} %pad_maximum_fusion.1), channel_id=1, source_target_pairs={{0,64},{8,10},{16,80},{24,26},{32,96},{40,42},{48,112},{56,58},{4,... | collective-permute-start | bytes 1572872 | tf_op jit(solution)/shard_map/ppermute | solution.py:45
  39.6 21.0 %all-to-all-start.1 = ((bf16[8,16,4096]{2,1,0:T(8,128)(2,1)}), bf16[8,16,4096]{2,1,0:T(8,128)(2,1)S(1)}, u32[]{:S(2)}, u32[]{:S(2)}) async-start(bf16[8,16,4096]{2,1,0:T(8,128)(2,1)} %bitcast.5), calls=%async_computation.1 | async-start | bytes 2097152 | tf_op jit(solution)/shard_map/all_to_all | solution.py:590
  49.4 48.1 %collective-permute-start.12 = (bf16[256,4096]{1,0:T(8,128)(2,1)}, bf16[256,4096]{1,0:T(8,128)(2,1)S(1)}, u32[]{:S(2)}, u32[]{:S(2)}) collective-permute-start(bf16[256,4096]{1,0:T(8,128)(2,1)} %constant_dynamic-update-slice_fusion.7.refs_6_), channel_id=1, source_target_pairs={{0,16},{8,12},{16,32},{24,28},{32,48},{40,44},{48,0},{56,60},{4,20... | collective-permute-start | bytes 6291464 | tf_op jit(solution)/shard_map/ppermute | solution.py:45
  49.4 48.2 %collective-permute-start.13 = (bf16[256,4096]{1,0:T(8,128)(2,1)}, bf16[256,4096]{1,0:T(8,128)(2,1)}, u32[]{:S(2)}, u32[]{:S(2)}) collective-permute-start(bf16[256,4096]{1,0:T(8,128)(2,1)} %constant_dynamic-update-slice_fusion.7.refs_6_), channel_id=1, source_target_pairs={{0,48},{8,76},{16,0},{24,92},{32,16},{40,108},{48,32},{56,124},{4,... | collective-permute-start | bytes 6291464 | tf_op jit(solution)/shard_map/ppermute | solution.py:45
  71.6 13.3 %collective-permute-start.3 = (bf16[64,4224]{1,0:T(8,128)(2,1)S(1)}, bf16[64,4224]{1,0:T(8,128)(2,1)S(1)}, u32[]{:S(2)}, u32[]{:S(2)}) collective-permute-start(bf16[64,4224]{1,0:T(8,128)(2,1)S(1)} %pad_maximum_fusion), channel_id=1, source_target_pairs={{0,4},{8,9},{16,20},{24,25},{32,36},{40,41},{48,52},{56,57},{4,64}... | collective-permute-start | bytes 1622024 | tf_op jit(solution)/shard_map/ppermute | solution.py:45
  72.2 15.2 %collective-permute-start.4 = (bf16[64,4224]{1,0:T(8,128)(2,1)S(1)}, bf16[64,4224]{1,0:T(8,128)(2,1)S(1)}, u32[]{:S(2)}, u32[]{:S(2)}) collective-permute-start(bf16[64,4224]{1,0:T(8,128)(2,1)S(1)} %pad_maximum_fusion), channel_id=1, source_target_pairs={{0,68},{8,11},{16,84},{24,27},{32,100},{40,43},{48,116},{56,59},{4... | collective-permute-start | bytes 1622024 | tf_op jit(solution)/shard_map/ppermute | solution.py:45
  74.9 22.6 %collective-permute-start.5 = (bf16[64,4224]{1,0:T(8,128)(2,1)S(1)}, bf16[64,4224]{1,0:T(8,128)(2,1)S(1)}, u32[]{:S(2)}, u32[]{:S(2)}) collective-permute-start(bf16[64,4224]{1,0:T(8,128)(2,1)S(1)} %pad_maximum_fusion), channel_id=1, source_target_pairs={{0,64},{8,10},{16,80},{24,26},{32,96},{40,42},{48,112},{56,58},{4,... | collective-permute-start | bytes 1622024 | tf_op jit(solution)/shard_map/ppermute | solution.py:45
  97.6 28.0 %collective-permute-start.15 = (bf16[256,4224]{1,0:T(8,128)(2,1)S(1)}, bf16[256,4224]{1,0:T(8,128)(2,1)S(1)}, u32[]{:S(2)}, u32[]{:S(2)}) collective-permute-start(bf16[256,4224]{1,0:T(8,128)(2,1)S(1)} %constant_dynamic-update-slice_fusion.refs_0_.refs_1_), channel_id=1, source_target_pairs={{0,16},{8,12},{16,32},{24,28},{32,48},{40,44},{48,0},{56,60},{4,20... | collective-permute-start | bytes 6488072 | tf_op jit(solution)/shard_map/ppermute | solution.py:45
  97.6 27.9 %collective-permute-start.16 = (bf16[256,4224]{1,0:T(8,128)(2,1)S(1)}, bf16[256,4224]{1,0:T(8,128)(2,1)S(1)}, u32[]{:S(2)}, u32[]{:S(2)}) collective-permute-start(bf16[256,4224]{1,0:T(8,128)(2,1)S(1)} %constant_dynamic-update-slice_fusion.refs_0_.refs_1_), channel_id=1, source_target_pairs={{0,48},{8,76},{16,0},{24,92},{32,16},{40,108},{48,32},{56,124},{4,... | collective-permute-start | bytes 6488072 | tf_op jit(solution)/shard_map/ppermute | solution.py:45
  111.8 18.3 %collective-permute-start.17 = (bf16[2,80,4096]{2,1,0:T(8,128)(2,1)S(1)}, bf16[2,80,4096]{2,1,0:T(8,128)(2,1)S(1)}, u32[]{:S(2)}, u32[]{:S(2)}) collective-permute-start(bf16[2,80,4096]{2,1,0:T(8,128)(2,1)S(1)} %get-tuple-element.76), channel_id=1, source_target_pairs={{0,8},{8,0},{1,9},{9,1},{2,10},{10,2},{3,11},{11,3},{4,12},{12,4},... | collective-permute-start | bytes 3932168 | tf_op jit(solution)/shard_map/ppermute | solution.py:49
  129.9 16.4 %collective-permute-start.21 = (bf16[128,4224]{1,0:T(8,128)(2,1)S(1)}, bf16[128,4224]{1,0:T(8,128)(2,1)S(1)}, u32[]{:S(2)}, u32[]{:S(2)}) collective-permute-start(bf16[128,4224]{1,0:T(8,128)(2,1)S(1)} %slice.55), channel_id=1, source_target_pairs={{0,16},{8,12},{16,32},{24,28},{32,48},{40,44},{48,0},{56,60},{4,20... | collective-permute-start | bytes 3244040 | tf_op jit(solution)/shard_map/ppermute | solution.py:45
  130.1 16.3 %collective-permute-start.22 = (bf16[128,4224]{1,0:T(8,128)(2,1)S(1)}, bf16[128,4224]{1,0:T(8,128)(2,1)S(1)}, u32[]{:S(2)}, u32[]{:S(2)}) collective-permute-start(bf16[128,4224]{1,0:T(8,128)(2,1)S(1)} %slice.56), channel_id=1, source_target_pairs={{0,48},{8,76},{16,0},{24,92},{32,16},{40,108},{48,32},{56,124},{4,... | collective-permute-start | bytes 3244040 | tf_op jit(solution)/shard_map/ppermute | solution.py:45
  144.3 16.4 %collective-permute-start.25 = (bf16[2,160,4096]{2,1,0:T(8,128)(2,1)}, bf16[2,160,4096]{2,1,0:T(8,128)(2,1)S(1)}, u32[]{:S(2)}, u32[]{:S(2)}) collective-permute-start(bf16[2,160,4096]{2,1,0:T(8,128)(2,1)} %get-tuple-element.89), channel_id=1, source_target_pairs={{0,8},{8,0},{1,9},{9,1},{2,10},{10,2},{3,11},{11,3},{4,12},{12,4},... | collective-permute-start | bytes 7864328 | tf_op jit(solution)/shard_map/ppermute | solution.py:49
  149.5 16.2 %collective-permute-start.26 = (bf16[128,4096]{1,0:T(8,128)(2,1)S(1)}, bf16[128,4096]{1,0:T(8,128)(2,1)S(1)}, u32[]{:S(2)}, u32[]{:S(2)}) collective-permute-start(bf16[128,4096]{1,0:T(8,128)(2,1)S(1)} %slice.57), channel_id=1, source_target_pairs={{0,16},{8,12},{16,32},{24,28},{32,48},{40,44},{48,0},{56,60},{4,20... | collective-permute-start | bytes 3145736 | tf_op jit(solution)/shard_map/ppermute | solution.py:45
  152.5 14.9 %collective-permute-start.27 = (bf16[128,4096]{1,0:T(8,128)(2,1)S(1)}, bf16[128,4096]{1,0:T(8,128)(2,1)S(1)}, u32[]{:S(2)}, u32[]{:S(2)}) collective-permute-start(bf16[128,4096]{1,0:T(8,128)(2,1)S(1)} %slice.58), channel_id=1, source_target_pairs={{0,48},{8,76},{16,0},{24,92},{32,16},{40,108},{48,32},{56,124},{4,... | collective-permute-start | bytes 3145736 | tf_op jit(solution)/shard_map/ppermute | solution.py:45
  170.8 15.4 %collective-permute-start.30 = (bf16[128,4096]{1,0:T(8,128)(2,1)S(1)}, bf16[128,4096]{1,0:T(8,128)(2,1)S(1)}, u32[]{:S(2)}, u32[]{:S(2)}) collective-permute-start(bf16[128,4096]{1,0:T(8,128)(2,1)S(1)} %get-tuple-element.98), channel_id=1, source_target_pairs={{0,48},{8,76},{16,0},{24,92},{32,16},{40,108},{48,32},{56,124},{4,... | collective-permute-start | bytes 3145736 | tf_op jit(solution)/shard_map/ppermute | solution.py:45
  173.9 16.4 %collective-permute-start.35 = (bf16[128,4096]{1,0:T(8,128)(2,1)S(1)}, bf16[128,4096]{1,0:T(8,128)(2,1)S(1)}, u32[]{:S(2)}, u32[]{:S(2)}) collective-permute-start(bf16[128,4096]{1,0:T(8,128)(2,1)S(1)} %get-tuple-element.102), channel_id=1, source_target_pairs={{0,16},{8,12},{16,32},{24,28},{32,48},{40,44},{48,0},{56,60},{4,20... | collective-permute-start | bytes 3145736 | tf_op jit(solution)/shard_map/ppermute | solution.py:45
  173.9 27.2 %collective-permute-start.32 = (bf16[128,4096]{1,0:T(8,128)(2,1)S(1)}, bf16[128,4096]{1,0:T(8,128)(2,1)S(1)}, u32[]{:S(2)}, u32[]{:S(2)}) collective-permute-start(bf16[128,4096]{1,0:T(8,128)(2,1)S(1)} %get-tuple-element.99), channel_id=1, source_target_pairs={{0,16},{8,12},{16,32},{24,28},{32,48},{40,44},{48,0},{56,60},{4,20... | collective-permute-start | bytes 3145736 | tf_op jit(solution)/shard_map/ppermute | solution.py:45
  174.9 26.2 %collective-permute-start.34 = (bf16[128,4096]{1,0:T(8,128)(2,1)S(1)}, bf16[128,4096]{1,0:T(8,128)(2,1)S(1)}, u32[]{:S(2)}, u32[]{:S(2)}) collective-permute-start(bf16[128,4096]{1,0:T(8,128)(2,1)S(1)} %get-tuple-element.100), channel_id=1, source_target_pairs={{0,48},{8,76},{16,0},{24,92},{32,16},{40,108},{48,32},{56,124},{4,... | collective-permute-start | bytes 3145736 | tf_op jit(solution)/shard_map/ppermute | solution.py:45
  186.6 22.2 %collective-permute-start.31 = (bf16[128,4096]{1,0:T(8,128)(2,1)S(1)}, bf16[128,4096]{1,0:T(8,128)(2,1)}, u32[]{:S(2)}, u32[]{:S(2)}) collective-permute-start(bf16[128,4096]{1,0:T(8,128)(2,1)S(1)} %add_convert_fusion.3), channel_id=1, source_target_pairs={{0,48},{8,76},{16,0},{24,92},{32,16},{40,108},{48,32},{56,124},{4,... | collective-permute-start | bytes 3145736 | tf_op jit(solution)/shard_map/ppermute | solution.py:45
  190.6 22.0 %collective-permute-start.36 = (bf16[128,4096]{1,0:T(8,128)(2,1)S(1)}, bf16[128,4096]{1,0:T(8,128)(2,1)}, u32[]{:S(2)}, u32[]{:S(2)}) collective-permute-start(bf16[128,4096]{1,0:T(8,128)(2,1)S(1)} %add_convert_fusion.1), channel_id=1, source_target_pairs={{0,16},{8,12},{16,32},{24,28},{32,48},{40,44},{48,0},{56,60},{4,20... | collective-permute-start | bytes 3145736 | tf_op jit(solution)/shard_map/ppermute | solution.py:45
  201.2 14.8 %collective-permute-start.42 = (bf16[2,80,4096]{2,1,0:T(8,128)(2,1)S(1)}, bf16[2,80,4096]{2,1,0:T(8,128)(2,1)S(1)}, u32[]{:S(2)}, u32[]{:S(2)}) collective-permute-start(bf16[2,80,4096]{2,1,0:T(8,128)(2,1)S(1)} %get-tuple-element.105), channel_id=1, source_target_pairs={{0,8},{8,0},{1,9},{9,1},{2,10},{10,2},{3,11},{11,3},{4,12},{12,4},... | collective-permute-start | bytes 3932168 | tf_op jit(solution)/shard_map/ppermute | solution.py:49
  201.2 17.0 %collective-permute-start.43 = (bf16[2,80,4096]{2,1,0:T(8,128)(2,1)S(1)}, bf16[2,80,4096]{2,1,0:T(8,128)(2,1)S(1)}, u32[]{:S(2)}, u32[]{:S(2)}) collective-permute-start(bf16[2,80,4096]{2,1,0:T(8,128)(2,1)S(1)} %get-tuple-element.107), channel_id=1, source_target_pairs={{0,8},{8,0},{1,9},{9,1},{2,10},{10,2},{3,11},{11,3},{4,12},{12,4},... | collective-permute-start | bytes 3932168 | tf_op jit(solution)/shard_map/ppermute | solution.py:49
  201.7 17.6 %collective-permute-start.44 = (bf16[2,80,4096]{2,1,0:T(8,128)(2,1)S(1)}, bf16[2,80,4096]{2,1,0:T(8,128)(2,1)S(1)}, u32[]{:S(2)}, u32[]{:S(2)}) collective-permute-start(bf16[2,80,4096]{2,1,0:T(8,128)(2,1)S(1)} %get-tuple-element.109), channel_id=1, source_target_pairs={{0,8},{8,0},{1,9},{9,1},{2,10},{10,2},{3,11},{11,3},{4,12},{12,4},... | collective-permute-start | bytes 3932168 | tf_op jit(solution)/shard_map/ppermute | solution.py:49
  208.7 10.6 %collective-permute-start.45 = (bf16[2,80,4096]{2,1,0:T(8,128)(2,1)S(1)}, bf16[2,80,4096]{2,1,0:T(8,128)(2,1)S(1)}, u32[]{:S(2)}, u32[]{:S(2)}) collective-permute-start(bf16[2,80,4096]{2,1,0:T(8,128)(2,1)S(1)} %get-tuple-element.111), channel_id=1, source_target_pairs={{0,8},{8,0},{1,9},{9,1},{2,10},{10,2},{3,11},{11,3},{4,12},{12,4},... | collective-permute-start | bytes 3932168 | tf_op jit(solution)/shard_map/ppermute | solution.py:49
  215.3 18.0 %collective-permute-start.38 = (bf16[64,4096]{1,0:T(8,128)(2,1)S(1)}, bf16[64,4096]{1,0:T(8,128)(2,1)S(1)}, u32[]{:S(2)}, u32[]{:S(2)}) collective-permute-start(bf16[64,4096]{1,0:T(8,128)(2,1)S(1)} %get-tuple-element.125), channel_id=1, source_target_pairs={{0,64},{8,10},{16,80},{24,26},{32,96},{40,42},{48,112},{56,58},{4,... | collective-permute-start | bytes 1572872 | tf_op jit(solution)/shard_map/ppermute | solution.py:45
  216.0 17.3 %collective-permute-start.37 = (bf16[64,4096]{1,0:T(8,128)(2,1)S(1)}, bf16[64,4096]{1,0:T(8,128)(2,1)S(1)}, u32[]{:S(2)}, u32[]{:S(2)}) collective-permute-start(bf16[64,4096]{1,0:T(8,128)(2,1)S(1)} %get-tuple-element.124), channel_id=1, source_target_pairs={{0,4},{8,9},{16,20},{24,25},{32,36},{40,41},{48,52},{56,57},{4,64}... | collective-permute-start | bytes 1572872 | tf_op jit(solution)/shard_map/ppermute | solution.py:45
  218.2 15.1 %collective-permute-start.33 = (bf16[64,4096]{1,0:T(8,128)(2,1)S(1)}, bf16[64,4096]{1,0:T(8,128)(2,1)S(1)}, u32[]{:S(2)}, u32[]{:S(2)}) collective-permute-start(bf16[64,4096]{1,0:T(8,128)(2,1)S(1)} %slice.70), channel_id=1, source_target_pairs={{0,68},{8,11},{16,84},{24,27},{32,100},{40,43},{48,116},{56,59},{4... | collective-permute-start | bytes 1572872 | tf_op jit(solution)/shard_map/ppermute | solution.py:45
  233.6 9.7 %collective-permute-start.41 = (bf16[16,4096]{1,0:T(8,128)(2,1)S(1)}, bf16[16,4096]{1,0:T(8,128)(2,1)S(1)}, u32[]{:S(2)}, u32[]{:S(2)}) collective-permute-start(bf16[16,4096]{1,0:T(8,128)(2,1)S(1)} %get-tuple-element.127), channel_id=1, source_target_pairs={{0,2},{8,40},{16,18},{24,56},{32,34},{40,8},{48,50},{56,24},{4,6},... | collective-permute-start | bytes 393224 | tf_op jit(solution)/shard_map/ppermute | solution.py:45
  (47 other events, 393.3 us)

commit v5 on v4

--- a/solution.py
+++ b/solution.py
@@ -493,19 +493,18 @@
     )
 
 
-def attend(base, queries, pairs, out_proj):
+def attend(base, queries, blocks, positions, out_proj):
     rows, width = queries.shape[0], out_proj.shape[1]
-    tokens = pairs.shape[0]
+    tokens = positions.shape[1]
     steps = queries.shape[1] // (2 * HEAD)
 
-    def kernel(base_ref, query_ref, pairs_ref, proj_ref, out_ref, sum_ref):
+    def kernel(base_ref, query_ref, first_ref, second_ref, pos_ref, proj_ref, out_ref, sum_ref):
         both = query_ref[...]
         query = jnp.concatenate([both[:, :HEAD], both[:, HEAD:]], 0)
-        pairs = pairs_ref[...]
+        pairs = jnp.concatenate([first_ref[...], second_ref[...]], 0)
         scores = dot_t(query, pairs[:, :HEAD]) * (1.0 / math.sqrt(HEAD))
         query_pos = lax.broadcasted_iota(jnp.int32, (2 * rows, 1), 0) % rows + base_ref[0]
-        key_pos = lax.broadcasted_iota(jnp.int32, (1, tokens), 1)
-        scores = jnp.where(key_pos <= query_pos, scores, -1e30)
+        scores = jnp.where(pos_ref[...] <= query_pos, scores, -1e30)
         probs = jnp.exp(scores - jnp.max(scores, axis=1, keepdims=True))
         denom = jnp.sum(probs, axis=1, keepdims=True)
         heads = jnp.dot(
@@ -528,14 +527,17 @@
         def _():
             out_ref[...] = sum_ref[...].astype(jnp.bfloat16)
 
+    half = pl.BlockSpec((tokens // 2, 2 * HEAD), lambda h: (0, 0))
     return call(
         kernel,
         (steps,),
-        (base, queries, pairs, out_proj),
+        (base, queries, *blocks, positions, out_proj),
         [
             pl.BlockSpec(memory_space=pltpu.SMEM),
             pl.BlockSpec((rows, 2 * HEAD), lambda h: (0, h)),
-            pl.BlockSpec((tokens, 2 * HEAD), lambda h: (0, 0)),
+            half,
+            half,
+            pl.BlockSpec((1, tokens), lambda h: (0, 0)),
             pl.BlockSpec((2 * HEAD, width), lambda h: (h, 0)),
         ],
         [shape((rows, width))],
@@ -544,6 +546,12 @@
         [pltpu.VMEM((rows, width), jnp.float32)],
         limit=56,
     )[0]
+
+
+def key_positions(tok_ctx):
+    k = lax.axis_index("k")
+    groups = jnp.concatenate([2 * jnp.arange(8) + k, 2 * jnp.arange(8) + (1 - k)]).astype(jnp.int32)
+    return (groups[:, None] * tok_ctx + jnp.arange(tok_ctx, dtype=jnp.int32)[None, :]).reshape(1, -1)
 
 
 def shards(
@@ -570,8 +578,9 @@
     value_mine = lax.dynamic_slice_in_dim(values, yl * HEAD, HEAD, 1)
     pair = jnp.concatenate([key_mine, value_mine], 1)
     pairs = lax.all_to_all(
-        jnp.broadcast_to(pair, (16,) + pair.shape), ("yh", "z", "k"), 0, 0, tiled=True
-    ).reshape(16 * tok_ctx, 2 * HEAD)
+        jnp.broadcast_to(pair, (8,) + pair.shape), ("yh", "z"), 0, 0, tiled=True
+    ).reshape(8 * tok_ctx, 2 * HEAD)
+    blocks = [pairs] + swap_cores([pairs])
 
     rest = gates
     pieces = [expert_ids.astype(jnp.bfloat16)]
@@ -586,7 +595,7 @@
     cot_sides = gather_sides(cot_near)
 
     base = (ctx * tok_ctx).reshape(1)
-    mixed = attend(base, queries, pairs, out_proj)
+    mixed = attend(base, queries, blocks, key_positions(tok_ctx), out_proj)
     mixed = lax.all_to_all(mixed, ("yl", "x"), 0, 0, tiled=True).reshape(8, ROWS, width)
     stream = resid.astype(jnp.float32) + jnp.sum(mixed.astype(jnp.float32), axis=0)
     normed = (

time: 245 us -> 242 us (0.988)
  waiting for transfers between devices: 91.5 us -> 86 us
    ppermute x32, waiting for transfers between devices: 73 us -> 66.9 us  [send(): return lax.ppermute(array, AXES, shifted(dims, step))]
    unnamed x72 -> x70, local copies, waits for them, and re-layouts: 5.89 us -> 7.37 us
  transfers between devices with their start and end apart: 48 -> 49, of which waited for: 21 -> 17; matrix products, arithmetic and copies ran while one was open for 5% -> 7% of each run, Pallas kernels for 28% -> 28%
where the time goes in v5:
time: 242 us; the launch traced here: 241 us
  waiting for transfers between devices  86 us (36%)
  Pallas kernels  70.8 us (29%)
  starting transfers between devices  62.5 us (26%)
  local copies, waits for them, and re-layouts  12.9 us (5%)
  other arithmetic  7.76 us (3%)
    ppermute x32, waiting for transfers between devices, send(): return lax.ppermute(array, AXES, shifted(dims, step))  66.9 us
    pallas_call x11, Pallas kernels, call(): pl.pallas_call(kernel, grid=grid, in_specs=in_specs, out_specs=out_specs,...  61.9 us
    ppermute x32, starting transfers between devices, send(): return lax.ppermute(array, AXES, shifted(dims, step))  47.8 us
    pallas_call x3, Pallas kernels, merge(): pl.pallas_call(kernel, grid=(width // chunk,), in_specs=[pl.BlockSpec(pla...  8.85 us
    all_to_all x1, waiting for transfers between devices, shards(): lax.all_to_all(mixed, ('yl', 'x'), 0, 0, tiled=True).reshape(8, ROWS, width)  8.8 us
    all_to_all x1, starting transfers between devices, shards(): lax.all_to_all(jnp.broadcast_to(pair, (8,) + pair.shape), ('yh', 'z'), 0,...  7.94 us
    unnamed x70, local copies, waits for them, and re-layouts  7.37 us
    all_to_all x1, waiting for transfers between devices, shards(): lax.all_to_all(jnp.broadcast_to(pair, (8,) + pair.shape), ('yh', 'z'), 0,...  7.21 us
  transfers between devices with their start and end apart: 49, of which 17 were waited for; matrix products, arithmetic and copies ran while one was open for 7% of the time, Pallas kernels for 28%

profile of v5, /device:TPU:0, one launch (start us, length us, event | category | flops | bytes accessed | tf_op | source)
XLA Modules:
  0.0 241.2 jit_solution(5501642323561658939)
XLA Ops:
  0.6 3.2 %collective-permute-start.9 = (bf16[16,4096]{1,0:T(8,128)(2,1)}, bf16[16,4096]{1,0:T(8,128)(2,1)S(1)}, u32[]{:S(2)}, u32[]{:S(2)}) collective-permute-start(bf16[16,4096]{1,0:T(8,128)(2,1)} %param.23), channel_id=1, source_target_pairs={{0,2},{8,40},{16,18},{24,56},{32,34},{40,8},{48,50},{56,24},{4,6},... | collective-permute-start | bytes 393224 | tf_op jit(solution)/shard_map/ppermute | solution.py:45
  7.5 7.9 %all-to-all-start = ((bf16[8,128,256]{2,1,0:T(8,128)(2,1)}), bf16[8,128,256]{2,1,0:T(8,128)(2,1)S(1)}, u32[]{:S(2)}, u32[]{:S(2)}) async-start(bf16[8,128,256]{2,1,0:T(8,128)(2,1)} %broadcast_in_dim.4), calls=%async_computation | async-start | bytes 1048576 | tf_op jit(solution)/shard_map/all_to_all | solution.py:580
  18.0 7.2 %all-to-all-done = bf16[8,128,256]{2,1,0:T(8,128)(2,1)S(1)} async-done(((bf16[8,128,256]{2,1,0:T(8,128)(2,1)}), bf16[8,128,256]{2,1,0:T(8,128)(2,1)S(1)}, u32[]{:S(2)}, u32[]{:S(2)}) %all-to-all-start) | async-done | bytes 524320 | tf_op jit(solution)/shard_map/all_to_all | solution.py:580
  26.6 2.6 %collective-permute-start.11 = (bf16[64,4096]{1,0:T(8,128)(2,1)S(1)}, bf16[64,4096]{1,0:T(8,128)(2,1)}, u32[]{:S(2)}, u32[]{:S(2)}) collective-permute-start(bf16[64,4096]{1,0:T(8,128)(2,1)S(1)} %pad_maximum_fusion.1), channel_id=1, source_target_pairs={{0,68},{8,11},{16,84},{24,27},{32,100},{40,43},{48,116},{56,59},{4... | collective-permute-start | bytes 1572872 | tf_op jit(solution)/shard_map/ppermute | solution.py:45
  30.8 6.4 %shard_map.147 = bf16[128,4096]{1,0:T(8,128)(2,1)} custom-call(s32[1]{0:T(128)} %bitcast.base_ref, bf16[128,512]{1,0:T(8,128)(2,1)} %query_ref.1, bf16[1024,256]{1,0:T(8,128)(2,1)} %bitcast.7, bf16[1024,256]{1,0:T(8,128)(2,1)} %copy-done.28, s32[1,2048]{1,0:T(1,128)} %bitcast.8, bf16[512,4096]{1,0:T(8,128)(2,1)} %proj_ref.1), custom_call_target="tpu_custom_call" | custom-call | tf_op jit(solution)/shard_map/pallas_call | solution.py:139
  37.3 3.9 %all-to-all-start.1 = ((bf16[8,16,4096]{2,1,0:T(8,128)(2,1)}), bf16[8,16,4096]{2,1,0:T(8,128)(2,1)S(1)}, u32[]{:S(2)}, u32[]{:S(2)}) async-start(bf16[8,16,4096]{2,1,0:T(8,128)(2,1)} %bitcast.5), calls=%async_computation.1 | async-start | bytes 2097152 | tf_op jit(solution)/shard_map/all_to_all | solution.py:599
  46.2 2.8 %collective-permute-start.14 = (bf16[256,4096]{1,0:T(8,128)(2,1)}, bf16[256,4096]{1,0:T(8,128)(2,1)}, u32[]{:S(2)}, u32[]{:S(2)}) collective-permute-start(bf16[256,4096]{1,0:T(8,128)(2,1)} %constant_dynamic-update-slice_fusion.7.refs_6_), channel_id=1, source_target_pairs={{0,48},{8,76},{16,0},{24,92},{32,16},{40,108},{48,32},{56,124},{4,... | collective-permute-start | bytes 6291464 | tf_op jit(solution)/shard_map/ppermute | solution.py:45
  49.0 8.8 %all-to-all-done.1 = bf16[8,16,4096]{2,1,0:T(8,128)(2,1)S(1)} async-done(((bf16[8,16,4096]{2,1,0:T(8,128)(2,1)}), bf16[8,16,4096]{2,1,0:T(8,128)(2,1)S(1)}, u32[]{:S(2)}, u32[]{:S(2)}) %all-to-all-start.1) | async-done | bytes 1048608 | tf_op jit(solution)/shard_map/all_to_all | solution.py:599
  62.4 3.0 %collective-permute-done.1 = bf16[16,4224]{1,0:T(8,128)(2,1)S(1)} collective-permute-done((bf16[16,4224]{1,0:T(8,128)(2,1)S(1)}, bf16[16,4224]{1,0:T(8,128)(2,1)S(1)}, u32[]{:S(2)}, u32[]{:S(2)}) %collective-permute-start.1) | collective-permute-done | bytes 135200 | tf_op jit(solution)/shard_map/ppermute | solution.py:45
  66.4 2.5 %collective-permute-done.3 = bf16[16,4224]{1,0:T(8,128)(2,1)S(1)} collective-permute-done((bf16[16,4224]{1,0:T(8,128)(2,1)S(1)}, bf16[16,4224]{1,0:T(8,128)(2,1)S(1)}, u32[]{:S(2)}, u32[]{:S(2)}) %collective-permute-start.3) | collective-permute-done | bytes 135200 | tf_op jit(solution)/shard_map/ppermute | solution.py:45
  69.6 2.7 %collective-permute-start.5 = (bf16[64,4224]{1,0:T(8,128)(2,1)S(1)}, bf16[64,4224]{1,0:T(8,128)(2,1)S(1)}, u32[]{:S(2)}, u32[]{:S(2)}) collective-permute-start(bf16[64,4224]{1,0:T(8,128)(2,1)S(1)} %pad_maximum_fusion), channel_id=1, source_target_pairs={{0,68},{8,11},{16,84},{24,27},{32,100},{40,43},{48,116},{56,59},{4... | collective-permute-start | bytes 1622024 | tf_op jit(solution)/shard_map/ppermute | solution.py:45
  72.6 9.7 %collective-permute-done.4 = bf16[64,4224]{1,0:T(8,128)(2,1)S(1)} collective-permute-done((bf16[64,4224]{1,0:T(8,128)(2,1)S(1)}, bf16[64,4224]{1,0:T(8,128)(2,1)S(1)}, u32[]{:S(2)}, u32[]{:S(2)}) %collective-permute-start.4) | collective-permute-done | bytes 540704 | tf_op jit(solution)/shard_map/ppermute | solution.py:45
  84.8 8.3 %collective-permute-done.6 = bf16[64,4224]{1,0:T(8,128)(2,1)S(1)} collective-permute-done((bf16[64,4224]{1,0:T(8,128)(2,1)S(1)}, bf16[64,4224]{1,0:T(8,128)(2,1)S(1)}, u32[]{:S(2)}, u32[]{:S(2)}) %collective-permute-start.6) | collective-permute-done | bytes 540704 | tf_op jit(solution)/shard_map/ppermute | solution.py:45
  98.8 3.0 %collective-permute-done.15.refs_0_.refs_3_ = bf16[2,80,4096]{2,1,0:T(8,128)(2,1)S(1)} collective-permute-done((bf16[2,80,4096]{2,1,0:T(8,128)(2,1)S(1)}, bf16[2,80,4096]{2,1,0:T(8,128)(2,1)S(1)}, u32[]{:S(2)}, u32[]{:S(2)}) %collective-permute-start.15) | collective-permute-done | bytes 1310752 | tf_op jit(solution)/shard_map/ppermute | solution.py:49
  101.9 5.6 %shard_map.149 = (bf16[2,80,4096]{2,1,0:T(8,128)(2,1)S(1)}, bf16[2,80,4096]{2,1,0:T(8,128)(2,1)S(1)}, f32[2,2,160,192]{3,2,1,0:T(8,128)S(1)}) custom-call(bf16[2,80,4096]{2,1,0:T(8,128)(2,1)S(1)} %get-tuple-element.67.own_ref.refs_0_, bf16[2,80,4096]{2,1,0:T(8,128)(2,1)S(1)} %collective-permute-done.15.refs_0_.refs_3_, bf16[2,192,4096]{2,1,0:T(8,128)(2,1)S(1)} %copy-done.1, ...), custom_call_target="tpu_custom_call" | custom-call | tf_op jit(solution)/shard_map/pallas_call | solution.py:139
  107.8 13.4 %collective-permute-done.16.refs_0_.refs_2_ = bf16[256,4224]{1,0:T(8,128)(2,1)S(1)} collective-permute-done((bf16[256,4224]{1,0:T(8,128)(2,1)S(1)}, bf16[256,4224]{1,0:T(8,128)(2,1)S(1)}, u32[]{:S(2)}, u32[]{:S(2)}) %collective-permute-start.16) | collective-permute-done | bytes 2162720 | tf_op jit(solution)/shard_map/ppermute | solution.py:45
  121.2 3.6 %shard_map.150 = (bf16[2,160,4096]{2,1,0:T(8,128)(2,1)S(1)}, bf16[2,48,4096]{2,1,0:T(8,128)(2,1)S(1)}, bf16[2,64,4096]{2,1,0:T(8,128)(2,1)S(1)}, bf16[2,48,4096]...) custom-call(s32[1]{0:T(128)} %bitcast.4.me_ref, ...), custom_call_target="tpu_custom_call" | custom-call | tf_op jit(solution)/shard_map/pallas_call | solution.py:139
  125.7 3.3 %collective-permute-start.23 = (bf16[128,4224]{1,0:T(8,128)(2,1)S(1)}, bf16[128,4224]{1,0:T(8,128)(2,1)S(1)}, u32[]{:S(2)}, u32[]{:S(2)}) collective-permute-start(bf16[128,4224]{1,0:T(8,128)(2,1)S(1)} %slice.56), channel_id=1, source_target_pairs={{0,48},{8,76},{16,0},{24,92},{32,16},{40,108},{48,32},{56,124},{4,... | collective-permute-start | bytes 3244040 | tf_op jit(solution)/shard_map/ppermute | solution.py:45
  131.5 8.4 %shard_map.152 = (bf16[2,160,4096]{2,1,0:T(8,128)(2,1)S(1)}, bf16[2,160,4096]{2,1,0:T(8,128)(2,1)}, f32[2,2,320,192]{3,2,1,0:T(8,128)S(1)}) custom-call(bf16[2,160,4096]{2,1,0:T(8,128)(2,1)S(1)} %get-tuple-element.80.own_ref.refs_1_, bf16[2,48,4096]{2,1,0:T(8,128)(2,1)S(1)} %collective-permute-done.19.refs_0_.refs_4_, ...), custom_call_target="tpu_custom_call" | custom-call | tf_op jit(solution)/shard_map/pallas_call | solution.py:139
  150.0 5.7 %shard_map.154 = (bf16[2,80,4096]{2,1,0:T(8,128)(2,1)S(1)}, bf16[2,48,4096]{2,1,0:T(8,128)(2,1)S(1)}, bf16[2,32,4096]{2,1,0:T(8,128)(2,1)S(1)}, f32[2,2,160,192]{3,2,1,0:T(8,128)S(1)}) custom-call(bf16[2,80,4096]{2,1,0:T(8,128)(2,1)S(1)} %get-tuple-element.84.own_ref.refs_2_, bf16[2,48,4096]{2,1,0:T(8,128)(2,1)S(1)} %collective-permute-done.24.refs_0_.refs_7_, ...), custom_call_target="tpu_custom_call" | custom-call | tf_op jit(solution)/shard_map/pallas_call | solution.py:139
  156.3 4.0 %shard_map.155 = (bf16[128,4096]{1,0:T(8,128)(2,1)S(1)}, bf16[128,4096]{1,0:T(8,128)(2,1)S(1)}, bf16[128,4096]{1,0:T(8,128)(2,1)S(1)}, bf16[128,4096]{1,0:T(8,128)(2,1)S(1)}) custom-call(bf16[2,320,256]{2,1,0:T(8,128)(2,1)S(1)} %get-tuple-element.77.place_ref.refs_1_, f32[2,320,128]{2,1,0:T(8,128)S(1)} %get-tuple-element.78.weight_ref.refs_4_, ...), custom_call_target="tpu_custom_call" | custom-call | tf_op jit(solution)/shard_map/pallas_call | solution.py:286
  166.5 3.1 %collective-permute-start.31 = (bf16[128,4096]{1,0:T(8,128)(2,1)S(1)}, bf16[128,4096]{1,0:T(8,128)(2,1)S(1)}, u32[]{:S(2)}, u32[]{:S(2)}) collective-permute-start(bf16[128,4096]{1,0:T(8,128)(2,1)S(1)} %get-tuple-element.98), channel_id=1, source_target_pairs={{0,48},{8,76},{16,0},{24,92},{32,16},{40,108},{48,32},{56,124},{4,... | collective-permute-start | bytes 3145736 | tf_op jit(solution)/shard_map/ppermute | solution.py:45
  172.8 9.0 %collective-permute-done.31 = bf16[128,4096]{1,0:T(8,128)(2,1)S(1)} collective-permute-done((bf16[128,4096]{1,0:T(8,128)(2,1)S(1)}, bf16[128,4096]{1,0:T(8,128)(2,1)S(1)}, u32[]{:S(2)}, u32[]{:S(2)}) %collective-permute-start.31) | collective-permute-done | bytes 1048608 | tf_op jit(solution)/shard_map/ppermute | solution.py:45
  182.2 3.8 %collective-permute-start.32 = (bf16[128,4096]{1,0:T(8,128)(2,1)S(1)}, bf16[128,4096]{1,0:T(8,128)(2,1)}, u32[]{:S(2)}, u32[]{:S(2)}) collective-permute-start(bf16[128,4096]{1,0:T(8,128)(2,1)S(1)} %add_convert_fusion.3), channel_id=1, source_target_pairs={{0,48},{8,76},{16,0},{24,92},{32,16},{40,108},{48,32},{56,124},{4,... | collective-permute-start | bytes 3145736 | tf_op jit(solution)/shard_map/ppermute | solution.py:45
  186.3 7.5 %shard_map.157 = (bf16[2,320,4096]{2,1,0:T(8,128)(2,1)S(1)}, bf16[2,80,4096]{2,1,0:T(8,128)(2,1)S(1)}, bf16[2,80,4096]{2,1,0:T(8,128)(2,1)S(1)}, bf16[2,80,4096]...) custom-call(bf16[1,320,256]{2,1,0:T(8,128)(2,1)S(1)} %get-tuple-element.65.place_ref.refs_0_, ...), custom_call_target="tpu_custom_call" | custom-call | flops 2684354560 | bytes 20185088 | tf_op jit(solution)/shard_map/pallas_call | solution.py:139
  193.8 3.0 %collective-permute-done.33 = bf16[128,4096]{1,0:T(8,128)(2,1)S(1)} collective-permute-done((bf16[128,4096]{1,0:T(8,128)(2,1)S(1)}, bf16[128,4096]{1,0:T(8,128)(2,1)S(1)}, u32[]{:S(2)}, u32[]{:S(2)}) %collective-permute-start.33) | collective-permute-done | bytes 1048608 | tf_op jit(solution)/shard_map/ppermute | solution.py:45
  197.3 7.0 %collective-permute-done.32 = bf16[128,4096]{1,0:T(8,128)(2,1)} collective-permute-done((bf16[128,4096]{1,0:T(8,128)(2,1)S(1)}, bf16[128,4096]{1,0:T(8,128)(2,1)}, u32[]{:S(2)}, u32[]{:S(2)}) %collective-permute-start.32) | collective-permute-done | bytes 1048608 | tf_op jit(solution)/shard_map/ppermute | solution.py:45
  204.4 3.8 %collective-permute-done.37 = bf16[128,4096]{1,0:T(8,128)(2,1)} collective-permute-done((bf16[128,4096]{1,0:T(8,128)(2,1)S(1)}, bf16[128,4096]{1,0:T(8,128)(2,1)}, u32[]{:S(2)}, u32[]{:S(2)}) %collective-permute-start.37) | collective-permute-done | bytes 1048608 | tf_op jit(solution)/shard_map/ppermute | solution.py:45
  208.2 2.7 %add_convert_fusion.2 = (bf16[128,4096]{1,0:T(8,128)(2,1)S(1)}, bf16[128,4096]{1,0:T(8,128)(2,1)S(1)}) fusion(bf16[128,4096]{1,0:T(8,128)(2,1)S(1)} %collective-permute-done.33, bf16[128,4096]{1,0:T(8,128)(2,1)} %collective-permute-done.32, bf16[256,4096]{1,0:T(8,128)(2,1)S(1)} %shard_map.151, bf16[128,4096]{1,0:T(8,128)(2,1)} %collective-permute-done.37, ...), kind=kLoop, calls=%fused_computation.2 | loop fusion | flops 6291456 | bytes 8388608 | tf_op jit(solution)/shard_map/convert
  216.4 4.7 %shard_map.158.back_ref = f32[2,640,192]{2,1,0:T(8,128)S(1)} custom-call(bf16[2,320,4096]{2,1,0:T(8,128)(2,1)S(1)} %get-tuple-element.117.refs_0_, bf16[2,80,4096]{2,1,0:T(8,128)(2,1)S(1)} %collective-permute-done.43.refs_1_, bf16[2,80,4096]{2,1,0:T(8,128)(2,1)S(1)} %collective-permute-done.44.refs_2_, ...), custom_call_target="tpu_custom_call" | custom-call | flops 2013265920 | bytes 14614528 | tf_op jit(solution)/shard_map/pallas_call | solution.py:139
  221.3 9.1 %shard_map.159 = (bf16[2,192,4096]{2,1,0:T(8,128)(2,1)}, bf16[2,192,4096]{2,1,0:T(8,128)(2,1)}) custom-call(f32[2,640,192]{2,1,0:T(8,128)S(1)} %shard_map.158.back_ref, bf16[2,80,4096]{2,1,0:T(8,128)(2,1)S(1)} %get-tuple-element.67.own_ref.refs_0_, bf16[2,160,4096]{2,1,0:T(8,128)(2,1)S(1)} %get-tuple-element.80.own_ref.refs_1_, ...), custom_call_target="tpu_custom_call" | custom-call | flops 4026531840 | bytes 19726336 | tf_op jit(solution)/shard_map/pallas_call | solution.py:139
  234.1 6.3 %shard_map.160 = bf16[2,192,4096]{2,1,0:T(8,128)(2,1)} custom-call(bf16[2,320,4096]{2,1,0:T(8,128)(2,1)S(1)} %get-tuple-element.117.refs_0_, bf16[2,80,4096]{2,1,0:T(8,128)(2,1)S(1)} %collective-permute-done.43.refs_1_, bf16[2,80,4096]{2,1,0:T(8,128)(2,1)S(1)} %collective-permute-done.44.refs_2_, bf16[2,80,4096]{2,1,0:T(8,128)(2,1)S(1)} %collective-permute-done.45.refs_3_, ...), custom_call_target="tpu_custom_call" | custom-call | flops 2013265920 | bytes 15597568 | tf_op jit(solution)/shard_map/pallas_call | solution.py:139
  (183 shorter events, 63.9 us)
Async XLA Ops:
  0.6 16.4 %collective-permute-start.9 = (bf16[16,4096]{1,0:T(8,128)(2,1)}, bf16[16,4096]{1,0:T(8,128)(2,1)S(1)}, u32[]{:S(2)}, u32[]{:S(2)}) collective-permute-start(bf16[16,4096]{1,0:T(8,128)(2,1)} %param.23), channel_id=1, source_target_pairs={{0,2},{8,40},{16,18},{24,56},{32,34},{40,8},{48,50},{56,24},{4,6},... | collective-permute-start | bytes 393224 | tf_op jit(solution)/shard_map/ppermute | solution.py:45
  3.8 13.2 %collective-permute-start.8 = (bf16[16,4096]{1,0:T(8,128)(2,1)}, bf16[16,4096]{1,0:T(8,128)(2,1)S(1)}, u32[]{:S(2)}, u32[]{:S(2)}) collective-permute-start(bf16[16,4096]{1,0:T(8,128)(2,1)} %param.23), channel_id=1, source_target_pairs={{0,3},{8,56},{16,19},{24,8},{32,35},{40,24},{48,51},{56,40},{4,7},... | collective-permute-start | bytes 393224 | tf_op jit(solution)/shard_map/ppermute | solution.py:45
  7.5 17.7 %all-to-all-start = ((bf16[8,128,256]{2,1,0:T(8,128)(2,1)}), bf16[8,128,256]{2,1,0:T(8,128)(2,1)S(1)}, u32[]{:S(2)}, u32[]{:S(2)}) async-start(bf16[8,128,256]{2,1,0:T(8,128)(2,1)} %broadcast_in_dim.4), calls=%async_computation | async-start | bytes 1048576 | tf_op jit(solution)/shard_map/all_to_all | solution.py:580
  25.2 16.0 %collective-permute-start.10 = (bf16[64,4096]{1,0:T(8,128)(2,1)S(1)}, bf16[64,4096]{1,0:T(8,128)(2,1)S(1)}, u32[]{:S(2)}, u32[]{:S(2)}) collective-permute-start(bf16[64,4096]{1,0:T(8,128)(2,1)S(1)} %pad_maximum_fusion.1), channel_id=1, source_target_pairs={{0,4},{8,9},{16,20},{24,25},{32,36},{40,41},{48,52},{56,57},{4,64}... | collective-permute-start | bytes 1572872 | tf_op jit(solution)/shard_map/ppermute | solution.py:45
  26.6 15.4 %collective-permute-start.11 = (bf16[64,4096]{1,0:T(8,128)(2,1)S(1)}, bf16[64,4096]{1,0:T(8,128)(2,1)}, u32[]{:S(2)}, u32[]{:S(2)}) collective-permute-start(bf16[64,4096]{1,0:T(8,128)(2,1)S(1)} %pad_maximum_fusion.1), channel_id=1, source_target_pairs={{0,68},{8,11},{16,84},{24,27},{32,100},{40,43},{48,116},{56,59},{4... | collective-permute-start | bytes 1572872 | tf_op jit(solution)/shard_map/ppermute | solution.py:45
  30.0 13.9 %collective-permute-start.12 = (bf16[64,4096]{1,0:T(8,128)(2,1)S(1)}, bf16[64,4096]{1,0:T(8,128)(2,1)}, u32[]{:S(2)}, u32[]{:S(2)}) collective-permute-start(bf16[64,4096]{1,0:T(8,128)(2,1)S(1)} %pad_maximum_fusion.1), channel_id=1, source_target_pairs={{0,64},{8,10},{16,80},{24,26},{32,96},{40,42},{48,112},{56,58},{4,... | collective-permute-start | bytes 1572872 | tf_op jit(solution)/shard_map/ppermute | solution.py:45
  37.3 20.6 %all-to-all-start.1 = ((bf16[8,16,4096]{2,1,0:T(8,128)(2,1)}), bf16[8,16,4096]{2,1,0:T(8,128)(2,1)S(1)}, u32[]{:S(2)}, u32[]{:S(2)}) async-start(bf16[8,16,4096]{2,1,0:T(8,128)(2,1)} %bitcast.5), calls=%async_computation.1 | async-start | bytes 2097152 | tf_op jit(solution)/shard_map/all_to_all | solution.py:599
  45.8 47.3 %collective-permute-start.13 = (bf16[256,4096]{1,0:T(8,128)(2,1)}, bf16[256,4096]{1,0:T(8,128)(2,1)S(1)}, u32[]{:S(2)}, u32[]{:S(2)}) collective-permute-start(bf16[256,4096]{1,0:T(8,128)(2,1)} %constant_dynamic-update-slice_fusion.7.refs_6_), channel_id=1, source_target_pairs={{0,16},{8,12},{16,32},{24,28},{32,48},{40,44},{48,0},{56,60},{4,20... | collective-permute-start | bytes 6291464 | tf_op jit(solution)/shard_map/ppermute | solution.py:45
  46.2 46.9 %collective-permute-start.14 = (bf16[256,4096]{1,0:T(8,128)(2,1)}, bf16[256,4096]{1,0:T(8,128)(2,1)}, u32[]{:S(2)}, u32[]{:S(2)}) collective-permute-start(bf16[256,4096]{1,0:T(8,128)(2,1)} %constant_dynamic-update-slice_fusion.7.refs_6_), channel_id=1, source_target_pairs={{0,48},{8,76},{16,0},{24,92},{32,16},{40,108},{48,32},{56,124},{4,... | collective-permute-start | bytes 6291464 | tf_op jit(solution)/shard_map/ppermute | solution.py:45
  68.9 13.4 %collective-permute-start.4 = (bf16[64,4224]{1,0:T(8,128)(2,1)S(1)}, bf16[64,4224]{1,0:T(8,128)(2,1)S(1)}, u32[]{:S(2)}, u32[]{:S(2)}) collective-permute-start(bf16[64,4224]{1,0:T(8,128)(2,1)S(1)} %pad_maximum_fusion), channel_id=1, source_target_pairs={{0,4},{8,9},{16,20},{24,25},{32,36},{40,41},{48,52},{56,57},{4,64}... | collective-permute-start | bytes 1622024 | tf_op jit(solution)/shard_map/ppermute | solution.py:45
  69.6 15.2 %collective-permute-start.5 = (bf16[64,4224]{1,0:T(8,128)(2,1)S(1)}, bf16[64,4224]{1,0:T(8,128)(2,1)S(1)}, u32[]{:S(2)}, u32[]{:S(2)}) collective-permute-start(bf16[64,4224]{1,0:T(8,128)(2,1)S(1)} %pad_maximum_fusion), channel_id=1, source_target_pairs={{0,68},{8,11},{16,84},{24,27},{32,100},{40,43},{48,116},{56,59},{4... | collective-permute-start | bytes 1622024 | tf_op jit(solution)/shard_map/ppermute | solution.py:45
  72.2 20.9 %collective-permute-start.6 = (bf16[64,4224]{1,0:T(8,128)(2,1)S(1)}, bf16[64,4224]{1,0:T(8,128)(2,1)S(1)}, u32[]{:S(2)}, u32[]{:S(2)}) collective-permute-start(bf16[64,4224]{1,0:T(8,128)(2,1)S(1)} %pad_maximum_fusion), channel_id=1, source_target_pairs={{0,64},{8,10},{16,80},{24,26},{32,96},{40,42},{48,112},{56,58},{4,... | collective-permute-start | bytes 1622024 | tf_op jit(solution)/shard_map/ppermute | solution.py:45
  93.2 28.0 %collective-permute-start.16 = (bf16[256,4224]{1,0:T(8,128)(2,1)S(1)}, bf16[256,4224]{1,0:T(8,128)(2,1)S(1)}, u32[]{:S(2)}, u32[]{:S(2)}) collective-permute-start(bf16[256,4224]{1,0:T(8,128)(2,1)S(1)} %constant_dynamic-update-slice_fusion.refs_0_.refs_1_), channel_id=1, source_target_pairs={{0,16},{8,12},{16,32},{24,28},{32,48},{40,44},{48,0},{56,60},{4,20... | collective-permute-start | bytes 6488072 | tf_op jit(solution)/shard_map/ppermute | solution.py:45
  94.4 26.8 %collective-permute-start.17 = (bf16[256,4224]{1,0:T(8,128)(2,1)S(1)}, bf16[256,4224]{1,0:T(8,128)(2,1)S(1)}, u32[]{:S(2)}, u32[]{:S(2)}) collective-permute-start(bf16[256,4224]{1,0:T(8,128)(2,1)S(1)} %constant_dynamic-update-slice_fusion.refs_0_.refs_1_), channel_id=1, source_target_pairs={{0,48},{8,76},{16,0},{24,92},{32,16},{40,108},{48,32},{56,124},{4,... | collective-permute-start | bytes 6488072 | tf_op jit(solution)/shard_map/ppermute | solution.py:45
  107.4 18.3 %collective-permute-start.18 = (bf16[2,80,4096]{2,1,0:T(8,128)(2,1)S(1)}, bf16[2,80,4096]{2,1,0:T(8,128)(2,1)S(1)}, u32[]{:S(2)}, u32[]{:S(2)}) collective-permute-start(bf16[2,80,4096]{2,1,0:T(8,128)(2,1)S(1)} %get-tuple-element.76), channel_id=1, source_target_pairs={{0,8},{8,0},{1,9},{9,1},{2,10},{10,2},{3,11},{11,3},{4,12},{12,4},... | collective-permute-start | bytes 3932168 | tf_op jit(solution)/shard_map/ppermute | solution.py:49
  125.5 16.4 %collective-permute-start.22 = (bf16[128,4224]{1,0:T(8,128)(2,1)S(1)}, bf16[128,4224]{1,0:T(8,128)(2,1)S(1)}, u32[]{:S(2)}, u32[]{:S(2)}) collective-permute-start(bf16[128,4224]{1,0:T(8,128)(2,1)S(1)} %slice.55), channel_id=1, source_target_pairs={{0,16},{8,12},{16,32},{24,28},{32,48},{40,44},{48,0},{56,60},{4,20... | collective-permute-start | bytes 3244040 | tf_op jit(solution)/shard_map/ppermute | solution.py:45
  125.7 16.3 %collective-permute-start.23 = (bf16[128,4224]{1,0:T(8,128)(2,1)S(1)}, bf16[128,4224]{1,0:T(8,128)(2,1)S(1)}, u32[]{:S(2)}, u32[]{:S(2)}) collective-permute-start(bf16[128,4224]{1,0:T(8,128)(2,1)S(1)} %slice.56), channel_id=1, source_target_pairs={{0,48},{8,76},{16,0},{24,92},{32,16},{40,108},{48,32},{56,124},{4,... | collective-permute-start | bytes 3244040 | tf_op jit(solution)/shard_map/ppermute | solution.py:45
  139.9 16.4 %collective-permute-start.26 = (bf16[2,160,4096]{2,1,0:T(8,128)(2,1)}, bf16[2,160,4096]{2,1,0:T(8,128)(2,1)S(1)}, u32[]{:S(2)}, u32[]{:S(2)}) collective-permute-start(bf16[2,160,4096]{2,1,0:T(8,128)(2,1)} %get-tuple-element.89), channel_id=1, source_target_pairs={{0,8},{8,0},{1,9},{9,1},{2,10},{10,2},{3,11},{11,3},{4,12},{12,4},... | collective-permute-start | bytes 7864328 | tf_op jit(solution)/shard_map/ppermute | solution.py:49
  145.1 16.2 %collective-permute-start.27 = (bf16[128,4096]{1,0:T(8,128)(2,1)S(1)}, bf16[128,4096]{1,0:T(8,128)(2,1)S(1)}, u32[]{:S(2)}, u32[]{:S(2)}) collective-permute-start(bf16[128,4096]{1,0:T(8,128)(2,1)S(1)} %slice.57), channel_id=1, source_target_pairs={{0,16},{8,12},{16,32},{24,28},{32,48},{40,44},{48,0},{56,60},{4,20... | collective-permute-start | bytes 3145736 | tf_op jit(solution)/shard_map/ppermute | solution.py:45
  148.1 14.9 %collective-permute-start.28 = (bf16[128,4096]{1,0:T(8,128)(2,1)S(1)}, bf16[128,4096]{1,0:T(8,128)(2,1)S(1)}, u32[]{:S(2)}, u32[]{:S(2)}) collective-permute-start(bf16[128,4096]{1,0:T(8,128)(2,1)S(1)} %slice.58), channel_id=1, source_target_pairs={{0,48},{8,76},{16,0},{24,92},{32,16},{40,108},{48,32},{56,124},{4,... | collective-permute-start | bytes 3145736 | tf_op jit(solution)/shard_map/ppermute | solution.py:45
  166.5 15.4 %collective-permute-start.31 = (bf16[128,4096]{1,0:T(8,128)(2,1)S(1)}, bf16[128,4096]{1,0:T(8,128)(2,1)S(1)}, u32[]{:S(2)}, u32[]{:S(2)}) collective-permute-start(bf16[128,4096]{1,0:T(8,128)(2,1)S(1)} %get-tuple-element.98), channel_id=1, source_target_pairs={{0,48},{8,76},{16,0},{24,92},{32,16},{40,108},{48,32},{56,124},{4,... | collective-permute-start | bytes 3145736 | tf_op jit(solution)/shard_map/ppermute | solution.py:45
  169.6 16.4 %collective-permute-start.36 = (bf16[128,4096]{1,0:T(8,128)(2,1)S(1)}, bf16[128,4096]{1,0:T(8,128)(2,1)S(1)}, u32[]{:S(2)}, u32[]{:S(2)}) collective-permute-start(bf16[128,4096]{1,0:T(8,128)(2,1)S(1)} %get-tuple-element.102), channel_id=1, source_target_pairs={{0,16},{8,12},{16,32},{24,28},{32,48},{40,44},{48,0},{56,60},{4,20... | collective-permute-start | bytes 3145736 | tf_op jit(solution)/shard_map/ppermute | solution.py:45
  169.6 27.2 %collective-permute-start.33 = (bf16[128,4096]{1,0:T(8,128)(2,1)S(1)}, bf16[128,4096]{1,0:T(8,128)(2,1)S(1)}, u32[]{:S(2)}, u32[]{:S(2)}) collective-permute-start(bf16[128,4096]{1,0:T(8,128)(2,1)S(1)} %get-tuple-element.99), channel_id=1, source_target_pairs={{0,16},{8,12},{16,32},{24,28},{32,48},{40,44},{48,0},{56,60},{4,20... | collective-permute-start | bytes 3145736 | tf_op jit(solution)/shard_map/ppermute | solution.py:45
  170.6 26.2 %collective-permute-start.35 = (bf16[128,4096]{1,0:T(8,128)(2,1)S(1)}, bf16[128,4096]{1,0:T(8,128)(2,1)S(1)}, u32[]{:S(2)}, u32[]{:S(2)}) collective-permute-start(bf16[128,4096]{1,0:T(8,128)(2,1)S(1)} %get-tuple-element.100), channel_id=1, source_target_pairs={{0,48},{8,76},{16,0},{24,92},{32,16},{40,108},{48,32},{56,124},{4,... | collective-permute-start | bytes 3145736 | tf_op jit(solution)/shard_map/ppermute | solution.py:45
  182.2 22.2 %collective-permute-start.32 = (bf16[128,4096]{1,0:T(8,128)(2,1)S(1)}, bf16[128,4096]{1,0:T(8,128)(2,1)}, u32[]{:S(2)}, u32[]{:S(2)}) collective-permute-start(bf16[128,4096]{1,0:T(8,128)(2,1)S(1)} %add_convert_fusion.3), channel_id=1, source_target_pairs={{0,48},{8,76},{16,0},{24,92},{32,16},{40,108},{48,32},{56,124},{4,... | collective-permute-start | bytes 3145736 | tf_op jit(solution)/shard_map/ppermute | solution.py:45
  186.2 22.0 %collective-permute-start.37 = (bf16[128,4096]{1,0:T(8,128)(2,1)S(1)}, bf16[128,4096]{1,0:T(8,128)(2,1)}, u32[]{:S(2)}, u32[]{:S(2)}) collective-permute-start(bf16[128,4096]{1,0:T(8,128)(2,1)S(1)} %add_convert_fusion.1), channel_id=1, source_target_pairs={{0,16},{8,12},{16,32},{24,28},{32,48},{40,44},{48,0},{56,60},{4,20... | collective-permute-start | bytes 3145736 | tf_op jit(solution)/shard_map/ppermute | solution.py:45
  196.8 16.2 %collective-permute-start.43 = (bf16[2,80,4096]{2,1,0:T(8,128)(2,1)S(1)}, bf16[2,80,4096]{2,1,0:T(8,128)(2,1)S(1)}, u32[]{:S(2)}, u32[]{:S(2)}) collective-permute-start(bf16[2,80,4096]{2,1,0:T(8,128)(2,1)S(1)} %get-tuple-element.105), channel_id=1, source_target_pairs={{0,8},{8,0},{1,9},{9,1},{2,10},{10,2},{3,11},{11,3},{4,12},{12,4},... | collective-permute-start | bytes 3932168 | tf_op jit(solution)/shard_map/ppermute | solution.py:49
  196.8 17.5 %collective-permute-start.44 = (bf16[2,80,4096]{2,1,0:T(8,128)(2,1)S(1)}, bf16[2,80,4096]{2,1,0:T(8,128)(2,1)S(1)}, u32[]{:S(2)}, u32[]{:S(2)}) collective-permute-start(bf16[2,80,4096]{2,1,0:T(8,128)(2,1)S(1)} %get-tuple-element.107), channel_id=1, source_target_pairs={{0,8},{8,0},{1,9},{9,1},{2,10},{10,2},{3,11},{11,3},{4,12},{12,4},... | collective-permute-start | bytes 3932168 | tf_op jit(solution)/shard_map/ppermute | solution.py:49
  197.3 19.0 %collective-permute-start.45 = (bf16[2,80,4096]{2,1,0:T(8,128)(2,1)S(1)}, bf16[2,80,4096]{2,1,0:T(8,128)(2,1)S(1)}, u32[]{:S(2)}, u32[]{:S(2)}) collective-permute-start(bf16[2,80,4096]{2,1,0:T(8,128)(2,1)S(1)} %get-tuple-element.109), channel_id=1, source_target_pairs={{0,8},{8,0},{1,9},{9,1},{2,10},{10,2},{3,11},{11,3},{4,12},{12,4},... | collective-permute-start | bytes 3932168 | tf_op jit(solution)/shard_map/ppermute | solution.py:49
  211.0 19.4 %collective-permute-start.39 = (bf16[64,4096]{1,0:T(8,128)(2,1)S(1)}, bf16[64,4096]{1,0:T(8,128)(2,1)S(1)}, u32[]{:S(2)}, u32[]{:S(2)}) collective-permute-start(bf16[64,4096]{1,0:T(8,128)(2,1)S(1)} %get-tuple-element.125), channel_id=1, source_target_pairs={{0,64},{8,10},{16,80},{24,26},{32,96},{40,42},{48,112},{56,58},{4,... | collective-permute-start | bytes 1572872 | tf_op jit(solution)/shard_map/ppermute | solution.py:45
  213.1 17.3 %collective-permute-start.38 = (bf16[64,4096]{1,0:T(8,128)(2,1)S(1)}, bf16[64,4096]{1,0:T(8,128)(2,1)S(1)}, u32[]{:S(2)}, u32[]{:S(2)}) collective-permute-start(bf16[64,4096]{1,0:T(8,128)(2,1)S(1)} %get-tuple-element.124), channel_id=1, source_target_pairs={{0,4},{8,9},{16,20},{24,25},{32,36},{40,41},{48,52},{56,57},{4,64}... | collective-permute-start | bytes 1572872 | tf_op jit(solution)/shard_map/ppermute | solution.py:45
  214.3 16.0 %collective-permute-start.34 = (bf16[64,4096]{1,0:T(8,128)(2,1)S(1)}, bf16[64,4096]{1,0:T(8,128)(2,1)S(1)}, u32[]{:S(2)}, u32[]{:S(2)}) collective-permute-start(bf16[64,4096]{1,0:T(8,128)(2,1)S(1)} %slice.70), channel_id=1, source_target_pairs={{0,68},{8,11},{16,84},{24,27},{32,100},{40,43},{48,116},{56,59},{4... | collective-permute-start | bytes 1572872 | tf_op jit(solution)/shard_map/ppermute | solution.py:45
  (47 other events, 385.1 us)
